TPU v7x, 32 devices: a whole 2x2x4 slice. The times are simulated.
32 devices in a mesh: groups: 2 (over x), bfly: 8 (over z, y), rhs: 2 (over core).
Axes of the slice: x: 2, y: 2, z: 4, core: 2. Of those that a mesh axis runs over, the one named last changes fastest.
Arguments:
- right_sides: bfloat16 [262144, 128], P(('groups', 'bfly', 'rhs')), parts along dimension 0, may hold values from -6 to 6
- leaf_basis: bfloat16 [512, 64, 256], P(('bfly', 'rhs')), may hold values from -0.375 to 0.375
- translations: bfloat16 [512, 9, 64, 128], P(('bfly', 'rhs')), may hold values from -0.5 to 0.5
- node_target: int32 [512], P(('bfly', 'rhs')), may hold values from 0 to 511, as said below
- out_basis: bfloat16 [512, 64, 256], P(('bfly', 'rhs')), may hold values from -0.75 to 0.75
Outputs:
- applied: bfloat16 [262144, 128], P(('groups', 'bfly', 'rhs')), parts along dimension 0
There are 2 independent parts, one for each index of `groups`. A program takes and returns all parts, laid end to end along the dimension named above; an argument that names none is the same for every part. Nothing has to cross between parts.
Inputs may be any that keep to these rules, and one draw needn't show every extreme that they name: node_target is a permutation of the 512 boxes, and node_target[b] // 32 equals r // 32, where r is b with its binary digits (as many as the base-2 logarithm of 512) in reverse order.
All inputs are finite; a program needn't handle non-finite values.
Results may differ from a plain program's by a relative error of at most 0.015.
Values may be sent and summed in bfloat16 or wider, within the bound.
No kernel may reach another device: no remote copies, remote signals or barrier semaphores. Data moves between devices by JAX's collectives and lax.ppermute only.
A program may use at most 64 MiB of HBM per device.

v0:
```python
import jax
import jax.numpy as jnp
from jax import lax
from jax.sharding import PartitionSpec as P


def from_partner(value, axis, distance):
    mask = 2**distance
    pairs = [(source, source ^ mask) for source in range(lax.axis_size(axis))]
    return lax.ppermute(value, axis, pairs)


def combine(current, partner_part, matrices):
    width = current.shape[1]
    own_term = jnp.einsum(
        "bij,bjc->bic", matrices[:, :, :width], current, preferred_element_type=jnp.float32
    )
    other_term = jnp.einsum(
        "bij,bjc->bic", matrices[:, :, width:], partner_part, preferred_element_type=jnp.float32
    )
    return (own_term + other_term).astype(jnp.bfloat16)


def pack_slots(flat_coefficients, slot_key, capacity, slot_total, target_spot):
    box_count = flat_coefficients.shape[0]
    box_iota = jnp.arange(box_count, dtype=jnp.int32)
    earlier = (slot_key[:, None] == slot_key[None, :]) & (box_iota[None, :] < box_iota[:, None])
    order_within = jnp.sum(earlier.astype(jnp.int32), axis=1)
    slot_of_box = slot_key * capacity + order_within
    selector = jnp.arange(slot_total, dtype=jnp.int32)[:, None] == slot_of_box[None, :]
    outgoing = jnp.dot(
        selector.astype(jnp.bfloat16), flat_coefficients, preferred_element_type=jnp.float32
    ).astype(jnp.bfloat16)
    outgoing_spot = jnp.sum(jnp.where(selector, target_spot[None, :] + 1, 0), axis=1) - 1
    return (outgoing, outgoing_spot)


def per_device(right_sides, leaf_basis, translations, node_target, out_basis):
    box_count = leaf_basis.shape[0]
    rank_width = leaf_basis.shape[1]
    leaf_rows = leaf_basis.shape[2]
    column_count = right_sides.shape[1]
    point_rows = right_sides.reshape(box_count, leaf_rows, column_count)
    coefficients = jnp.einsum(
        "brl,blc->brc", leaf_basis, point_rows, preferred_element_type=jnp.float32
    ).astype(jnp.bfloat16)
    local_levels = box_count.bit_length() - 1
    for level_index in range(local_levels):
        span = 2**level_index
        blocks = coefficients.reshape(box_count // (2 * span), 2, span, rank_width, column_count)
        partner_part = jnp.flip(blocks, 1).reshape(box_count, rank_width, column_count)
        coefficients = combine(coefficients, partner_part, translations[:, level_index])
    device_count = lax.axis_size(("bfly", "rhs"))
    device_levels = device_count.bit_length() - 1
    for section_index in range(device_levels):
        partner_part = from_partner(coefficients, ("bfly", "rhs"), section_index)
        coefficients = combine(
            coefficients, partner_part, translations[:, local_levels + section_index]
        )
    target_device = node_target // box_count
    target_spot = node_target % box_count
    box_iota = jnp.arange(box_count, dtype=jnp.int32)
    flat_coefficients = coefficients.reshape(box_count, rank_width * column_count)
    capacity = max(1, box_count // device_count)
    slot_total = device_count * capacity
    outgoing, outgoing_spot = pack_slots(
        flat_coefficients, target_device, capacity, slot_total, target_spot
    )
    incoming, incoming_spot = (
        lax.all_to_all(outgoing, ("bfly", "rhs"), split_axis=0, concat_axis=0, tiled=True),
        lax.all_to_all(outgoing_spot, ("bfly", "rhs"), split_axis=0, concat_axis=0, tiled=True),
    )
    placement_table = (box_iota[:, None] == incoming_spot[None, :]).astype(jnp.bfloat16)
    placed = jnp.dot(placement_table, incoming, preferred_element_type=jnp.float32).astype(
        jnp.bfloat16
    )
    placed = placed.reshape(box_count, rank_width, column_count)
    applied = jnp.einsum("brl,brc->blc", out_basis, placed, preferred_element_type=jnp.float32)
    return applied.astype(jnp.bfloat16).reshape(box_count * leaf_rows, column_count)


def solution(mesh):
    in_specs = (
        P(("groups", "bfly", "rhs"), None),
        P(("bfly", "rhs"), None, None),
        P(("bfly", "rhs"), None, None, None),
        P(("bfly", "rhs")),
        P(("bfly", "rhs"), None, None),
    )
    out_specs = P(("groups", "bfly", "rhs"), None)
    return jax.shard_map(
        per_device, mesh=mesh, in_specs=in_specs, out_specs=out_specs, check_vma=False
    )
```

profile of v0, /device:TPU:0, one launch (start us, length us, event | category | flops | bytes accessed | tf_op | source)
XLA Modules:
  0.0 120.2 jit_solution(12586880520421218510)
XLA Ops:
  0.0 5.1 %slice_bitcast_fusion = (bf16[32,64,128]{2,1,0:T(8,128)(2,1)S(1)}, bf16[32,64,128]{2,1,0:T(8,128)(2,1)}, bf16[32,64,128]{2,1,0:T(8,128)(2,1)}, bf16[32,64,128]{2...) fusion(bf16[32,9,64,128]{3,2,1,0:T(8,128)(2,1)} %param.7), kind=kLoop, calls=%fused_computation.52 | loop fusion | bytes 9437184 | tf_op jit(solution)/shard_map/squeeze | solution.py:58
  6.4 1.3 %fusion.21 = f32[32,128,64]{1,2,0:T(8,128)} fusion(bf16[32,64,128]{2,1,0:T(8,128)(2,1)S(1)} %convolution_convert_fusion.2, bf16[32,64,128]{2,1,0:T(8,128)(2,1)S(1)} %get-tuple-element.13), kind=kOutput, calls=%fused_computation.34 | convolution fusion | flops 33554432 | bytes 2097152 | tf_op jit(solution)/shard_map/bij,bjc->bic/dot_general | solution.py:15
  7.7 1.9 %rev.20 = bf16[16,2,1,64,128]{4,3,1,0,2:T(8,128)(2,1)} reverse(bf16[16,2,1,64,128]{4,3,1,0,2:T(8,128)(2,1)} %bitcast.100), dimensions={1} | reverse | bytes 1048576 | tf_op jit(solution)/shard_map/jit(_flip)/rev | solution.py:51
  9.6 2.0 %fusion = bf16[32,128,64]{1,2,0:T(8,128)(2,1)S(1)} fusion(f32[32,128,64]{1,2,0:T(8,128)} %fusion.21, bf16[32,64,128]{2,1,0:T(8,128)(2,1)} %bitcast.101, bf16[32,64,128]{2,1,0:T(8,128)(2,1)} %copy-done.7), kind=kOutput, calls=%fused_computation.13 | convolution fusion | flops 34078720 | bytes 2621440 | tf_op jit(solution)/shard_map/bij,bjc->bic/dot_general | solution.py:18
  11.6 1.3 %fusion.23 = f32[32,128,64]{1,2,0:T(8,128)} fusion(bf16[32,128,64]{1,2,0:T(8,128)(2,1)S(1)} %fusion, bf16[32,64,128]{2,1,0:T(8,128)(2,1)S(1)} %copy-done.6), kind=kOutput, calls=%fused_computation.36 | convolution fusion | flops 33554432 | bytes 2097152 | tf_op jit(solution)/shard_map/bij,bjc->bic/dot_general | solution.py:15
  12.8 1.9 %rev.21 = bf16[8,2,2,64,128]{4,3,2,1,0:T(8,128)(2,1)} reverse(bf16[8,2,2,64,128]{4,3,2,1,0:T(8,128)(2,1)} %bitcast.96), dimensions={1} | reverse | bytes 1048576 | tf_op jit(solution)/shard_map/jit(_flip)/rev | solution.py:51
  14.7 1.9 %fusion.1 = bf16[32,128,64]{1,2,0:T(8,128)(2,1)S(1)} fusion(f32[32,128,64]{1,2,0:T(8,128)} %fusion.23, bf16[32,64,128]{2,1,0:T(8,128)(2,1)} %bitcast.102, bf16[32,64,128]{2,1,0:T(8,128)(2,1)} %get-tuple-element.6), kind=kOutput, calls=%fused_computation.14 | convolution fusion | flops 34078720 | bytes 2621440 | tf_op jit(solution)/shard_map/bij,bjc->bic/dot_general | solution.py:18
  16.7 1.3 %fusion.25 = f32[32,128,64]{1,2,0:T(8,128)} fusion(bf16[32,128,64]{1,2,0:T(8,128)(2,1)S(1)} %fusion.1, bf16[32,64,128]{2,1,0:T(8,128)(2,1)S(1)} %copy-done.5), kind=kOutput, calls=%fused_computation.38 | convolution fusion | flops 33554432 | bytes 2097152 | tf_op jit(solution)/shard_map/bij,bjc->bic/dot_general | solution.py:15
  17.9 1.9 %rev.22 = bf16[4,2,4,64,128]{4,3,2,1,0:T(8,128)(2,1)} reverse(bf16[4,2,4,64,128]{4,3,2,1,0:T(8,128)(2,1)} %bitcast.97), dimensions={1} | reverse | bytes 1048576 | tf_op jit(solution)/shard_map/jit(_flip)/rev | solution.py:51
  19.8 1.9 %fusion.2 = bf16[32,128,64]{1,2,0:T(8,128)(2,1)S(1)} fusion(f32[32,128,64]{1,2,0:T(8,128)} %fusion.25, bf16[32,64,128]{2,1,0:T(8,128)(2,1)} %bitcast.103, bf16[32,64,128]{2,1,0:T(8,128)(2,1)} %get-tuple-element.7), kind=kOutput, calls=%fused_computation.15 | convolution fusion | flops 34078720 | bytes 2621440 | tf_op jit(solution)/shard_map/bij,bjc->bic/dot_general | solution.py:18
  21.8 1.3 %fusion.27 = f32[32,128,64]{1,2,0:T(8,128)} fusion(bf16[32,128,64]{1,2,0:T(8,128)(2,1)S(1)} %fusion.2, bf16[32,64,128]{2,1,0:T(8,128)(2,1)S(1)} %copy-done.4), kind=kOutput, calls=%fused_computation.40 | convolution fusion | flops 33554432 | bytes 2097152 | tf_op jit(solution)/shard_map/bij,bjc->bic/dot_general | solution.py:15
  23.1 1.9 %rev.23 = bf16[2,2,8,64,128]{4,3,2,1,0:T(8,128)(2,1)} reverse(bf16[2,2,8,64,128]{4,3,2,1,0:T(8,128)(2,1)} %bitcast.98), dimensions={1} | reverse | bytes 1048576 | tf_op jit(solution)/shard_map/jit(_flip)/rev | solution.py:51
  24.9 2.0 %fusion.3 = bf16[32,128,64]{1,2,0:T(8,128)(2,1)S(1)} fusion(f32[32,128,64]{1,2,0:T(8,128)} %fusion.27, bf16[32,64,128]{2,1,0:T(8,128)(2,1)} %bitcast.104, bf16[32,64,128]{2,1,0:T(8,128)(2,1)} %get-tuple-element.8), kind=kOutput, calls=%fused_computation.16 | convolution fusion | flops 34078720 | bytes 2621440 | tf_op jit(solution)/shard_map/bij,bjc->bic/dot_general | solution.py:18
  26.9 1.3 %fusion.29 = f32[32,128,64]{1,2,0:T(8,128)} fusion(bf16[32,128,64]{1,2,0:T(8,128)(2,1)S(1)} %fusion.3, bf16[32,64,128]{2,1,0:T(8,128)(2,1)S(1)} %copy-done.3), kind=kOutput, calls=%fused_computation.42 | convolution fusion | flops 33554432 | bytes 2097152 | tf_op jit(solution)/shard_map/bij,bjc->bic/dot_general | solution.py:15
  28.2 1.9 %rev.24 = bf16[1,2,16,64,128]{4,3,2,1,0:T(8,128)(2,1)} reverse(bf16[1,2,16,64,128]{4,3,2,1,0:T(8,128)(2,1)} %bitcast.99), dimensions={1} | reverse | bytes 1048576 | tf_op jit(solution)/shard_map/jit(_flip)/rev | solution.py:51
  30.1 1.9 %fusion.4 = bf16[32,128,64]{1,2,0:T(8,128)(2,1)S(1)} fusion(f32[32,128,64]{1,2,0:T(8,128)} %fusion.29, bf16[32,64,128]{2,1,0:T(8,128)(2,1)} %bitcast.105, bf16[32,64,128]{2,1,0:T(8,128)(2,1)} %get-tuple-element.9), kind=kOutput, calls=%fused_computation.17 | convolution fusion | flops 34078720 | bytes 2621440 | tf_op jit(solution)/shard_map/bij,bjc->bic/dot_general | solution.py:18
  32.8 1.2 %collective-permute-done = bf16[32,64,128]{2,1,0:T(8,128)(2,1)S(1)} collective-permute-done((bf16[32,64,128]{2,1,0:T(8,128)(2,1)S(1)}, bf16[32,64,128]{2,1,0:T(8,128)(2,1)S(1)}, u32[]{:S(2)}, u32[]{:S(2)}) %collective-permute-start) | collective-permute-done | bytes 524320 | tf_op jit(solution)/shard_map/ppermute | solution.py:10
  34.4 3.0 %collective-permute-start.1 = (bf16[32,64,128]{2,1,0:T(8,128)(2,1)S(1)}, bf16[32,64,128]{2,1,0:T(8,128)(2,1)S(1)}, u32[]{:S(2)}, u32[]{:S(2)}) collective-permute-start(bf16[32,64,128]{2,1,0:T(8,128)(2,1)S(1)} %bitcast.109), channel_id=1, source_target_pairs={{0,2},{1,3},{2,0},{3,1},{4,6},{5,7},{6,4},{7,5},{8,10},{9,11},{10,... | collective-permute-start | bytes 1572872 | tf_op jit(solution)/shard_map/ppermute | solution.py:10
  37.7 11.9 %collective-permute-done.1 = bf16[32,64,128]{2,1,0:T(8,128)(2,1)S(1)} collective-permute-done((bf16[32,64,128]{2,1,0:T(8,128)(2,1)S(1)}, bf16[32,64,128]{2,1,0:T(8,128)(2,1)S(1)}, u32[]{:S(2)}, u32[]{:S(2)}) %collective-permute-start.1) | collective-permute-done | bytes 524320 | tf_op jit(solution)/shard_map/ppermute | solution.py:10
  50.0 1.9 %collective-permute-start.2 = (bf16[32,64,128]{2,1,0:T(8,128)(2,1)S(1)}, bf16[32,64,128]{2,1,0:T(8,128)(2,1)S(1)}, u32[]{:S(2)}, u32[]{:S(2)}) collective-permute-start(bf16[32,64,128]{2,1,0:T(8,128)(2,1)S(1)} %bitcast.108), channel_id=1, source_target_pairs={{0,4},{1,5},{2,6},{3,7},{4,0},{5,1},{6,2},{7,3},{8,12},{9,13},{10,... | collective-permute-start | bytes 1572872 | tf_op jit(solution)/shard_map/ppermute | solution.py:10
  52.3 11.2 %collective-permute-done.2 = bf16[32,64,128]{2,1,0:T(8,128)(2,1)S(1)} collective-permute-done((bf16[32,64,128]{2,1,0:T(8,128)(2,1)S(1)}, bf16[32,64,128]{2,1,0:T(8,128)(2,1)S(1)}, u32[]{:S(2)}, u32[]{:S(2)}) %collective-permute-start.2) | collective-permute-done | bytes 524320 | tf_op jit(solution)/shard_map/ppermute | solution.py:10
  63.5 1.1 fusion.7
  64.7 2.5 %collective-permute-start.3 = (bf16[32,64,128]{2,1,0:T(8,128)(2,1)}, bf16[32,64,128]{2,1,0:T(8,128)(2,1)}, u32[]{:S(2)}, u32[]{:S(2)}) collective-permute-start(bf16[32,64,128]{2,1,0:T(8,128)(2,1)} %bitcast.28), channel_id=1, source_target_pairs={{0,8},{1,9},{2,10},{3,11},{4,12},{5,13},{6,14},{7,15},{8,0},{9,1},... | collective-permute-start | bytes 1572872 | tf_op jit(solution)/shard_map/ppermute | solution.py:10
  68.0 3.9 %all-to-all-start = ((s32[16,2,1]{1,2,0:T(1,128)}), s32[16,2,1]{1,2,0:T(1,128)S(1)}, u32[]{:S(2)}, u32[]{:S(2)}) async-start(s32[16,2,1]{1,2,0:T(1,128)} %bitcast), calls=%async_computation | async-start | bytes 16384 | tf_op jit(solution)/shard_map/all_to_all | solution.py:71
  71.9 1.3 %fusion.37 = f32[32,128,64]{1,2,0:T(8,128)S(1)} fusion(bf16[32,128,64]{1,2,0:T(8,128)(2,1)} %fusion.7, bf16[32,64,128]{2,1,0:T(8,128)(2,1)S(1)} %get-tuple-element.5), kind=kOutput, calls=%fused_computation.50 | convolution fusion | flops 33554432 | bytes 2097152 | tf_op jit(solution)/shard_map/bij,bjc->bic/dot_general | solution.py:15
  73.2 16.6 %collective-permute-done.3 = bf16[32,64,128]{2,1,0:T(8,128)(2,1)} collective-permute-done((bf16[32,64,128]{2,1,0:T(8,128)(2,1)}, bf16[32,64,128]{2,1,0:T(8,128)(2,1)}, u32[]{:S(2)}, u32[]{:S(2)}) %collective-permute-start.3) | collective-permute-done | bytes 524320 | tf_op jit(solution)/shard_map/ppermute | solution.py:10
  89.8 1.4 %fusion.8 = bf16[32,128,64]{1,2,0:T(8,128)(2,1)S(1)} fusion(f32[32,128,64]{1,2,0:T(8,128)S(1)} %fusion.37, bf16[32,64,128]{2,1,0:T(8,128)(2,1)} %collective-permute-done.3, bf16[32,64,128]{2,1,0:T(8,128)(2,1)S(1)} %get-tuple-element.5), kind=kOutput, calls=%fused_computation.21 | convolution fusion | flops 34078720 | bytes 2621440 | tf_op jit(solution)/shard_map/bij,bjc->bic/dot_general | solution.py:18
  91.6 1.1 all_to_all.13
  92.8 5.3 %all-to-all-start.1 = ((bf16[16,2,8192]{2,1,0:T(2,128)(2,1)}), bf16[16,2,8192]{2,1,0:T(2,128)(2,1)S(1)}, u32[]{:S(2)}, u32[]{:S(2)}) async-start(bf16[16,2,8192]{2,1,0:T(2,128)(2,1)} %all_to_all.13), calls=%async_computation.1 | async-start | bytes 1048576 | tf_op jit(solution)/shard_map/all_to_all | solution.py:70
  99.3 13.3 %all-to-all-done.1 = bf16[16,2,8192]{2,1,0:T(2,128)(2,1)S(1)} async-done(((bf16[16,2,8192]{2,1,0:T(2,128)(2,1)}), bf16[16,2,8192]{2,1,0:T(2,128)(2,1)S(1)}, u32[]{:S(2)}, u32[]{:S(2)}) %all-to-all-start.1) | async-done | bytes 524320 | tf_op jit(solution)/shard_map/all_to_all | solution.py:70
  114.0 2.1 %convert_bitcast_fusion = bf16[32,256,128]{1,2,0:T(8,128)(2,1)} fusion(bf16[32,64,128]{2,1,0:T(8,128)(2,1)S(1)} %bitcast.106, bf16[32,64,256]{2,1,0:T(8,128)(2,1)S(1)} %copy-done.14), kind=kOutput, calls=%fused_computation.2 | convolution fusion | flops 135266304 | bytes 3670016 | tf_op jit(solution)/shard_map/brl,brc->blc/dot_general | solution.py:78
  116.1 4.1 %copy.46 = bf16[32,256,128]{2,1,0:T(8,128)(2,1)} copy(bf16[32,256,128]{1,2,0:T(8,128)(2,1)} %convert_bitcast_fusion) | data formatting | bytes 4194304 | tf_op jit(solution)/shard_map/convert_element_type | solution.py:79
  (53 shorter events, 7.4 us)
Async XLA Ops:
  0.0 5.1 %copy-start = (bf16[8192,128]{1,0:T(8,128)(2,1)S(1)}, bf16[8192,128]{1,0:T(8,128)(2,1)}, u32[]{:S(2)}) copy-start(bf16[8192,128]{1,0:T(8,128)(2,1)} %param.5) | copy-start | bytes 6291460
  0.0 5.1 %copy-start.13 = (bf16[32,64,256]{2,1,0:T(8,128)(2,1)S(1)}, bf16[32,64,256]{2,1,0:T(8,128)(2,1)}, u32[]{:S(2)}) copy-start(bf16[32,64,256]{2,1,0:T(8,128)(2,1)} %param.6) | copy-start | bytes 3145732
  5.1 2.6 %copy-start.7 = (bf16[32,64,128]{2,1,0:T(8,128)(2,1)}, bf16[32,64,128]{2,1,0:T(8,128)(2,1)S(1)}, u32[]{:S(2)}) copy-start(bf16[32,64,128]{2,1,0:T(8,128)(2,1)S(1)} %get-tuple-element.13) | copy-start | bytes 1572868
  5.6 0.8 copy-start.12
  9.6 2.0 %copy-start.6 = (bf16[32,64,128]{2,1,0:T(8,128)(2,1)S(1)}, bf16[32,64,128]{2,1,0:T(8,128)(2,1)}, u32[]{:S(2)}) copy-start(bf16[32,64,128]{2,1,0:T(8,128)(2,1)} %get-tuple-element.6) | copy-start | bytes 1572868
  11.5 1.3 %copy-start.8 = (bf16[32,128,64]{1,2,0:T(8,128)(2,1)}, bf16[32,128,64]{1,2,0:T(8,128)(2,1)S(1)}, u32[]{:S(2)}) copy-start(bf16[32,128,64]{1,2,0:T(8,128)(2,1)S(1)} %fusion) | copy-start | bytes 1572868
  14.7 2.0 %copy-start.5 = (bf16[32,64,128]{2,1,0:T(8,128)(2,1)S(1)}, bf16[32,64,128]{2,1,0:T(8,128)(2,1)}, u32[]{:S(2)}) copy-start(bf16[32,64,128]{2,1,0:T(8,128)(2,1)} %get-tuple-element.7) | copy-start | bytes 1572868
  16.7 1.3 %copy-start.9 = (bf16[32,128,64]{1,2,0:T(8,128)(2,1)}, bf16[32,128,64]{1,2,0:T(8,128)(2,1)S(1)}, u32[]{:S(2)}) copy-start(bf16[32,128,64]{1,2,0:T(8,128)(2,1)S(1)} %fusion.1) | copy-start | bytes 1572868
  19.8 2.0 %copy-start.4 = (bf16[32,64,128]{2,1,0:T(8,128)(2,1)S(1)}, bf16[32,64,128]{2,1,0:T(8,128)(2,1)}, u32[]{:S(2)}) copy-start(bf16[32,64,128]{2,1,0:T(8,128)(2,1)} %get-tuple-element.8) | copy-start | bytes 1572868
  21.8 1.3 %copy-start.10 = (bf16[32,128,64]{1,2,0:T(8,128)(2,1)}, bf16[32,128,64]{1,2,0:T(8,128)(2,1)S(1)}, u32[]{:S(2)}) copy-start(bf16[32,128,64]{1,2,0:T(8,128)(2,1)S(1)} %fusion.2) | copy-start | bytes 1572868
  24.9 2.0 %copy-start.3 = (bf16[32,64,128]{2,1,0:T(8,128)(2,1)S(1)}, bf16[32,64,128]{2,1,0:T(8,128)(2,1)}, u32[]{:S(2)}) copy-start(bf16[32,64,128]{2,1,0:T(8,128)(2,1)} %get-tuple-element.9) | copy-start | bytes 1572868
  26.9 1.3 %copy-start.11 = (bf16[32,128,64]{1,2,0:T(8,128)(2,1)}, bf16[32,128,64]{1,2,0:T(8,128)(2,1)S(1)}, u32[]{:S(2)}) copy-start(bf16[32,128,64]{1,2,0:T(8,128)(2,1)S(1)} %fusion.3) | copy-start | bytes 1572868
  30.1 2.5 %copy-start.2 = (bf16[32,64,128]{2,1,0:T(8,128)(2,1)S(1)}, bf16[32,64,128]{2,1,0:T(8,128)(2,1)}, u32[]{:S(2)}) copy-start(bf16[32,64,128]{2,1,0:T(8,128)(2,1)} %get-tuple-element.10) | copy-start | bytes 1572868
  32.0 2.0 %collective-permute-start = (bf16[32,64,128]{2,1,0:T(8,128)(2,1)S(1)}, bf16[32,64,128]{2,1,0:T(8,128)(2,1)S(1)}, u32[]{:S(2)}, u32[]{:S(2)}) collective-permute-start(bf16[32,64,128]{2,1,0:T(8,128)(2,1)S(1)} %bitcast.110), channel_id=1, source_target_pairs={{0,1},{1,0},{2,3},{3,2},{4,5},{5,4},{6,7},{7,6},{8,9},{9,8},{10,11... | collective-permute-start | bytes 1572872 | tf_op jit(solution)/shard_map/ppermute | solution.py:10
  32.5 4.9 %copy-start.15 = (s32[32]{0:T(128)S(1)}, s32[32]{0:T(128)}, u32[]{:S(2)}) copy-start(s32[32]{0:T(128)} %param.8) | copy-start | bytes 388
  32.5 4.9 %copy-start.1 = (bf16[32,64,128]{2,1,0:T(8,128)(2,1)S(1)}, bf16[32,64,128]{2,1,0:T(8,128)(2,1)}, u32[]{:S(2)}) copy-start(bf16[32,64,128]{2,1,0:T(8,128)(2,1)} %get-tuple-element.11) | copy-start | bytes 1572868
  34.4 15.2 %collective-permute-start.1 = (bf16[32,64,128]{2,1,0:T(8,128)(2,1)S(1)}, bf16[32,64,128]{2,1,0:T(8,128)(2,1)S(1)}, u32[]{:S(2)}, u32[]{:S(2)}) collective-permute-start(bf16[32,64,128]{2,1,0:T(8,128)(2,1)S(1)} %bitcast.109), channel_id=1, source_target_pairs={{0,2},{1,3},{2,0},{3,1},{4,6},{5,7},{6,4},{7,5},{8,10},{9,11},{10,... | collective-permute-start | bytes 1572872 | tf_op jit(solution)/shard_map/ppermute | solution.py:10
  50.0 13.5 %collective-permute-start.2 = (bf16[32,64,128]{2,1,0:T(8,128)(2,1)S(1)}, bf16[32,64,128]{2,1,0:T(8,128)(2,1)S(1)}, u32[]{:S(2)}, u32[]{:S(2)}) collective-permute-start(bf16[32,64,128]{2,1,0:T(8,128)(2,1)S(1)} %bitcast.108), channel_id=1, source_target_pairs={{0,4},{1,5},{2,6},{3,7},{4,0},{5,1},{6,2},{7,3},{8,12},{9,13},{10,... | collective-permute-start | bytes 1572872 | tf_op jit(solution)/shard_map/ppermute | solution.py:10
  64.7 25.1 %collective-permute-start.3 = (bf16[32,64,128]{2,1,0:T(8,128)(2,1)}, bf16[32,64,128]{2,1,0:T(8,128)(2,1)}, u32[]{:S(2)}, u32[]{:S(2)}) collective-permute-start(bf16[32,64,128]{2,1,0:T(8,128)(2,1)} %bitcast.28), channel_id=1, source_target_pairs={{0,8},{1,9},{2,10},{3,11},{4,12},{5,13},{6,14},{7,15},{8,0},{9,1},... | collective-permute-start | bytes 1572872 | tf_op jit(solution)/shard_map/ppermute | solution.py:10
  68.0 24.8 %all-to-all-start = ((s32[16,2,1]{1,2,0:T(1,128)}), s32[16,2,1]{1,2,0:T(1,128)S(1)}, u32[]{:S(2)}, u32[]{:S(2)}) async-start(s32[16,2,1]{1,2,0:T(1,128)} %bitcast), calls=%async_computation | async-start | bytes 16384 | tf_op jit(solution)/shard_map/all_to_all | solution.py:71
  92.8 19.8 %all-to-all-start.1 = ((bf16[16,2,8192]{2,1,0:T(2,128)(2,1)}), bf16[16,2,8192]{2,1,0:T(2,128)(2,1)S(1)}, u32[]{:S(2)}, u32[]{:S(2)}) async-start(bf16[16,2,8192]{2,1,0:T(2,128)(2,1)} %all_to_all.13), calls=%async_computation.1 | async-start | bytes 1048576 | tf_op jit(solution)/shard_map/all_to_all | solution.py:70
  112.8 1.2 %copy-start.14 = (bf16[32,64,256]{2,1,0:T(8,128)(2,1)S(1)}, bf16[32,64,256]{2,1,0:T(8,128)(2,1)}, u32[]{:S(2)}) copy-start(bf16[32,64,256]{2,1,0:T(8,128)(2,1)} %param.9) | copy-start | bytes 3145732
where the time goes:
time: 121 us; the launch traced here: 120 us
  waiting for transfers between devices  54.3 us (45%)
  matrix products  24.7 us (20%)
  local copies, waits for them, and re-layouts  23 us (19%)
  starting transfers between devices  17.1 us (14%)
    ppermute x4, waiting for transfers between devices, from_partner(): return lax.ppermute(value, axis, pairs)  40.9 us
    all_to_all x1, waiting for transfers between devices, per_device(): lax.all_to_all(outgoing, ('bfly', 'rhs'), split_axis=0, concat_axis=0, ti...  13.3 us
    dot_general x9, matrix products, combine(): jnp.einsum('bij,bjc->bic', matrices[:, :, width:], partner_part, preferre...  13 us
    rev x5, local copies, waits for them, and re-layouts, per_device(): jnp.flip(blocks, 1).reshape(box_count, rank_width, column_count)  9.43 us
    dot_general x9, matrix products, combine(): jnp.einsum('bij,bjc->bic', matrices[:, :, :width], current, preferred_ele...  8.45 us
    ppermute x4, starting transfers between devices, from_partner(): return lax.ppermute(value, axis, pairs)  7.82 us
    all_to_all x1, starting transfers between devices, per_device(): lax.all_to_all(outgoing, ('bfly', 'rhs'), split_axis=0, concat_axis=0, ti...  5.35 us
    squeeze x1, local copies, waits for them, and re-layouts, per_device(): translations[:, local_levels + section_index]  5.1 us
  transfers between devices with their start and end apart: 6, of which 5 were waited for; matrix products, arithmetic and copies ran while one was open for 5% of the time, Pallas kernels for 0%

commit v1 on v0

v1 whole, which is shorter than its diff:
```python
import jax
import jax.numpy as jnp
from jax import lax
from jax.experimental import pallas as pl
from jax.experimental.pallas import tpu as pltpu
from jax.sharding import PartitionSpec as P

AXES = ("bfly", "rhs")
BF16 = jnp.bfloat16
TILE = 16
VMEM_LIMIT = 48 * 2**20


def from_partner(value, axis, distance):
    mask = 2**distance
    pairs = [(source, source ^ mask) for source in range(lax.axis_size(axis))]
    return lax.ppermute(value, axis, pairs)


def combine(current, partner_part, matrices):
    width = current.shape[1]
    own_term = jnp.einsum(
        "bij,bjc->bic", matrices[:, :, :width], current, preferred_element_type=jnp.float32
    )
    other_term = jnp.einsum(
        "bij,bjc->bic", matrices[:, :, width:], partner_part, preferred_element_type=jnp.float32
    )
    return (own_term + other_term).astype(BF16)


def pack_slots(flat_coefficients, slot_key, capacity, slot_total, target_spot):
    box_count = flat_coefficients.shape[0]
    box_iota = jnp.arange(box_count, dtype=jnp.int32)
    earlier = (slot_key[:, None] == slot_key[None, :]) & (box_iota[None, :] < box_iota[:, None])
    order_within = jnp.sum(earlier.astype(jnp.int32), axis=1)
    slot_of_box = slot_key * capacity + order_within
    selector = jnp.arange(slot_total, dtype=jnp.int32)[:, None] == slot_of_box[None, :]
    outgoing = jnp.dot(
        selector.astype(BF16), flat_coefficients, preferred_element_type=jnp.float32
    ).astype(BF16)
    outgoing_spot = jnp.sum(jnp.where(selector, target_spot[None, :] + 1, 0), axis=1) - 1
    return (outgoing, outgoing_spot)


def exchange_every_level(right_sides, leaf_basis, translations, node_target, out_basis):
    box_count = leaf_basis.shape[0]
    rank_width = leaf_basis.shape[1]
    leaf_rows = leaf_basis.shape[2]
    column_count = right_sides.shape[1]
    point_rows = right_sides.reshape(box_count, leaf_rows, column_count)
    coefficients = jnp.einsum(
        "brl,blc->brc", leaf_basis, point_rows, preferred_element_type=jnp.float32
    ).astype(BF16)
    local_levels = box_count.bit_length() - 1
    for level_index in range(local_levels):
        span = 2**level_index
        blocks = coefficients.reshape(box_count // (2 * span), 2, span, rank_width, column_count)
        partner_part = jnp.flip(blocks, 1).reshape(box_count, rank_width, column_count)
        coefficients = combine(coefficients, partner_part, translations[:, level_index])
    device_count = lax.axis_size(AXES)
    device_levels = device_count.bit_length() - 1
    for section_index in range(device_levels):
        partner_part = from_partner(coefficients, AXES, section_index)
        coefficients = combine(
            coefficients, partner_part, translations[:, local_levels + section_index]
        )
    target_device = node_target // box_count
    target_spot = node_target % box_count
    box_iota = jnp.arange(box_count, dtype=jnp.int32)
    flat_coefficients = coefficients.reshape(box_count, rank_width * column_count)
    capacity = max(1, box_count // device_count)
    slot_total = device_count * capacity
    outgoing, outgoing_spot = pack_slots(
        flat_coefficients, target_device, capacity, slot_total, target_spot
    )
    incoming, incoming_spot = (
        lax.all_to_all(outgoing, AXES, split_axis=0, concat_axis=0, tiled=True),
        lax.all_to_all(outgoing_spot, AXES, split_axis=0, concat_axis=0, tiled=True),
    )
    placement_table = (box_iota[:, None] == incoming_spot[None, :]).astype(BF16)
    placed = jnp.dot(placement_table, incoming, preferred_element_type=jnp.float32).astype(BF16)
    placed = placed.reshape(box_count, rank_width, column_count)
    applied = jnp.einsum("brl,brc->blc", out_basis, placed, preferred_element_type=jnp.float32)
    return applied.astype(BF16).reshape(box_count * leaf_rows, column_count)


def low_index(place, i4, i0):
    z0, y, c = place >> 2, place >> 1 & 1, place & 1
    return i4 * 16 + c * 8 + y * 4 + z0 * 2 + i0


def product(matrix, rows):
    return jnp.dot(matrix, rows, preferred_element_type=jnp.float32).astype(BF16)


def half_index():
    return lax.axis_index("bfly") // (lax.axis_size("bfly") // 2)


def pack_kernel(rank, target_ref, trans_ref, early_ref, late_ref, spots, sem, spot_sem):
    mine = half_index()
    copies = []
    for place in range(8):
        for slot in range(4):
            box = low_index(place, slot & 1, slot >> 1)
            for level in range(2):
                rows = pl.ds((slot * 2 + level) * rank, rank)
                copies.append((trans_ref.at[box, 6 + level], early_ref.at[place, rows]))
        for i4 in range(2):
            box = low_index(place, i4, 0)
            rows = pl.ds((8 + i4) * rank, rank)
            copies.append((trans_ref.at[box + mine, 8], early_ref.at[place, rows]))
            rows = pl.ds(i4 * rank, rank)
            copies.append((trans_ref.at[box + 1 - mine, 8], late_ref.at[place, rows]))
    copies = [pltpu.make_async_copy(source, target, sem) for source, target in copies]
    for copy in copies:
        copy.start()
    first = lax.broadcasted_iota(jnp.int32, (TILE, spots.shape[-1]), 0) == 0
    for place in range(8):
        for side, bit in enumerate((mine, 1 - mine)):
            spot = [target_ref[low_index(place, i4, 0) + bit] % 32 for i4 in range(2)]
            tile = jnp.where(first, spot[0], spot[1]).astype(jnp.float32)
            spots[side, place] = tile.astype(BF16)
    tiles = []
    for place in range(8):
        tiles.append((spots.at[0, place], early_ref.at[place, pl.ds(10 * rank, TILE)]))
        tiles.append((spots.at[1, place], late_ref.at[place, pl.ds(2 * rank, TILE)]))
    tiles = [pltpu.make_async_copy(source, target, spot_sem) for source, target in tiles]
    for copy in tiles:
        copy.start()
    for copy in copies + tiles:
        copy.wait()


def local_kernel(levels, rs_ref, leaf_ref, trans_ref, out_ref, rs, leaf, trans, ping, pong, sem, trans_sem):
    boxes = leaf_ref.shape[0]
    step = boxes // 4
    loads = []
    for part in range(4):
        rows = pl.ds(part * step, step)
        loads.append(
            (
                pltpu.make_async_copy(rs_ref.at[rows], rs.at[rows], sem.at[part, 0]),
                pltpu.make_async_copy(leaf_ref.at[rows], leaf.at[rows], sem.at[part, 1]),
            )
        )
    level_loads = [
        pltpu.make_async_copy(trans_ref.at[:, level], trans.at[level], trans_sem.at[level])
        for level in range(levels)
    ]
    for pair in loads:
        for copy in pair:
            copy.start()
    for copy in level_loads:
        copy.start()
    for part in range(4):
        for copy in loads[part]:
            copy.wait()
        for box in range(part * step, (part + 1) * step):
            ping[box] = product(leaf[box], rs[box])
    source, target = ping, pong
    for level in range(levels):
        level_loads[level].wait()
        if level == levels - 1:
            target = out_ref
        for box in range(boxes):
            rows = jnp.concatenate([source[box], source[box ^ (1 << level)]], axis=0)
            target[box] = product(trans[level, box], rows)
        source, target = target, source


def chip_kernel(level, own_ref, other_ref, trans_ref, out_ref, trans, sem):
    load = pltpu.make_async_copy(trans_ref.at[:, level], trans, sem)
    load.start()
    load.wait()
    for place in range(8):
        for slot in range(4):
            box = low_index(place, slot & 1, slot >> 1)
            rows = jnp.concatenate([own_ref[box], other_ref[box]], axis=0)
            out_ref[place, slot] = product(trans[box], rows)


def quad_kernel(rank, box_ref, trans_ref, keep_ref, send_ref, middle):
    for place in range(8):
        for slot in range(4):
            rows = jnp.concatenate([box_ref[place, slot], box_ref[place ^ 2, slot]], axis=0)
            middle[place, slot] = product(trans_ref[place, pl.ds(slot * 2 * rank, rank)], rows)
    mine = half_index()
    for place in range(8):
        for i4 in range(2):
            for out_ref, bit in ((keep_ref, mine), (send_ref, 1 - mine)):
                slot = bit * 2 + i4
                rows = jnp.concatenate([middle[place, slot], middle[place ^ 4, slot]], axis=0)
                start = pl.multiple_of((slot * 2 + 1) * rank, rank)
                out_ref[place, i4] = product(trans_ref[place, pl.ds(start, rank)], rows)


def final_kernel(rank, keep_ref, recv_ref, early_ref, late_ref, basis_ref, out_ref, result, sem):
    copies = []
    for place in range(8):
        spots = [
            ref[place, pl.ds(start, TILE), :].astype(jnp.float32)
            for ref, start in ((early_ref, 10 * rank), (late_ref, 2 * rank))
        ]
        for i4 in range(2):
            own, other = keep_ref[place, i4], recv_ref[place, i4]
            for side, (ref, start, first, second) in enumerate(
                ((early_ref, 8 + i4, own, other), (late_ref, i4, other, own))
            ):
                rows = jnp.concatenate([first, second], axis=0)
                box = product(ref[place, pl.ds(start * rank, rank)], rows)
                spot = jnp.max(spots[side][i4 : i4 + 1]).astype(jnp.int32)
                slot = place * 4 + i4 * 2 + side
                result[slot] = lax.dot_general(
                    basis_ref[spot],
                    box,
                    (((0,), (0,)), ((), ())),
                    preferred_element_type=jnp.float32,
                ).astype(BF16)
                copy = pltpu.make_async_copy(result.at[slot], out_ref.at[spot], sem)
                copy.start()
                copies.append(copy)
    for copy in copies:
        copy.wait()


def call(kernel, out_shapes, in_spaces, out_spaces, scratch, flops, moved):
    return pl.pallas_call(
        kernel,
        out_shape=out_shapes,
        in_specs=[pl.BlockSpec(memory_space=space) for space in in_spaces],
        out_specs=jax.tree.map(lambda space: pl.BlockSpec(memory_space=space), out_spaces),
        scratch_shapes=scratch,
        compiler_params=pltpu.CompilerParams(vmem_limit_bytes=VMEM_LIMIT),
        cost_estimate=pl.CostEstimate(flops=flops, bytes_accessed=moved, transcendentals=0),
    )


def shape(*dims):
    return jax.ShapeDtypeStruct(dims, BF16)


def bind(kernel, *values):
    return lambda *refs: kernel(*values, *refs)


def move_early(right_sides, leaf_basis, translations, node_target, out_basis):
    boxes, rank, leaf_rows = leaf_basis.shape
    columns = right_sides.shape[1]
    local_levels = boxes.bit_length() - 1
    width = 2 * rank
    block = 2 * rank * columns * 2
    any_, vmem, smem, dma = pl.ANY, pltpu.VMEM, pltpu.SMEM, pltpu.SemaphoreType.DMA
    eighths = [list(range(8)), list(range(8, 16))]

    def among_eight(value):
        rows = value.reshape(-1, value.shape[-1])
        out = lax.all_to_all(rows, AXES, 0, 0, axis_index_groups=eighths, tiled=True)
        return out.reshape(value.shape)

    def across(value):
        return lax.ppermute(value, AXES, [(s, s ^ 8) for s in range(16)])

    early, late = call(
        bind(pack_kernel, rank),
        (shape(8, 10 * rank + TILE, width), shape(8, 2 * rank + TILE, width)),
        (smem, any_),
        (any_, any_),
        [vmem((2, 8, TILE, width), BF16), dma, dma],
        0,
        3 * 2**20,
    )(node_target, translations)
    early = among_eight(early)
    late = across(late)
    coefficients = call(
        bind(local_kernel, local_levels),
        shape(boxes, rank, columns),
        (any_, any_, any_),
        vmem,
        [
            vmem((boxes, leaf_rows, columns), BF16),
            vmem((boxes, rank, leaf_rows), BF16),
            vmem((local_levels, boxes, rank, width), BF16),
            vmem((boxes, rank, columns), BF16),
            vmem((boxes, rank, columns), BF16),
            dma((4, 2)),
            dma((local_levels,)),
        ],
        boxes * rank * columns * 2 * (leaf_rows + local_levels * width),
        6 * 2**20,
    )(right_sides.reshape(boxes, leaf_rows, columns), leaf_basis, translations)
    partner = from_partner(coefficients, AXES, 0)
    coefficients = call(
        bind(chip_kernel, local_levels),
        shape(8, 4, rank, columns),
        (vmem, vmem, any_),
        vmem,
        [vmem((boxes, rank, width), BF16), dma],
        boxes * block * width,
        2**21,
    )(coefficients, partner, translations)
    coefficients = among_eight(coefficients)
    keep, send = call(
        bind(quad_kernel, rank),
        (shape(8, 2, rank, columns), shape(8, 2, rank, columns)),
        (vmem, vmem),
        (vmem, vmem),
        [vmem((8, 4, rank, columns), BF16)],
        2 * boxes * block * width,
        2**21,
    )(coefficients, early)
    received = across(send)
    late = among_eight(late)
    applied = call(
        bind(final_kernel, rank),
        shape(boxes, leaf_rows, columns),
        (vmem, vmem, vmem, vmem, vmem),
        any_,
        [vmem((boxes, leaf_rows, columns), BF16), dma],
        3 * boxes * block * width,
        2**22,
    )(keep, received, early, late, out_basis)
    return applied.reshape(boxes * leaf_rows, columns)


def solution(mesh):
    in_specs = (
        P(("groups", "bfly", "rhs"), None),
        P(("bfly", "rhs"), None, None),
        P(("bfly", "rhs"), None, None, None),
        P(("bfly", "rhs")),
        P(("bfly", "rhs"), None, None),
    )
    out_specs = P(("groups", "bfly", "rhs"), None)

    def per_device(right_sides, leaf_basis, translations, node_target, out_basis):
        devices = lax.axis_size(AXES)
        fits = devices == 16 and leaf_basis.shape[0] == 32
        apply = move_early if fits else exchange_every_level
        return apply(right_sides, leaf_basis, translations, node_target, out_basis)

    return jax.shard_map(
        per_device, mesh=mesh, in_specs=in_specs, out_specs=out_specs, check_vma=False
    )
```

time: 121 us -> 111 us (0.917)
  Pallas kernels: 0 us -> 52.1 us
  matrix products: 24.7 us -> 0 us
  local copies, waits for them, and re-layouts: 23 us -> 2.83 us
  waiting for transfers between devices: 54.3 us -> 37.9 us
    pallas_call x0 -> x5, Pallas kernels: none -> 52.1 us  [the longest x1 41.4 us: move_early(): call(bind(pack_kernel, rank), (shape(8, 10 * rank + TILE, width), shape(8...]
    ppermute x4 -> x1, waiting for transfers between devices: 40.9 us -> 1.54 us  [from_partner(): return lax.ppermute(value, axis, pairs)]
    ppermute x0 -> x2, waiting for transfers between devices: none -> 28.7 us  [across(): return lax.ppermute(value, AXES, [(s, s ^ 8) for s in range(16)])]
    dot_general x22 -> x0, matrix products: 24.7 us -> none  [the longest x9 13 us: combine(): jnp.einsum('bij,bjc->bic', matrices[:, :, width:], partner_part, preferre...]
    rev x5 -> x0, local copies, waits for them, and re-layouts: 9.43 us -> none  [per_device(): jnp.flip(blocks, 1).reshape(box_count, rank_width, column_count)]
    ppermute x4 -> x1, starting transfers between devices: 7.82 us -> 0.52 us  [from_partner(): return lax.ppermute(value, axis, pairs)]
    all_to_all x2 -> x3, waiting for transfers between devices: 13.3 us -> 7.68 us  [among_eight(): lax.all_to_all(rows, AXES, 0, 0, axis_index_groups=eighths, tiled=True)]
    all_to_all x2 -> x3, starting transfers between devices: 9.26 us -> 14.4 us  [among_eight(): lax.all_to_all(rows, AXES, 0, 0, axis_index_groups=eighths, tiled=True)]
  transfers between devices with their start and end apart: 6 -> 6, of which waited for: 5 -> 5; matrix products, arithmetic and copies ran while one was open for 5% -> 0% of each run, Pallas kernels for 0% -> 39%
where the time goes in v1:
time: 111 us
  Pallas kernels  52.1 us (47%)
  waiting for transfers between devices  37.9 us (34%)
  starting transfers between devices  18 us (16%)
  local copies, waits for them, and re-layouts  2.83 us (3%)
    pallas_call x1, Pallas kernels, move_early(): call(bind(pack_kernel, rank), (shape(8, 10 * rank + TILE, width), shape(8...  41.4 us
    ppermute x2, waiting for transfers between devices, across(): return lax.ppermute(value, AXES, [(s, s ^ 8) for s in range(16)])  28.7 us
    all_to_all x3, starting transfers between devices, among_eight(): lax.all_to_all(rows, AXES, 0, 0, axis_index_groups=eighths, tiled=True)  14.4 us
    all_to_all x3, waiting for transfers between devices, among_eight(): lax.all_to_all(rows, AXES, 0, 0, axis_index_groups=eighths, tiled=True)  7.68 us
    pallas_call x1, Pallas kernels, move_early(): call(bind(final_kernel, rank), shape(boxes, leaf_rows, columns), (vmem, v...  3.58 us
    pallas_call x1, Pallas kernels, move_early(): call(bind(local_kernel, local_levels), shape(boxes, rank, columns), (any_...  3.42 us
    ppermute x2, starting transfers between devices, across(): return lax.ppermute(value, AXES, [(s, s ^ 8) for s in range(16)])  3.04 us
    unnamed x8, local copies, waits for them, and re-layouts  2.83 us
  transfers between devices with their start and end apart: 6, of which 5 were waited for; matrix products, arithmetic and copies ran while one was open for 0% of the time, Pallas kernels for 39%

profile of v1, /device:TPU:0, one launch (start us, length us, event | category | flops | bytes accessed | tf_op | source)
XLA Modules:
  0.0 110.9 jit_solution(14671804840910140744)
XLA Ops:
  0.0 0.0 copy-start
  0.0 1.6 %copy-done = bf16[8192,128]{1,0:T(8,128)(2,1)S(1)} copy-done((bf16[8192,128]{1,0:T(8,128)(2,1)S(1)}, bf16[8192,128]{1,0:T(8,128)(2,1)}, u32[]{:S(2)}) %copy-start) | copy-done | bytes 2097176
  1.6 0.0 copy-start.2
  1.6 1.2 %copy-done.2 = bf16[32,64,256]{2,1,0:T(8,128)(2,1)S(1)} copy-done((bf16[32,64,256]{2,1,0:T(8,128)(2,1)S(1)}, bf16[32,64,256]{2,1,0:T(8,128)(2,1)}, u32[]{:S(2)}) %copy-start.2) | copy-done | bytes 1048600
  2.8 3.4 %shard_map.55.refs_0_ = bf16[32,64,128]{2,1,0:T(8,128)(2,1)S(1)} custom-call(bf16[32,256,128]{2,1,0:T(8,128)(2,1)S(1)} %bitcast.5, bf16[32,64,256]{2,1,0:T(8,128)(2,1)S(1)} %copy-done.2, bf16[32,9,64,128]{3,2,1,0:T(8,128)(2,1)} %refs_1_.3), custom_call_target="tpu_custom_call" | custom-call | flops 469762048 | bytes 6291456 | tf_op jit(solution)/shard_map/pallas_call | solution.py:275
  6.2 0.0 copy-start.3
  6.3 0.5 collective-permute-start
  6.8 1.5 %collective-permute-done.refs_1_ = bf16[32,64,128]{2,1,0:T(8,128)(2,1)S(1)} collective-permute-done((bf16[32,64,128]{2,1,0:T(8,128)(2,1)S(1)}, bf16[32,64,128]{2,1,0:T(8,128)(2,1)S(1)}, u32[]{:S(2)}, u32[]{:S(2)}) %collective-permute-start) | collective-permute-done | bytes 524320 | tf_op jit(solution)/shard_map/ppermute | solution.py:17
  8.3 2.2 %shard_map.56 = bf16[8,4,64,128]{3,2,1,0:T(8,128)(2,1)} custom-call(bf16[32,64,128]{2,1,0:T(8,128)(2,1)S(1)} %shard_map.55.refs_0_, bf16[32,64,128]{2,1,0:T(8,128)(2,1)S(1)} %collective-permute-done.refs_1_, bf16[32,9,64,128]{3,2,1,0:T(8,128)(2,1)} %refs_1_.3), custom_call_target="tpu_custom_call" | custom-call | flops 134217728 | bytes 2097152 | tf_op jit(solution)/shard_map/pallas_call | solution.py:293
  10.6 5.2 %all-to-all-start = ((bf16[8,256,128]{2,1,0:T(8,128)(2,1)}), bf16[8,256,128]{2,1,0:T(8,128)(2,1)S(1)}, u32[]{:S(2)}, u32[]{:S(2)}) async-start(bf16[8,256,128]{2,1,0:T(8,128)(2,1)} %bitcast.1), calls=%async_computation | async-start | bytes 1048576 | tf_op jit(solution)/shard_map/all_to_all | solution.py:258
  15.8 0.0 copy-done.3
  15.8 41.4 %shard_map.57 = (bf16[8,656,128]{2,1,0:T(8,128)(2,1)}, bf16[8,144,128]{2,1,0:T(8,128)(2,1)S(1)}) custom-call(s32[32]{0:T(128)S(1)} %copy-done.3, bf16[32,9,64,128]{3,2,1,0:T(8,128)(2,1)} %refs_1_.3), custom_call_target="tpu_custom_call" | custom-call | bytes 3145728 | tf_op jit(solution)/shard_map/pallas_call | solution.py:264
  57.1 0.0 all-to-all-done
  57.1 0.0 copy-start.1
  57.2 4.3 %all-to-all-start.1 = ((bf16[8,656,128]{2,1,0:T(8,128)(2,1)}), bf16[8,656,128]{2,1,0:T(8,128)(2,1)S(1)}, u32[]{:S(2)}, u32[]{:S(2)}) async-start(bf16[8,656,128]{2,1,0:T(8,128)(2,1)} %get-tuple-element.9), calls=%async_computation.1 | async-start | bytes 2686976 | tf_op jit(solution)/shard_map/all_to_all | solution.py:258
  61.5 2.6 %collective-permute-start.2 = (bf16[8,144,128]{2,1,0:T(8,128)(2,1)S(1)}, bf16[8,144,128]{2,1,0:T(8,128)(2,1)}, u32[]{:S(2)}, u32[]{:S(2)}) collective-permute-start(bf16[8,144,128]{2,1,0:T(8,128)(2,1)S(1)} %get-tuple-element.12), channel_id=1, source_target_pairs={{0,8},{1,9},{2,10},{3,11},{4,12},{5,13},{6,14},{7,15},{8,0},{9,1},... | collective-permute-start | bytes 884744 | tf_op jit(solution)/shard_map/ppermute | solution.py:262
  64.1 19.3 %collective-permute-done.2 = bf16[8,144,128]{2,1,0:T(8,128)(2,1)} collective-permute-done((bf16[8,144,128]{2,1,0:T(8,128)(2,1)S(1)}, bf16[8,144,128]{2,1,0:T(8,128)(2,1)}, u32[]{:S(2)}, u32[]{:S(2)}) %collective-permute-start.2) | collective-permute-done | bytes 294944 | tf_op jit(solution)/shard_map/ppermute | solution.py:262
  83.4 2.1 %all-to-all-done.1.refs_1_.refs_2_ = bf16[8,656,128]{2,1,0:T(8,128)(2,1)S(1)} async-done(((bf16[8,656,128]{2,1,0:T(8,128)(2,1)}), bf16[8,656,128]{2,1,0:T(8,128)(2,1)S(1)}, u32[]{:S(2)}, u32[]{:S(2)}) %all-to-all-start.1) | async-done | bytes 1343520 | tf_op jit(solution)/shard_map/all_to_all | solution.py:258
  85.4 4.9 %all-to-all-start.2 = ((bf16[8,144,128]{2,1,0:T(8,128)(2,1)}), bf16[8,144,128]{2,1,0:T(8,128)(2,1)S(1)}, u32[]{:S(2)}, u32[]{:S(2)}) async-start(bf16[8,144,128]{2,1,0:T(8,128)(2,1)} %collective-permute-done.2), calls=%async_computation.2 | async-start | bytes 589824 | tf_op jit(solution)/shard_map/all_to_all | solution.py:258
  90.3 1.5 %shard_map.58 = (bf16[8,2,64,128]{3,2,1,0:T(8,128)(2,1)S(1)}, bf16[8,2,64,128]{3,2,1,0:T(8,128)(2,1)}) custom-call(bf16[8,4,64,128]{3,2,1,0:T(8,128)(2,1)S(1)} %bitcast.4, bf16[8,656,128]{2,1,0:T(8,128)(2,1)S(1)} %all-to-all-done.1.refs_1_.refs_2_), custom_call_target="tpu_custom_call" | custom-call | flops 268435456 | bytes 2097152 | tf_op jit(solution)/shard_map/pallas_call | solution.py:303
  91.8 0.5 collective-permute-start.1
  92.3 5.6 %all-to-all-done.2.refs_3_ = bf16[8,144,128]{2,1,0:T(8,128)(2,1)S(1)} async-done(((bf16[8,144,128]{2,1,0:T(8,128)(2,1)}), bf16[8,144,128]{2,1,0:T(8,128)(2,1)S(1)}, u32[]{:S(2)}, u32[]{:S(2)}) %all-to-all-start.2) | async-done | bytes 294944 | tf_op jit(solution)/shard_map/all_to_all | solution.py:258
  97.9 9.4 %collective-permute-done.1.refs_1_ = bf16[8,2,64,128]{3,2,1,0:T(8,128)(2,1)S(1)} collective-permute-done((bf16[8,2,64,128]{3,2,1,0:T(8,128)(2,1)}, bf16[8,2,64,128]{3,2,1,0:T(8,128)(2,1)S(1)}, u32[]{:S(2)}, u32[]{:S(2)}) %collective-permute-start.1) | collective-permute-done | bytes 262176 | tf_op jit(solution)/shard_map/ppermute | solution.py:262
  107.3 0.0 copy-done.1
  107.3 3.6 %shard_map.59 = bf16[32,256,128]{2,1,0:T(8,128)(2,1)} custom-call(bf16[8,2,64,128]{3,2,1,0:T(8,128)(2,1)S(1)} %get-tuple-element.10.refs_0_, bf16[8,2,64,128]{3,2,1,0:T(8,128)(2,1)S(1)} %collective-permute-done.1.refs_1_, bf16[8,656,128]{2,1,0:T(8,128)(2,1)S(1)} %all-to-all-done.1.refs_1_.refs_2_, bf16[8,144,128]{2,1,0:T(8,128)(2,1)S(1)} %all-to-all-done.2.refs_3_, ...), custom_call_target="tpu_custom_call" | custom-call | flops 402653184 | bytes 4194304 | tf_op jit(solution)/shard_map/pallas_call | solution.py:314
Async XLA Ops:
  0.0 1.6 %copy-start = (bf16[8192,128]{1,0:T(8,128)(2,1)S(1)}, bf16[8192,128]{1,0:T(8,128)(2,1)}, u32[]{:S(2)}) copy-start(bf16[8192,128]{1,0:T(8,128)(2,1)} %param.5) | copy-start | bytes 6291460
  1.6 1.2 %copy-start.2 = (bf16[32,64,256]{2,1,0:T(8,128)(2,1)S(1)}, bf16[32,64,256]{2,1,0:T(8,128)(2,1)}, u32[]{:S(2)}) copy-start(bf16[32,64,256]{2,1,0:T(8,128)(2,1)} %refs_1_.2) | copy-start | bytes 3145732
  6.2 9.5 %copy-start.3 = (s32[32]{0:T(128)S(1)}, s32[32]{0:T(128)}, u32[]{:S(2)}) copy-start(s32[32]{0:T(128)} %refs_0_.1) | copy-start | bytes 388
  6.3 2.1 %collective-permute-start = (bf16[32,64,128]{2,1,0:T(8,128)(2,1)S(1)}, bf16[32,64,128]{2,1,0:T(8,128)(2,1)S(1)}, u32[]{:S(2)}, u32[]{:S(2)}) collective-permute-start(bf16[32,64,128]{2,1,0:T(8,128)(2,1)S(1)} %shard_map.55.refs_0_), channel_id=1, source_target_pairs={{0,1},{1,0},{2,3},{3,2},{4,5},{5,4},{6,7},{7,6},{8,9},{9,8},{10,11... | collective-permute-start | bytes 1572872 | tf_op jit(solution)/shard_map/ppermute | solution.py:17
  10.6 46.6 %all-to-all-start = ((bf16[8,256,128]{2,1,0:T(8,128)(2,1)}), bf16[8,256,128]{2,1,0:T(8,128)(2,1)S(1)}, u32[]{:S(2)}, u32[]{:S(2)}) async-start(bf16[8,256,128]{2,1,0:T(8,128)(2,1)} %bitcast.1), calls=%async_computation | async-start | bytes 1048576 | tf_op jit(solution)/shard_map/all_to_all | solution.py:258
  57.1 50.2 %copy-start.1 = (bf16[32,64,256]{2,1,0:T(8,128)(2,1)S(1)}, bf16[32,64,256]{2,1,0:T(8,128)(2,1)}, u32[]{:S(2)}) copy-start(bf16[32,64,256]{2,1,0:T(8,128)(2,1)} %refs_4_.1) | copy-start | bytes 3145732
  57.2 28.3 %all-to-all-start.1 = ((bf16[8,656,128]{2,1,0:T(8,128)(2,1)}), bf16[8,656,128]{2,1,0:T(8,128)(2,1)S(1)}, u32[]{:S(2)}, u32[]{:S(2)}) async-start(bf16[8,656,128]{2,1,0:T(8,128)(2,1)} %get-tuple-element.9), calls=%async_computation.1 | async-start | bytes 2686976 | tf_op jit(solution)/shard_map/all_to_all | solution.py:258
  61.5 21.9 %collective-permute-start.2 = (bf16[8,144,128]{2,1,0:T(8,128)(2,1)S(1)}, bf16[8,144,128]{2,1,0:T(8,128)(2,1)}, u32[]{:S(2)}, u32[]{:S(2)}) collective-permute-start(bf16[8,144,128]{2,1,0:T(8,128)(2,1)S(1)} %get-tuple-element.12), channel_id=1, source_target_pairs={{0,8},{1,9},{2,10},{3,11},{4,12},{5,13},{6,14},{7,15},{8,0},{9,1},... | collective-permute-start | bytes 884744 | tf_op jit(solution)/shard_map/ppermute | solution.py:262
  85.4 12.5 %all-to-all-start.2 = ((bf16[8,144,128]{2,1,0:T(8,128)(2,1)}), bf16[8,144,128]{2,1,0:T(8,128)(2,1)S(1)}, u32[]{:S(2)}, u32[]{:S(2)}) async-start(bf16[8,144,128]{2,1,0:T(8,128)(2,1)} %collective-permute-done.2), calls=%async_computation.2 | async-start | bytes 589824 | tf_op jit(solution)/shard_map/all_to_all | solution.py:258
  91.8 15.5 %collective-permute-start.1 = (bf16[8,2,64,128]{3,2,1,0:T(8,128)(2,1)}, bf16[8,2,64,128]{3,2,1,0:T(8,128)(2,1)S(1)}, u32[]{:S(2)}, u32[]{:S(2)}) collective-permute-start(bf16[8,2,64,128]{3,2,1,0:T(8,128)(2,1)} %get-tuple-element.11), channel_id=1, source_target_pairs={{0,8},{1,9},{2,10},{3,11},{4,12},{5,13},{6,14},{7,15},{8,0},{9,1},... | collective-permute-start | bytes 786440 | tf_op jit(solution)/shard_map/ppermute | solution.py:262

commit v2 on v0

v2 whole, which is shorter than its diff:
```python
import jax
import jax.numpy as jnp
from jax import lax
from jax.experimental import pallas as pl
from jax.experimental.pallas import tpu as pltpu
from jax.sharding import PartitionSpec as P

AXES = ("bfly", "rhs")
BF16 = jnp.bfloat16
TILE = 16
VMEM_LIMIT = 12 * 2**20


def from_partner(value, axis, distance):
    mask = 2**distance
    pairs = [(source, source ^ mask) for source in range(lax.axis_size(axis))]
    return lax.ppermute(value, axis, pairs)


def combine(current, partner_part, matrices):
    width = current.shape[1]
    own_term = jnp.einsum(
        "bij,bjc->bic", matrices[:, :, :width], current, preferred_element_type=jnp.float32
    )
    other_term = jnp.einsum(
        "bij,bjc->bic", matrices[:, :, width:], partner_part, preferred_element_type=jnp.float32
    )
    return (own_term + other_term).astype(BF16)


def pack_slots(flat_coefficients, slot_key, capacity, slot_total, target_spot):
    box_count = flat_coefficients.shape[0]
    box_iota = jnp.arange(box_count, dtype=jnp.int32)
    earlier = (slot_key[:, None] == slot_key[None, :]) & (box_iota[None, :] < box_iota[:, None])
    order_within = jnp.sum(earlier.astype(jnp.int32), axis=1)
    slot_of_box = slot_key * capacity + order_within
    selector = jnp.arange(slot_total, dtype=jnp.int32)[:, None] == slot_of_box[None, :]
    outgoing = jnp.dot(
        selector.astype(BF16), flat_coefficients, preferred_element_type=jnp.float32
    ).astype(BF16)
    outgoing_spot = jnp.sum(jnp.where(selector, target_spot[None, :] + 1, 0), axis=1) - 1
    return (outgoing, outgoing_spot)


def exchange_every_level(right_sides, leaf_basis, translations, node_target, out_basis):
    box_count = leaf_basis.shape[0]
    rank_width = leaf_basis.shape[1]
    leaf_rows = leaf_basis.shape[2]
    column_count = right_sides.shape[1]
    point_rows = right_sides.reshape(box_count, leaf_rows, column_count)
    coefficients = jnp.einsum(
        "brl,blc->brc", leaf_basis, point_rows, preferred_element_type=jnp.float32
    ).astype(BF16)
    local_levels = box_count.bit_length() - 1
    for level_index in range(local_levels):
        span = 2**level_index
        blocks = coefficients.reshape(box_count // (2 * span), 2, span, rank_width, column_count)
        partner_part = jnp.flip(blocks, 1).reshape(box_count, rank_width, column_count)
        coefficients = combine(coefficients, partner_part, translations[:, level_index])
    device_count = lax.axis_size(AXES)
    device_levels = device_count.bit_length() - 1
    for section_index in range(device_levels):
        partner_part = from_partner(coefficients, AXES, section_index)
        coefficients = combine(
            coefficients, partner_part, translations[:, local_levels + section_index]
        )
    target_device = node_target // box_count
    target_spot = node_target % box_count
    box_iota = jnp.arange(box_count, dtype=jnp.int32)
    flat_coefficients = coefficients.reshape(box_count, rank_width * column_count)
    capacity = max(1, box_count // device_count)
    slot_total = device_count * capacity
    outgoing, outgoing_spot = pack_slots(
        flat_coefficients, target_device, capacity, slot_total, target_spot
    )
    incoming, incoming_spot = (
        lax.all_to_all(outgoing, AXES, split_axis=0, concat_axis=0, tiled=True),
        lax.all_to_all(outgoing_spot, AXES, split_axis=0, concat_axis=0, tiled=True),
    )
    placement_table = (box_iota[:, None] == incoming_spot[None, :]).astype(BF16)
    placed = jnp.dot(placement_table, incoming, preferred_element_type=jnp.float32).astype(BF16)
    placed = placed.reshape(box_count, rank_width, column_count)
    applied = jnp.einsum("brl,brc->blc", out_basis, placed, preferred_element_type=jnp.float32)
    return applied.astype(BF16).reshape(box_count * leaf_rows, column_count)


def product(matrix, rows):
    return jnp.dot(matrix, rows, preferred_element_type=jnp.float32).astype(BF16)


def stacked(first, second):
    return jnp.concatenate([first, second], axis=0)


def own_half():
    return lax.axis_index("bfly") // 4


def own_place():
    return lax.axis_index("bfly") % 4


def first_box(place):
    return (place % 2) * 4 + (place // 2) * 2


def pick(tile, start, step, count, index):
    rows = []
    for k in range(count):
        at = start + step * k
        rows.append(jnp.where(index == 0, tile[at : at + 1], tile[at + 1 : at + 2]))
    return rows


def pack_kernel(rank, target_ref, trans_ref, pair_ref, stay_ref, late_ref, target, sem, target_sem):
    half, own = own_half(), own_place()
    target_copy = pltpu.make_async_copy(target_ref, target, target_sem)
    target_copy.start()
    copies = []
    for place in range(4):
        z0, y = place // 2, place % 2
        source = trans_ref.at[:, y, z0, :, pl.ds(6 * rank, 2 * rank)]
        copies.append(pltpu.make_async_copy(source, pair_ref.at[place], sem))
        for ref, bit in ((stay_ref, half), (late_ref, 1 - half)):
            source = trans_ref.at[:, y, z0, bit, pl.ds(8 * rank, rank)]
            slots = ref.at[place ^ own, pl.ds(0, 4 * rank)].reshape(4, rank, ref.shape[-1])
            copies.append(pltpu.make_async_copy(source, slots, sem))
    for copy in copies:
        copy.start()
    target_copy.wait()
    row = lax.broadcasted_iota(jnp.int32, (TILE, stay_ref.shape[-1]), 0)
    for place in range(4):
        for ref, bit in ((stay_ref, half), (late_ref, 1 - half)):
            spots = [target[q * 8 + first_box(place) + bit] % 32 for q in range(4)]
            tile = jnp.where(
                row < 2,
                jnp.where(row == 0, spots[0], spots[1]),
                jnp.where(row == 2, spots[2], spots[3]),
            )
            ref[place ^ own, pl.ds(4 * rank, TILE), :] = tile.astype(jnp.float32).astype(BF16)
    for copy in copies:
        copy.wait()


def local_kernel(
    levels, rs_ref, leaf_ref, trans_ref, out_ref, next_ref, rs, leaf, trans, ping, pong, sem, trans_sem
):
    boxes = leaf_ref.shape[0]
    step = boxes // 4
    loads = []
    for part in range(4):
        rows = pl.ds(part * step, step)
        loads.append(
            (
                pltpu.make_async_copy(rs_ref.at[rows], rs.at[rows], sem.at[part, 0]),
                pltpu.make_async_copy(leaf_ref.at[rows], leaf.at[rows], sem.at[part, 1]),
            )
        )
    level_loads = [
        pltpu.make_async_copy(trans_ref.at[:, level], trans.at[level], trans_sem.at[level])
        for level in range(levels)
    ]
    level_loads.append(
        pltpu.make_async_copy(trans_ref.at[:, levels], next_ref, trans_sem.at[levels])
    )
    for pair in loads:
        for copy in pair:
            copy.start()
    for copy in level_loads:
        copy.start()
    for part in range(4):
        for copy in loads[part]:
            copy.wait()
        for box in range(part * step, (part + 1) * step):
            ping[box] = product(leaf[box], rs[box])
    source, target = ping, pong
    for level in range(levels):
        level_loads[level].wait()
        if level == levels - 1:
            target = out_ref
        for box in range(boxes):
            rows = stacked(source[box], source[box ^ (1 << level)])
            target[box] = product(trans[level, box], rows)
        source, target = target, source
    level_loads[levels].wait()


def chip_kernel(own_ref, other_ref, trans_ref, *out_refs):
    own = own_place()
    for r in (1, 2, 3, 0):
        base = first_box(own ^ r)
        for q in range(4):
            for i0 in range(2):
                box = base + q * 8 + i0
                rows = stacked(own_ref[box], other_ref[box])
                out_refs[r][q, i0] = product(trans_ref[box], rows)


def quad_kernel(rank, box0, box1, box2, box3, pair_ref, keep_ref, send_ref, middle):
    boxes = (box0, box1, box2, box3)
    own, half = own_place(), own_half()
    for r in range(4):
        for q in range(4):
            for i0 in range(2):
                rows = stacked(boxes[r][q, i0], boxes[r ^ 1][q, i0])
                middle[r, q, i0] = product(pair_ref[own ^ r, q, i0, pl.ds(0, rank)], rows)
    for out_ref, bit in ((send_ref, 1 - half), (keep_ref, half)):
        for r in range(4):
            for q in range(4):
                rows = stacked(middle[r, q, bit], middle[r ^ 2, q, bit])
                out_ref[r, q] = product(pair_ref[own ^ r, q, bit, pl.ds(rank, rank)], rows)


def merge_kernel(stay_ref, late_ref, *out_refs):
    for r in range(4):
        out_refs[r][0] = stay_ref[r]
        out_refs[r][1] = late_ref[r]


def last_kernel(rank, keep_ref, recv_ref, trans0, trans1, trans2, trans3, own_ref, send_ref):
    trans = (trans0, trans1, trans2, trans3)
    core = lax.axis_index("rhs")
    for out_ref, bit in ((send_ref, 1 - core), (own_ref, core)):
        tile = []
        for side in range(2):
            for r in range(4):
                spots = trans[r][side, pl.ds(4 * rank, TILE), :]
                tile += pick(spots.astype(jnp.float32), 0, 2, 2, bit)
                for i4 in range(2):
                    q = i4 * 2 + bit
                    sides = (keep_ref[r, q], recv_ref[r, q])
                    rows = stacked(sides[side], sides[1 - side])
                    start = pl.multiple_of(q * rank, TILE)
                    index = side * 8 + r * 2 + i4
                    matrix = trans[r][side, pl.ds(start, rank), :]
                    out_ref[pl.ds(index * rank, rank), :] = product(matrix, rows)
        out_ref[pl.ds(16 * rank, TILE), :] = jnp.concatenate(tile, axis=0).astype(BF16)


def output_kernel(rank, box_ref, basis_ref, *refs):
    out_ref, result, sem = refs[-3:]
    spots = box_ref[pl.ds(16 * rank, TILE), :].astype(jnp.float32)
    copies = []
    for index in range(16):
        spot = jnp.max(spots[index : index + 1]).astype(jnp.int32)
        result[index] = lax.dot_general(
            basis_ref[spot],
            box_ref[pl.ds(index * rank, rank), :],
            (((0,), (0,)), ((), ())),
            preferred_element_type=jnp.float32,
        ).astype(BF16)
        copy = pltpu.make_async_copy(result.at[index], out_ref.at[spot], sem)
        copy.start()
        copies.append(copy)
    for copy in copies:
        copy.wait()


def call(kernel, out_shapes, in_spaces, out_spaces, scratch, flops, moved, aliases=None):
    run = pl.pallas_call(
        kernel,
        out_shape=out_shapes,
        in_specs=[pl.BlockSpec(memory_space=space) for space in in_spaces],
        out_specs=jax.tree.map(lambda space: pl.BlockSpec(memory_space=space), out_spaces),
        scratch_shapes=scratch,
        input_output_aliases=aliases or {},
        compiler_params=pltpu.CompilerParams(vmem_limit_bytes=VMEM_LIMIT),
        cost_estimate=pl.CostEstimate(flops=flops, bytes_accessed=moved, transcendentals=0),
    )

    def placed(*operands):
        return run(
            *(
                pltpu.with_memory_space_constraint(operand, space) if space == pltpu.HBM else operand
                for operand, space in zip(operands, in_spaces)
            )
        )

    return placed


def shape(*dims):
    return jax.ShapeDtypeStruct(dims, BF16)


def bind(kernel, *values):
    return lambda *refs: kernel(*values, *refs)


def move_early(right_sides, leaf_basis, translations, node_target, out_basis):
    boxes, rank, leaf_rows = leaf_basis.shape
    columns = right_sides.shape[1]
    local_levels = boxes.bit_length() - 1
    width = 2 * rank
    block = 2 * rank * columns * 2
    hbm, vmem, smem, dma = pltpu.HBM, pltpu.VMEM, pltpu.SMEM, pltpu.SemaphoreType.DMA
    quads = [[first + 2 * place for place in range(4)] for first in (0, 1, 8, 9)]

    def among_places(value):
        return lax.all_to_all(value, AXES, 0, 0, axis_index_groups=quads, tiled=True)

    def across(value, mask):
        return lax.ppermute(value, AXES, [(s, s ^ mask) for s in range(16)])

    pair, stay, late = call(
        bind(pack_kernel, rank),
        (
            shape(4, 4, 2, 2 * rank, width),
            shape(4, 4 * rank + TILE, width),
            shape(4, 4 * rank + TILE, width),
        ),
        (hbm, hbm),
        (vmem, vmem, vmem),
        [smem((boxes,), jnp.int32), dma, dma],
        0,
        3 * 2**20,
    )(node_target, translations.reshape(4, 2, 2, 2, -1, width))
    right_sides, pair, late = lax.optimization_barrier((right_sides, pair, late))
    pair = among_places(pair)
    late = across(late, 8)
    coefficients, chip_translations = call(
        bind(local_kernel, local_levels),
        (shape(boxes, rank, columns), shape(boxes, rank, width)),
        (hbm, hbm, hbm),
        (vmem, vmem),
        [
            vmem((boxes, leaf_rows, columns), BF16),
            vmem((boxes, rank, leaf_rows), BF16),
            vmem((local_levels, boxes, rank, width), BF16),
            vmem((boxes, rank, columns), BF16),
            vmem((boxes, rank, columns), BF16),
            dma((4, 2)),
            dma((local_levels + 1,)),
        ],
        boxes * rank * columns * 2 * (leaf_rows + local_levels * width),
        6 * 2**20,
    )(right_sides.reshape(boxes, leaf_rows, columns), leaf_basis, translations)
    partner = across(coefficients, 1)
    slots = call(
        chip_kernel,
        (shape(4, 2, rank, columns),) * 4,
        (vmem,) * 3,
        (vmem,) * 4,
        [],
        boxes * block * width,
        2**21,
    )(coefficients, partner, chip_translations)
    slots = [slots[0]] + [across(slots[r], 2 * r) for r in (1, 2, 3)]
    stay, late, _ = lax.optimization_barrier((stay, late, slots[1]))
    last = call(
        merge_kernel,
        (shape(2, 4 * rank + TILE, width),) * 4,
        (vmem,) * 2,
        (vmem,) * 4,
        [],
        0,
        2**20,
    )(stay, late)
    slots, last = lax.optimization_barrier((slots, last))
    keep, send = call(
        bind(quad_kernel, rank),
        (shape(4, 4, rank, columns), shape(4, 4, rank, columns)),
        (vmem,) * 5,
        (vmem,) * 2,
        [vmem((4, 4, 2, rank, columns), BF16)],
        2 * boxes * block * width,
        2**21,
    )(*slots, pair)
    received = across(send, 8)
    last = [last[0]] + [across(last[r], 2 * r) for r in (1, 2, 3)]
    own, send = call(
        bind(last_kernel, rank),
        (shape(16 * rank + TILE, columns),) * 2,
        (vmem,) * 6,
        (vmem,) * 2,
        [],
        boxes * block * width,
        2**21,
    )(keep, received, *last)
    partner = across(send, 1)
    applied = None
    for part in (own, partner):
        before = () if applied is None else (applied,)
        applied = call(
            bind(output_kernel, rank),
            shape(boxes, leaf_rows, columns),
            (vmem, vmem) + (hbm,) * len(before),
            hbm,
            [vmem((16, leaf_rows, columns), BF16), dma],
            boxes * block * width,
            2**21,
            {2: 0} if before else None,
        )(part, out_basis, *before)
    return applied.reshape(boxes * leaf_rows, columns)


def solution(mesh):
    in_specs = (
        P(("groups", "bfly", "rhs"), None),
        P(("bfly", "rhs"), None, None),
        P(("bfly", "rhs"), None, None, None),
        P(("bfly", "rhs")),
        P(("bfly", "rhs"), None, None),
    )
    out_specs = P(("groups", "bfly", "rhs"), None)

    def per_device(right_sides, leaf_basis, translations, node_target, out_basis):
        devices = lax.axis_size(AXES)
        fits = devices == 16 and leaf_basis.shape[0] == 32
        apply = move_early if fits else exchange_every_level
        return apply(right_sides, leaf_basis, translations, node_target, out_basis)

    return jax.shard_map(
        per_device, mesh=mesh, in_specs=in_specs, out_specs=out_specs, check_vma=False
    )
```

time: 121 us -> 53.8 us (0.44)
  waiting for transfers between devices: 54.3 us -> 24.1 us
  matrix products: 24.7 us -> 0 us
  local copies, waits for them, and re-layouts: 23 us -> 0.01 us
  Pallas kernels: 0 us -> 11.6 us
    dot_general x22 -> x0, matrix products: 24.7 us -> none  [the longest x9 13 us: combine(): jnp.einsum('bij,bjc->bic', matrices[:, :, width:], partner_part, preferre...]
    ppermute x4 -> x10, waiting for transfers between devices: 40.9 us -> 24.1 us  [across(): return lax.ppermute(value, AXES, [(s, s ^ mask) for s in range(16)])]
    all_to_all x2 -> x1, waiting for transfers between devices: 13.3 us -> 0.01 us  [among_places(): lax.all_to_all(value, AXES, 0, 0, axis_index_groups=quads, tiled=True)]
    pallas_call x0 -> x8, Pallas kernels: none -> 11.6 us  [placed(): run(*(pltpu.with_memory_space_constraint(operand, space) if space == pltp...]
    rev x5 -> x0, local copies, waits for them, and re-layouts: 9.43 us -> none  [per_device(): jnp.flip(blocks, 1).reshape(box_count, rank_width, column_count)]
    squeeze x1 -> x0, local copies, waits for them, and re-layouts: 5.1 us -> none  [per_device(): translations[:, local_levels + section_index]]
    ppermute x4 -> x10, starting transfers between devices: 7.82 us -> 12.6 us  [across(): return lax.ppermute(value, AXES, [(s, s ^ mask) for s in range(16)])]
    convert_element_type x1 -> x0, local copies, waits for them, and re-layouts: 4.06 us -> none  [per_device(): applied.astype(jnp.bfloat16).reshape(box_count * leaf_rows, column_count)]
  transfers between devices with their start and end apart: 6 -> 11, of which waited for: 5 -> 7; matrix products, arithmetic and copies ran while one was open for 5% -> 0% of each run, Pallas kernels for 0% -> 13%
where the time goes in v2:
time: 53.8 us; the launch traced here: 53.6 us
  waiting for transfers between devices  24.1 us (45%)
  starting transfers between devices  17.8 us (33%)
  Pallas kernels  11.6 us (22%)
    ppermute x10, waiting for transfers between devices, across(): return lax.ppermute(value, AXES, [(s, s ^ mask) for s in range(16)])  24.1 us
    ppermute x10, starting transfers between devices, across(): return lax.ppermute(value, AXES, [(s, s ^ mask) for s in range(16)])  12.6 us
    pallas_call x8, Pallas kernels, placed(): run(*(pltpu.with_memory_space_constraint(operand, space) if space == pltp...  11.6 us
    all_to_all x1, starting transfers between devices, among_places(): lax.all_to_all(value, AXES, 0, 0, axis_index_groups=quads, tiled=True)  5.26 us
  transfers between devices with their start and end apart: 11, of which 7 were waited for; matrix products, arithmetic and copies ran while one was open for 0% of the time, Pallas kernels for 13%

profile of v2, /device:TPU:0, one launch (start us, length us, event | category | flops | bytes accessed | tf_op | source)
XLA Modules:
  0.0 53.6 jit_solution(2809638208484046154)
XLA Ops:
  0.0 2.3 %shard_map.55 = (bf16[4,4,2,128,128]{4,3,2,1,0:T(8,128)(2,1)}, bf16[4,272,128]{2,1,0:T(8,128)(2,1)S(1)}, bf16[4,272,128]{2,1,0:T(8,128)(2,1)S(1)}) custom-call(s32[32]{0:T(128)} %refs_0_.1, bf16[4,2,2,2,576,128]{5,4,3,2,1,0:T(8,128)(2,1)} %bitcast.3), custom_call_target="tpu_custom_call" | custom-call | bytes 3145728 | tf_op jit(solution)/shard_map/pallas_call | solution.py:272
  2.3 5.3 %all-to-all-start = ((bf16[4,4,2,128,128]{4,3,2,1,0:T(8,128)(2,1)}), bf16[4,4,2,128,128]{4,3,2,1,0:T(8,128)(2,1)S(1)}, u32[]{:S(2)}, u32[]{:S(2)}) async-start(bf16[4,4,2,128,128]{4,3,2,1,0:T(8,128)(2,1)} %get-tuple-element.56), calls=%async_computation | async-start | bytes 2097152 | tf_op jit(solution)/shard_map/all_to_all | solution.py:300
  7.6 5.0 %shard_map.56 = (bf16[32,64,128]{2,1,0:T(8,128)(2,1)S(1)}, bf16[32,64,128]{2,1,0:T(8,128)(2,1)S(1)}) custom-call(bf16[32,256,128]{2,1,0:T(8,128)(2,1)} %bitcast.4, bf16[32,64,256]{2,1,0:T(8,128)(2,1)} %refs_1_.3, bf16[32,9,64,128]{3,2,1,0:T(8,128)(2,1)} %refs_2_.1), custom_call_target="tpu_custom_call" | custom-call | flops 469762048 | bytes 6291456 | tf_op jit(solution)/shard_map/pallas_call | solution.py:272
  12.6 0.1 collective-permute-start
  12.7 2.7 %collective-permute-start.4 = (bf16[4,272,128]{2,1,0:T(8,128)(2,1)S(1)}, bf16[4,272,128]{2,1,0:T(8,128)(2,1)S(1)}, u32[]{:S(2)}, u32[]{:S(2)}) collective-permute-start(bf16[4,272,128]{2,1,0:T(8,128)(2,1)S(1)} %get-tuple-element.45), channel_id=1, source_target_pairs={{0,8},{1,9},{2,10},{3,11},{4,12},{5,13},{6,14},{7,15},{8,0},{9,1},... | collective-permute-start | bytes 835592 | tf_op jit(solution)/shard_map/ppermute | solution.py:303
  15.3 0.0 collective-permute-done.other_ref
  15.3 0.0 copy-start
  15.3 0.4 shard_map.57
  15.7 2.1 %collective-permute-start.1 = (bf16[4,2,64,128]{3,2,1,0:T(8,128)(2,1)S(1)}, bf16[4,2,64,128]{3,2,1,0:T(8,128)(2,1)S(1)}, u32[]{:S(2)}, u32[]{:S(2)}) collective-permute-start(bf16[4,2,64,128]{3,2,1,0:T(8,128)(2,1)S(1)} %get-tuple-element.41), channel_id=1, source_target_pairs={{0,2},{1,3},{2,0},{3,1},{4,6},{5,7},{6,4},{7,5},{8,10},{9,11},{10,... | collective-permute-start | bytes 393224 | tf_op jit(solution)/shard_map/ppermute | solution.py:303
  17.8 1.5 %collective-permute-start.2 = (bf16[4,2,64,128]{3,2,1,0:T(8,128)(2,1)S(1)}, bf16[4,2,64,128]{3,2,1,0:T(8,128)(2,1)S(1)}, u32[]{:S(2)}, u32[]{:S(2)}) collective-permute-start(bf16[4,2,64,128]{3,2,1,0:T(8,128)(2,1)S(1)} %get-tuple-element.42), channel_id=1, source_target_pairs={{0,4},{1,5},{2,6},{3,7},{4,0},{5,1},{6,2},{7,3},{8,12},{9,13},{10,... | collective-permute-start | bytes 393224 | tf_op jit(solution)/shard_map/ppermute | solution.py:303
  19.3 0.1 collective-permute-start.3
  19.4 6.8 %collective-permute-done.4.late_ref = bf16[4,272,128]{2,1,0:T(8,128)(2,1)S(1)} collective-permute-done((bf16[4,272,128]{2,1,0:T(8,128)(2,1)S(1)}, bf16[4,272,128]{2,1,0:T(8,128)(2,1)S(1)}, u32[]{:S(2)}, u32[]{:S(2)}) %collective-permute-start.4) | collective-permute-done | bytes 278560 | tf_op jit(solution)/shard_map/ppermute | solution.py:303
  26.2 0.0 collective-permute-done.1.refs_1_
  26.2 5.2 %collective-permute-done.2.refs_2_ = bf16[4,2,64,128]{3,2,1,0:T(8,128)(2,1)S(1)} collective-permute-done((bf16[4,2,64,128]{3,2,1,0:T(8,128)(2,1)S(1)}, bf16[4,2,64,128]{3,2,1,0:T(8,128)(2,1)S(1)}, u32[]{:S(2)}, u32[]{:S(2)}) %collective-permute-start.2) | collective-permute-done | bytes 131104 | tf_op jit(solution)/shard_map/ppermute | solution.py:303
  31.4 2.3 %collective-permute-done.3.refs_3_ = bf16[4,2,64,128]{3,2,1,0:T(8,128)(2,1)S(1)} collective-permute-done((bf16[4,2,64,128]{3,2,1,0:T(8,128)(2,1)S(1)}, bf16[4,2,64,128]{3,2,1,0:T(8,128)(2,1)S(1)}, u32[]{:S(2)}, u32[]{:S(2)}) %collective-permute-start.3) | collective-permute-done | bytes 131104 | tf_op jit(solution)/shard_map/ppermute | solution.py:303
  33.7 0.0 all-to-all-done.refs_4_
  33.7 0.8 %shard_map.59 = (bf16[4,4,64,128]{3,2,1,0:T(8,128)(2,1)S(1)}, bf16[4,4,64,128]{3,2,1,0:T(8,128)(2,1)S(1)}) custom-call(bf16[4,2,64,128]{3,2,1,0:T(8,128)(2,1)S(1)} %get-tuple-element.52.refs_0_, bf16[4,2,64,128]{3,2,1,0:T(8,128)(2,1)S(1)} %collective-permute-done.1.refs_1_, bf16[4,2,64,128]{3,2,1,0:T(8,128)(2,1)S(1)} %collective-permute-done.2.refs_2_, ...), custom_call_target="tpu_custom_call" | custom-call | flops 268435456 | bytes 2097152 | tf_op jit(solution)/shard_map/pallas_call | solution.py:272
  34.5 2.7 %collective-permute-start.5 = (bf16[4,4,64,128]{3,2,1,0:T(8,128)(2,1)S(1)}, bf16[4,4,64,128]{3,2,1,0:T(8,128)(2,1)S(1)}, u32[]{:S(2)}, u32[]{:S(2)}) collective-permute-start(bf16[4,4,64,128]{3,2,1,0:T(8,128)(2,1)S(1)} %get-tuple-element.58), channel_id=1, source_target_pairs={{0,8},{1,9},{2,10},{3,11},{4,12},{5,13},{6,14},{7,15},{8,0},{9,1},... | collective-permute-start | bytes 786440 | tf_op jit(solution)/shard_map/ppermute | solution.py:303
  37.2 0.6 %collective-permute-start.6 = (bf16[2,272,128]{2,1,0:T(8,128)(2,1)S(1)}, bf16[2,272,128]{2,1,0:T(8,128)(2,1)S(1)}, u32[]{:S(2)}, u32[]{:S(2)}) collective-permute-start(bf16[2,272,128]{2,1,0:T(8,128)(2,1)S(1)} %get-tuple-element.60), channel_id=1, source_target_pairs={{0,2},{1,3},{2,0},{3,1},{4,6},{5,7},{6,4},{7,5},{8,10},{9,11},{10,... | collective-permute-start | bytes 417800 | tf_op jit(solution)/shard_map/ppermute | solution.py:303
  37.8 0.3 collective-permute-start.7
  38.0 2.6 %collective-permute-start.8 = (bf16[2,272,128]{2,1,0:T(8,128)(2,1)S(1)}, bf16[2,272,128]{2,1,0:T(8,128)(2,1)S(1)}, u32[]{:S(2)}, u32[]{:S(2)}) collective-permute-start(bf16[2,272,128]{2,1,0:T(8,128)(2,1)S(1)} %get-tuple-element.62), channel_id=1, source_target_pairs={{0,6},{1,7},{2,4},{3,5},{4,2},{5,3},{6,0},{7,1},{8,14},{9,15},{10,... | collective-permute-start | bytes 417800 | tf_op jit(solution)/shard_map/ppermute | solution.py:303
  40.7 2.6 %collective-permute-done.6.refs_3_ = bf16[2,272,128]{2,1,0:T(8,128)(2,1)S(1)} collective-permute-done((bf16[2,272,128]{2,1,0:T(8,128)(2,1)S(1)}, bf16[2,272,128]{2,1,0:T(8,128)(2,1)S(1)}, u32[]{:S(2)}, u32[]{:S(2)}) %collective-permute-start.6) | collective-permute-done | bytes 139296 | tf_op jit(solution)/shard_map/ppermute | solution.py:303
  43.3 4.9 %collective-permute-done.7.refs_4_ = bf16[2,272,128]{2,1,0:T(8,128)(2,1)S(1)} collective-permute-done((bf16[2,272,128]{2,1,0:T(8,128)(2,1)S(1)}, bf16[2,272,128]{2,1,0:T(8,128)(2,1)S(1)}, u32[]{:S(2)}, u32[]{:S(2)}) %collective-permute-start.7) | collective-permute-done | bytes 139296 | tf_op jit(solution)/shard_map/ppermute | solution.py:303
  48.2 2.1 %collective-permute-done.8.refs_5_ = bf16[2,272,128]{2,1,0:T(8,128)(2,1)S(1)} collective-permute-done((bf16[2,272,128]{2,1,0:T(8,128)(2,1)S(1)}, bf16[2,272,128]{2,1,0:T(8,128)(2,1)S(1)}, u32[]{:S(2)}, u32[]{:S(2)}) %collective-permute-start.8) | collective-permute-done | bytes 139296 | tf_op jit(solution)/shard_map/ppermute | solution.py:303
  50.2 0.0 collective-permute-done.5.refs_1_
  50.2 0.4 shard_map.60
  50.6 0.1 collective-permute-start.9
  50.7 0.0 copy-done
  50.7 1.3 %shard_map.61.refs_2_ = bf16[32,256,128]{2,1,0:T(8,128)(2,1)} custom-call(bf16[1040,128]{1,0:T(8,128)(2,1)S(1)} %get-tuple-element.64.refs_0_, bf16[32,64,256]{2,1,0:T(8,128)(2,1)S(1)} %copy-done), custom_call_target="tpu_custom_call" | custom-call | flops 134217728 | bytes 2097152 | tf_op jit(solution)/shard_map/pallas_call | solution.py:272
  52.0 0.2 collective-permute-done.9.refs_0_
  52.3 1.3 %shard_map.62 = bf16[32,256,128]{2,1,0:T(8,128)(2,1)} custom-call(bf16[1040,128]{1,0:T(8,128)(2,1)S(1)} %collective-permute-done.9.refs_0_, bf16[32,64,256]{2,1,0:T(8,128)(2,1)S(1)} %copy-done, bf16[32,256,128]{2,1,0:T(8,128)(2,1)} %shard_map.61.refs_2_), custom_call_target="tpu_custom_call", output_to_operand_aliasing={{}: (2, {})} | custom-call | flops 134217728 | bytes 2097152 | tf_op jit(solution)/shard_map/pallas_call | solution.py:272
  (1 shorter events, 0.0 us)
Async XLA Ops:
  2.3 31.4 %all-to-all-start = ((bf16[4,4,2,128,128]{4,3,2,1,0:T(8,128)(2,1)}), bf16[4,4,2,128,128]{4,3,2,1,0:T(8,128)(2,1)S(1)}, u32[]{:S(2)}, u32[]{:S(2)}) async-start(bf16[4,4,2,128,128]{4,3,2,1,0:T(8,128)(2,1)} %get-tuple-element.56), calls=%async_computation | async-start | bytes 2097152 | tf_op jit(solution)/shard_map/all_to_all | solution.py:300
  12.6 2.7 %collective-permute-start = (bf16[32,64,128]{2,1,0:T(8,128)(2,1)S(1)}, bf16[32,64,128]{2,1,0:T(8,128)(2,1)S(1)}, u32[]{:S(2)}, u32[]{:S(2)}) collective-permute-start(bf16[32,64,128]{2,1,0:T(8,128)(2,1)S(1)} %get-tuple-element.38.own_ref), channel_id=1, source_target_pairs={{0,1},{1,0},{2,3},{3,2},{4,5},{5,4},{6,7},{7,6},{8,9},{9,8},{10,11... | collective-permute-start | bytes 1572872 | tf_op jit(solution)/shard_map/ppermute | solution.py:303
  12.7 13.5 %collective-permute-start.4 = (bf16[4,272,128]{2,1,0:T(8,128)(2,1)S(1)}, bf16[4,272,128]{2,1,0:T(8,128)(2,1)S(1)}, u32[]{:S(2)}, u32[]{:S(2)}) collective-permute-start(bf16[4,272,128]{2,1,0:T(8,128)(2,1)S(1)} %get-tuple-element.45), channel_id=1, source_target_pairs={{0,8},{1,9},{2,10},{3,11},{4,12},{5,13},{6,14},{7,15},{8,0},{9,1},... | collective-permute-start | bytes 835592 | tf_op jit(solution)/shard_map/ppermute | solution.py:303
  15.3 35.4 %copy-start = (bf16[32,64,256]{2,1,0:T(8,128)(2,1)S(1)}, bf16[32,64,256]{2,1,0:T(8,128)(2,1)}, u32[]{:S(2)}) copy-start(bf16[32,64,256]{2,1,0:T(8,128)(2,1)} %refs_1_.5) | copy-start | bytes 3145732
  15.7 10.4 %collective-permute-start.1 = (bf16[4,2,64,128]{3,2,1,0:T(8,128)(2,1)S(1)}, bf16[4,2,64,128]{3,2,1,0:T(8,128)(2,1)S(1)}, u32[]{:S(2)}, u32[]{:S(2)}) collective-permute-start(bf16[4,2,64,128]{3,2,1,0:T(8,128)(2,1)S(1)} %get-tuple-element.41), channel_id=1, source_target_pairs={{0,2},{1,3},{2,0},{3,1},{4,6},{5,7},{6,4},{7,5},{8,10},{9,11},{10,... | collective-permute-start | bytes 393224 | tf_op jit(solution)/shard_map/ppermute | solution.py:303
  17.8 13.6 %collective-permute-start.2 = (bf16[4,2,64,128]{3,2,1,0:T(8,128)(2,1)S(1)}, bf16[4,2,64,128]{3,2,1,0:T(8,128)(2,1)S(1)}, u32[]{:S(2)}, u32[]{:S(2)}) collective-permute-start(bf16[4,2,64,128]{3,2,1,0:T(8,128)(2,1)S(1)} %get-tuple-element.42), channel_id=1, source_target_pairs={{0,4},{1,5},{2,6},{3,7},{4,0},{5,1},{6,2},{7,3},{8,12},{9,13},{10,... | collective-permute-start | bytes 393224 | tf_op jit(solution)/shard_map/ppermute | solution.py:303
  19.3 14.4 %collective-permute-start.3 = (bf16[4,2,64,128]{3,2,1,0:T(8,128)(2,1)S(1)}, bf16[4,2,64,128]{3,2,1,0:T(8,128)(2,1)S(1)}, u32[]{:S(2)}, u32[]{:S(2)}) collective-permute-start(bf16[4,2,64,128]{3,2,1,0:T(8,128)(2,1)S(1)} %get-tuple-element.43), channel_id=1, source_target_pairs={{0,6},{1,7},{2,4},{3,5},{4,2},{5,3},{6,0},{7,1},{8,14},{9,15},{10,... | collective-permute-start | bytes 393224 | tf_op jit(solution)/shard_map/ppermute | solution.py:303
  34.5 15.7 %collective-permute-start.5 = (bf16[4,4,64,128]{3,2,1,0:T(8,128)(2,1)S(1)}, bf16[4,4,64,128]{3,2,1,0:T(8,128)(2,1)S(1)}, u32[]{:S(2)}, u32[]{:S(2)}) collective-permute-start(bf16[4,4,64,128]{3,2,1,0:T(8,128)(2,1)S(1)} %get-tuple-element.58), channel_id=1, source_target_pairs={{0,8},{1,9},{2,10},{3,11},{4,12},{5,13},{6,14},{7,15},{8,0},{9,1},... | collective-permute-start | bytes 786440 | tf_op jit(solution)/shard_map/ppermute | solution.py:303
  37.2 6.1 %collective-permute-start.6 = (bf16[2,272,128]{2,1,0:T(8,128)(2,1)S(1)}, bf16[2,272,128]{2,1,0:T(8,128)(2,1)S(1)}, u32[]{:S(2)}, u32[]{:S(2)}) collective-permute-start(bf16[2,272,128]{2,1,0:T(8,128)(2,1)S(1)} %get-tuple-element.60), channel_id=1, source_target_pairs={{0,2},{1,3},{2,0},{3,1},{4,6},{5,7},{6,4},{7,5},{8,10},{9,11},{10,... | collective-permute-start | bytes 417800 | tf_op jit(solution)/shard_map/ppermute | solution.py:303
  37.8 10.4 %collective-permute-start.7 = (bf16[2,272,128]{2,1,0:T(8,128)(2,1)S(1)}, bf16[2,272,128]{2,1,0:T(8,128)(2,1)S(1)}, u32[]{:S(2)}, u32[]{:S(2)}) collective-permute-start(bf16[2,272,128]{2,1,0:T(8,128)(2,1)S(1)} %get-tuple-element.61), channel_id=1, source_target_pairs={{0,4},{1,5},{2,6},{3,7},{4,0},{5,1},{6,2},{7,3},{8,12},{9,13},{10,... | collective-permute-start | bytes 417800 | tf_op jit(solution)/shard_map/ppermute | solution.py:303
  38.0 12.2 %collective-permute-start.8 = (bf16[2,272,128]{2,1,0:T(8,128)(2,1)S(1)}, bf16[2,272,128]{2,1,0:T(8,128)(2,1)S(1)}, u32[]{:S(2)}, u32[]{:S(2)}) collective-permute-start(bf16[2,272,128]{2,1,0:T(8,128)(2,1)S(1)} %get-tuple-element.62), channel_id=1, source_target_pairs={{0,6},{1,7},{2,4},{3,5},{4,2},{5,3},{6,0},{7,1},{8,14},{9,15},{10,... | collective-permute-start | bytes 417800 | tf_op jit(solution)/shard_map/ppermute | solution.py:303
  50.6 1.6 %collective-permute-start.9 = (bf16[1040,128]{1,0:T(8,128)(2,1)S(1)}, bf16[1040,128]{1,0:T(8,128)(2,1)S(1)}, u32[]{:S(2)}, u32[]{:S(2)}) collective-permute-start(bf16[1040,128]{1,0:T(8,128)(2,1)S(1)} %get-tuple-element.63), channel_id=1, source_target_pairs={{0,1},{1,0},{2,3},{3,2},{4,5},{5,4},{6,7},{7,6},{8,9},{9,8},{10,11... | collective-permute-start | bytes 798728 | tf_op jit(solution)/shard_map/ppermute | solution.py:303

commit v3 on v2

--- a/solution.py
+++ b/solution.py
@@ -104,47 +104,62 @@
     return (place % 2) * 4 + (place // 2) * 2
 
 
-def pick(tile, start, step, count, index):
-    rows = []
-    for k in range(count):
-        at = start + step * k
-        rows.append(jnp.where(index == 0, tile[at : at + 1], tile[at + 1 : at + 2]))
-    return rows
-
-
-def pack_kernel(rank, target_ref, trans_ref, pair_ref, stay_ref, late_ref, target, sem, target_sem):
-    half, own = own_half(), own_place()
+def level_rows(trans_ref, rank, i4, place, i0, level, count):
+    return trans_ref.at[i4, :, place % 2, place // 2, i0, pl.ds(level * rank, count * rank)]
+
+
+def start_all(pairs, sem):
+    copies = [pltpu.make_async_copy(source, target, sem) for source, target in pairs]
+    for copy in copies:
+        copy.start()
+    return copies
+
+
+BOTH = pl.ds(0, 2)
+
+
+def last_level(rank, trans_ref, i4, r, side, rows_ref):
+    slots = rows_ref.reshape(2, rank, trans_ref.shape[-1])
+    return level_rows(trans_ref, rank, i4, own_place() ^ r, own_half() ^ side, 8, 1), slots
+
+
+def spot_tile(target, i4, r, side, columns):
+    first = lax.broadcasted_iota(jnp.int32, (TILE, columns), 0) == 0
+    box = i4 * 16 + first_box(own_place() ^ r) + (own_half() ^ side)
+    return jnp.where(first, target[box] % 32, target[box + 8] % 32).astype(jnp.float32).astype(BF16)
+
+
+def pack_kernel(rank, target_ref, trans_ref, *refs):
+    out_refs, (target, sem, target_sem) = refs[:3], refs[3:]
+    group, columns = lax.axis_index("groups"), trans_ref.shape[-1]
     target_copy = pltpu.make_async_copy(target_ref, target, target_sem)
     target_copy.start()
-    copies = []
-    for place in range(4):
-        z0, y = place // 2, place % 2
-        source = trans_ref.at[:, y, z0, :, pl.ds(6 * rank, 2 * rank)]
-        copies.append(pltpu.make_async_copy(source, pair_ref.at[place], sem))
-        for ref, bit in ((stay_ref, half), (late_ref, 1 - half)):
-            source = trans_ref.at[:, y, z0, bit, pl.ds(8 * rank, rank)]
-            slots = ref.at[place ^ own, pl.ds(0, 4 * rank)].reshape(4, rank, ref.shape[-1])
-            copies.append(pltpu.make_async_copy(source, slots, sem))
-    for copy in copies:
-        copy.start()
+    pairs = []
+    for r in (3, 2, 1):
+        ref = out_refs[r - 1]
+        slots = ref.at[pl.ds(0, 8 * rank)].reshape(2, 2, 2 * rank, columns)
+        pairs.append((level_rows(trans_ref, rank, group, own_place() ^ r, BOTH, 6, 2), slots))
+        pairs.append(last_level(rank, trans_ref, group, r, 0, ref.at[pl.ds(8 * rank, 2 * rank)]))
+    copies = start_all(pairs, sem)
     target_copy.wait()
-    row = lax.broadcasted_iota(jnp.int32, (TILE, stay_ref.shape[-1]), 0)
-    for place in range(4):
-        for ref, bit in ((stay_ref, half), (late_ref, 1 - half)):
-            spots = [target[q * 8 + first_box(place) + bit] % 32 for q in range(4)]
-            tile = jnp.where(
-                row < 2,
-                jnp.where(row == 0, spots[0], spots[1]),
-                jnp.where(row == 2, spots[2], spots[3]),
-            )
-            ref[place ^ own, pl.ds(4 * rank, TILE), :] = tile.astype(jnp.float32).astype(BF16)
+    for r in (3, 2, 1):
+        out_refs[r - 1][pl.ds(10 * rank, TILE), :] = spot_tile(target, group, r, 0, columns)
     for copy in copies:
         copy.wait()
 
 
+def gather_kernel(near1, near2, near3, out_ref):
+    for index, ref in enumerate((near1, near2, near3)):
+        out_ref[index] = ref[...]
+
+
 def local_kernel(
-    levels, rs_ref, leaf_ref, trans_ref, out_ref, next_ref, rs, leaf, trans, ping, pong, sem, trans_sem
+    levels, rs_ref, leaf_ref, trans_ref, grid_ref, target_ref, out_ref, next_ref, pair_ref, stay_ref, late_ref,
+    rs, leaf, trans, ping, pong, target_smem, sem, trans_sem, rest_sem, target_sem
 ):
+    rank = leaf_ref.shape[1]
+    target_copy = pltpu.make_async_copy(target_ref, target_smem, target_sem)
+    target_copy.start()
     boxes = leaf_ref.shape[0]
     step = boxes // 4
     loads = []
@@ -168,6 +183,18 @@
             copy.start()
     for copy in level_loads:
         copy.start()
+    group, columns = lax.axis_index("groups"), grid_ref.shape[-1]
+    rest = [(level_rows(grid_ref, rank, BOTH, own_place(), BOTH, 6, 2), pair_ref)]
+    two = pl.ds(0, 2 * rank)
+    rest += [last_level(rank, grid_ref, i4, 0, 0, stay_ref.at[i4, two]) for i4 in range(2)]
+    rest += [last_level(rank, grid_ref, group, r, 1, late_ref.at[r, two]) for r in range(4)]
+    rest = start_all(rest, rest_sem)
+    target_copy.wait()
+    tile = pl.ds(2 * rank, TILE)
+    for i4 in range(2):
+        stay_ref[i4, tile, :] = spot_tile(target_smem, i4, 0, 0, columns)
+    for r in range(4):
+        late_ref[r, tile, :] = spot_tile(target_smem, group, r, 1, columns)
     for part in range(4):
         for copy in loads[part]:
             copy.wait()
@@ -183,6 +210,8 @@
             target[box] = product(trans[level, box], rows)
         source, target = target, source
     level_loads[levels].wait()
+    for copy in rest:
+        copy.wait()
 
 
 def chip_kernel(own_ref, other_ref, trans_ref, *out_refs):
@@ -196,44 +225,68 @@
                 out_refs[r][q, i0] = product(trans_ref[box], rows)
 
 
-def quad_kernel(rank, box0, box1, box2, box3, pair_ref, keep_ref, send_ref, middle):
+def quad_kernel(
+    rank, box0, box1, box2, box3, pair_ref, near1, near2, near3, far_ref, keep_ref, send_ref, middle
+):
     boxes = (box0, box1, box2, box3)
-    own, half = own_place(), own_half()
+    half, group = own_half(), lax.axis_index("groups")
+
+    def matrix(r, h, i3, i0, level):
+        if r == 0:
+            return pair_ref[group ^ h, i3, i0, pl.ds(level * rank, rank)]
+        ref = far_ref.at[r - 1] if h else (near1, near2, near3)[r - 1]
+        start = pl.multiple_of(((i3 * 2 + i0) * 2 + level) * rank, TILE)
+        return ref[pl.ds(start, rank), :]
+
+    order = [(r, h, i3) for r in range(4) for h in range(2) for i3 in range(2)]
+    for r, h, i3 in order:
+        q = (group ^ h) * 2 + i3
+        for i0 in range(2):
+            rows = stacked(boxes[r][q, i0], boxes[r ^ 1][q, i0])
+            middle[r, q, i0] = product(matrix(r, h, i3, i0, 0), rows)
+    for out_ref, bit in ((send_ref, 1 - half), (keep_ref, half)):
+        for r, h, i3 in order:
+            q = (group ^ h) * 2 + i3
+            rows = stacked(middle[r, q, bit], middle[r ^ 2, q, bit])
+            out_ref[r, q] = product(matrix(r, h, i3, bit, 1), rows)
+
+
+def split_kernel(late_ref, *out_refs):
     for r in range(4):
-        for q in range(4):
-            for i0 in range(2):
-                rows = stacked(boxes[r][q, i0], boxes[r ^ 1][q, i0])
-                middle[r, q, i0] = product(pair_ref[own ^ r, q, i0, pl.ds(0, rank)], rows)
-    for out_ref, bit in ((send_ref, 1 - half), (keep_ref, half)):
-        for r in range(4):
-            for q in range(4):
-                rows = stacked(middle[r, q, bit], middle[r ^ 2, q, bit])
-                out_ref[r, q] = product(pair_ref[own ^ r, q, bit, pl.ds(rank, rank)], rows)
-
-
-def merge_kernel(stay_ref, late_ref, *out_refs):
-    for r in range(4):
-        out_refs[r][0] = stay_ref[r]
-        out_refs[r][1] = late_ref[r]
-
-
-def last_kernel(rank, keep_ref, recv_ref, trans0, trans1, trans2, trans3, own_ref, send_ref):
-    trans = (trans0, trans1, trans2, trans3)
-    core = lax.axis_index("rhs")
+        out_refs[r][...] = late_ref[r]
+
+
+def collect_kernel(late0, late1, late2, late3, out_ref):
+    for r, ref in enumerate((late0, late1, late2, late3)):
+        out_ref[r] = ref[...]
+
+
+def last_kernel(
+    rank, keep_ref, recv_ref, stay_ref, near1, near2, near3, far_ref, here_ref, cross_ref, own_ref, send_ref
+):
+    group, core = lax.axis_index("groups"), lax.axis_index("rhs")
+
+    def source(side, r, h):
+        if side:
+            return (here_ref, cross_ref)[h].at[r], 0
+        if r == 0:
+            return stay_ref.at[group ^ h], 0
+        return (far_ref.at[r - 1] if h else (near1, near2, near3)[r - 1]), 8 * rank
+
     for out_ref, bit in ((send_ref, 1 - core), (own_ref, core)):
         tile = []
         for side in range(2):
             for r in range(4):
-                spots = trans[r][side, pl.ds(4 * rank, TILE), :]
-                tile += pick(spots.astype(jnp.float32), 0, 2, 2, bit)
-                for i4 in range(2):
-                    q = i4 * 2 + bit
+                for h in range(2):
+                    ref, base = source(side, r, h)
+                    spots = ref[pl.ds(base + 2 * rank, TILE), :].astype(jnp.float32)
+                    tile.append(jnp.where(bit == 0, spots[0:1], spots[1:2]))
+                    q = (group ^ h) * 2 + bit
                     sides = (keep_ref[r, q], recv_ref[r, q])
                     rows = stacked(sides[side], sides[1 - side])
-                    start = pl.multiple_of(q * rank, TILE)
-                    index = side * 8 + r * 2 + i4
-                    matrix = trans[r][side, pl.ds(start, rank), :]
-                    out_ref[pl.ds(index * rank, rank), :] = product(matrix, rows)
+                    start = pl.multiple_of(base + bit * rank, TILE)
+                    index = side * 8 + r * 2 + h
+                    out_ref[pl.ds(index * rank, rank), :] = product(ref[pl.ds(start, rank), :], rows)
         out_ref[pl.ds(16 * rank, TILE), :] = jnp.concatenate(tile, axis=0).astype(BF16)
 
 
@@ -294,48 +347,60 @@
     width = 2 * rank
     block = 2 * rank * columns * 2
     hbm, vmem, smem, dma = pltpu.HBM, pltpu.VMEM, pltpu.SMEM, pltpu.SemaphoreType.DMA
-    quads = [[first + 2 * place for place in range(4)] for first in (0, 1, 8, 9)]
-
-    def among_places(value):
-        return lax.all_to_all(value, AXES, 0, 0, axis_index_groups=quads, tiled=True)
-
     def across(value, mask):
         return lax.ppermute(value, AXES, [(s, s ^ mask) for s in range(16)])
 
-    pair, stay, late = call(
+    def swapped(value):
+        return lax.ppermute(value, "groups", [(0, 1), (1, 0)])
+
+    grid = translations.reshape(2, 2, 2, 2, 2, -1, width)
+    part = shape(2 * rank + TILE, width)
+    near_part = shape(10 * rank + TILE, width)
+    near = call(
         bind(pack_kernel, rank),
-        (
-            shape(4, 4, 2, 2 * rank, width),
-            shape(4, 4 * rank + TILE, width),
-            shape(4, 4 * rank + TILE, width),
-        ),
+        (near_part,) * 3,
         (hbm, hbm),
-        (vmem, vmem, vmem),
+        (vmem,) * 3,
         [smem((boxes,), jnp.int32), dma, dma],
         0,
-        3 * 2**20,
-    )(node_target, translations.reshape(4, 2, 2, 2, -1, width))
-    right_sides, pair, late = lax.optimization_barrier((right_sides, pair, late))
-    pair = among_places(pair)
-    late = across(late, 8)
-    coefficients, chip_translations = call(
+        2**20,
+    )(node_target, grid)
+    right_sides, near = lax.optimization_barrier((right_sides, near))
+    near = [across(near[r - 1], 2 * r) for r in (1, 2, 3)]
+    coefficients, chip_translations, own_pair, stay, late = call(
         bind(local_kernel, local_levels),
-        (shape(boxes, rank, columns), shape(boxes, rank, width)),
-        (hbm, hbm, hbm),
-        (vmem, vmem),
+        (
+            shape(boxes, rank, columns),
+            shape(boxes, rank, width),
+            shape(2, 2, 2, 2 * rank, width),
+            shape(2, *part.shape),
+            shape(4, *part.shape),
+        ),
+        (hbm,) * 5,
+        (vmem,) * 5,
         [
             vmem((boxes, leaf_rows, columns), BF16),
             vmem((boxes, rank, leaf_rows), BF16),
             vmem((local_levels, boxes, rank, width), BF16),
             vmem((boxes, rank, columns), BF16),
             vmem((boxes, rank, columns), BF16),
+            smem((boxes,), jnp.int32),
             dma((4, 2)),
             dma((local_levels + 1,)),
+            dma,
+            dma,
         ],
         boxes * rank * columns * 2 * (leaf_rows + local_levels * width),
         6 * 2**20,
-    )(right_sides.reshape(boxes, leaf_rows, columns), leaf_basis, translations)
+    )(
+        right_sides.reshape(boxes, leaf_rows, columns), leaf_basis, translations, grid, node_target
+    )
+    late = across(late, 8)
+    coefficients, near = lax.optimization_barrier((coefficients, near))
     partner = across(coefficients, 1)
+    far = call(gather_kernel, shape(3, *near_part.shape), (vmem,) * 3, vmem, [], 0, 2**20)(*near)
+    partner, _ = lax.optimization_barrier((partner, far))
+    far = swapped(far)
     slots = call(
         chip_kernel,
         (shape(4, 2, rank, columns),) * 4,
@@ -346,37 +411,31 @@
         2**21,
     )(coefficients, partner, chip_translations)
     slots = [slots[0]] + [across(slots[r], 2 * r) for r in (1, 2, 3)]
-    stay, late, _ = lax.optimization_barrier((stay, late, slots[1]))
-    last = call(
-        merge_kernel,
-        (shape(2, 4 * rank + TILE, width),) * 4,
-        (vmem,) * 2,
-        (vmem,) * 4,
-        [],
-        0,
-        2**20,
-    )(stay, late)
-    slots, last = lax.optimization_barrier((slots, last))
+    late, *_ = lax.optimization_barrier((late, slots[1]))
+    late = call(split_kernel, (part,) * 4, (vmem,), (vmem,) * 4, [], 0, 2**20)(late)
+    late = [late[0]] + [across(late[r], 2 * r) for r in (1, 2, 3)]
+    here = call(collect_kernel, shape(4, *part.shape), (vmem,) * 4, vmem, [], 0, 2**20)(*late)
     keep, send = call(
         bind(quad_kernel, rank),
         (shape(4, 4, rank, columns), shape(4, 4, rank, columns)),
-        (vmem,) * 5,
+        (vmem,) * 9,
         (vmem,) * 2,
         [vmem((4, 4, 2, rank, columns), BF16)],
         2 * boxes * block * width,
         2**21,
-    )(*slots, pair)
+    )(*slots, own_pair, *near, far)
     received = across(send, 8)
-    last = [last[0]] + [across(last[r], 2 * r) for r in (1, 2, 3)]
+    here, _ = lax.optimization_barrier((here, send))
+    cross = swapped(here)
     own, send = call(
         bind(last_kernel, rank),
         (shape(16 * rank + TILE, columns),) * 2,
-        (vmem,) * 6,
+        (vmem,) * 9,
         (vmem,) * 2,
         [],
         boxes * block * width,
         2**21,
-    )(keep, received, *last)
+    )(keep, received, stay, *near, far, here, cross)
     partner = across(send, 1)
     applied = None
     for part in (own, partner):
@@ -406,7 +465,7 @@
 
     def per_device(right_sides, leaf_basis, translations, node_target, out_basis):
         devices = lax.axis_size(AXES)
-        fits = devices == 16 and leaf_basis.shape[0] == 32
+        fits = devices == 16 and lax.axis_size("groups") == 2 and leaf_basis.shape[0] == 32
         apply = move_early if fits else exchange_every_level
         return apply(right_sides, leaf_basis, translations, node_target, out_basis)
 

time: 53.8 us -> 48.7 us (0.905)
  waiting for transfers between devices: 24.1 us -> 17.9 us
  starting transfers between devices: 17.8 us -> 20.1 us
  Pallas kernels: 11.6 us -> 10.4 us
    ppermute x10 -> x13, waiting for transfers between devices: 24.1 us -> 8.83 us  [across(): return lax.ppermute(value, AXES, [(s, s ^ mask) for s in range(16)])]
    ppermute x0 -> x2, waiting for transfers between devices: none -> 9.04 us  [swapped(): return lax.ppermute(value, 'groups', [(0, 1), (1, 0)])]
    all_to_all x1 -> x0, starting transfers between devices: 5.26 us -> none  [among_places(): lax.all_to_all(value, AXES, 0, 0, axis_index_groups=quads, tiled=True)]
    ppermute x10 -> x13, starting transfers between devices: 12.6 us -> 16.9 us  [across(): return lax.ppermute(value, AXES, [(s, s ^ mask) for s in range(16)])]
    ppermute x0 -> x2, starting transfers between devices: none -> 3.26 us  [swapped(): return lax.ppermute(value, 'groups', [(0, 1), (1, 0)])]
    pallas_call x8 -> x10, Pallas kernels: 11.6 us -> 10.4 us  [placed(): run(*(pltpu.with_memory_space_constraint(operand, space) if space == pltp...]
  transfers between devices with their start and end apart: 11 -> 15, of which waited for: 7 -> 9; matrix products, arithmetic and copies ran while one was open for 0% -> 0% of each run, Pallas kernels for 13% -> 16%
where the time goes in v3:
time: 48.7 us; the launch traced here: 48.5 us
  starting transfers between devices  20.1 us (41%)
  waiting for transfers between devices  17.9 us (37%)
  Pallas kernels  10.4 us (21%)
    ppermute x13, starting transfers between devices, across(): return lax.ppermute(value, AXES, [(s, s ^ mask) for s in range(16)])  16.9 us
    pallas_call x10, Pallas kernels, placed(): run(*(pltpu.with_memory_space_constraint(operand, space) if space == pltp...  10.4 us
    ppermute x2, waiting for transfers between devices, swapped(): return lax.ppermute(value, 'groups', [(0, 1), (1, 0)])  9.04 us
    ppermute x13, waiting for transfers between devices, across(): return lax.ppermute(value, AXES, [(s, s ^ mask) for s in range(16)])  8.83 us
    ppermute x2, starting transfers between devices, swapped(): return lax.ppermute(value, 'groups', [(0, 1), (1, 0)])  3.26 us
  transfers between devices with their start and end apart: 15, of which 9 were waited for; matrix products, arithmetic and copies ran while one was open for 0% of the time, Pallas kernels for 16%

profile of v3, /device:TPU:0, one launch (start us, length us, event | category | flops | bytes accessed | tf_op | source)
XLA Modules:
  0.0 48.5 jit_solution(1274081052658823389)
XLA Ops:
  0.0 1.1 %shard_map.55 = (bf16[656,128]{1,0:T(8,128)(2,1)S(1)}, bf16[656,128]{1,0:T(8,128)(2,1)S(1)}, bf16[656,128]{1,0:T(8,128)(2,1)S(1)}) custom-call(s32[32]{0:T(128)} %refs_4_.1, bf16[2,2,2,2,2,576,128]{6,5,4,3,2,1,0:T(8,128)(2,1)} %bitcast.3), custom_call_target="tpu_custom_call" | custom-call | bytes 1048576 | tf_op jit(solution)/shard_map/pallas_call | solution.py:325
  1.1 3.0 %collective-permute-start = (bf16[656,128]{1,0:T(8,128)(2,1)S(1)}, bf16[656,128]{1,0:T(8,128)(2,1)S(1)}, u32[]{:S(2)}, u32[]{:S(2)}) collective-permute-start(bf16[656,128]{1,0:T(8,128)(2,1)S(1)} %get-tuple-element.41), channel_id=1, source_target_pairs={{0,2},{1,3},{2,0},{3,1},{4,6},{5,7},{6,4},{7,5},{8,10},{9,11},{10,... | collective-permute-start | bytes 503816 | tf_op jit(solution)/shard_map/ppermute | solution.py:351
  4.1 1.6 %collective-permute-start.1 = (bf16[656,128]{1,0:T(8,128)(2,1)S(1)}, bf16[656,128]{1,0:T(8,128)(2,1)S(1)}, u32[]{:S(2)}, u32[]{:S(2)}) collective-permute-start(bf16[656,128]{1,0:T(8,128)(2,1)S(1)} %get-tuple-element.42), channel_id=1, source_target_pairs={{0,4},{1,5},{2,6},{3,7},{4,0},{5,1},{6,2},{7,3},{8,12},{9,13},{10,... | collective-permute-start | bytes 503816 | tf_op jit(solution)/shard_map/ppermute | solution.py:351
  5.7 5.0 %shard_map.56 = (bf16[32,64,128]{2,1,0:T(8,128)(2,1)S(1)}, bf16[32,64,128]{2,1,0:T(8,128)(2,1)S(1)}, bf16[2,2,2,128,128]{4,3,2,1,0:T(8,128)(2,1)S(1)}, bf16[2,14...) custom-call(bf16[32,256,128]{2,1,0:T(8,128)(2,1)} %bitcast.5, bf16[32,64,256]{2,1,0:T(8,128)(2,1)} %refs_1_.3, ...), custom_call_target="tpu_custom_call" | custom-call | flops 469762048 | bytes 6291456 | tf_op jit(solution)/shard_map/pallas_call | solution.py:325
  10.7 0.0 collective-permute-done.near1.refs_5_.refs_3_
  10.7 0.6 %collective-permute-done.1.near2.refs_6_.refs_4_ = bf16[656,128]{1,0:T(8,128)(2,1)S(1)} collective-permute-done((bf16[656,128]{1,0:T(8,128)(2,1)S(1)}, bf16[656,128]{1,0:T(8,128)(2,1)S(1)}, u32[]{:S(2)}, u32[]{:S(2)}) %collective-permute-start.1) | collective-permute-done | bytes 167968 | tf_op jit(solution)/shard_map/ppermute | solution.py:351
  11.3 1.9 %collective-permute-done.2.near3.refs_7_.refs_5_ = bf16[656,128]{1,0:T(8,128)(2,1)S(1)} collective-permute-done((bf16[656,128]{1,0:T(8,128)(2,1)S(1)}, bf16[656,128]{1,0:T(8,128)(2,1)S(1)}, u32[]{:S(2)}, u32[]{:S(2)}) %collective-permute-start.2) | collective-permute-done | bytes 167968 | tf_op jit(solution)/shard_map/ppermute | solution.py:351
  13.3 0.0 collective-permute-start.3
  13.3 1.7 %collective-permute-start.7 = (bf16[3,656,128]{2,1,0:T(8,128)(2,1)S(1)}, bf16[3,656,128]{2,1,0:T(8,128)(2,1)S(1)}, u32[]{:S(2)}, u32[]{:S(2)}) collective-permute-start(bf16[3,656,128]{2,1,0:T(8,128)(2,1)S(1)} %shard_map.57), channel_id=1, source_target_pairs={{0,16},{16,0},{1,17},{17,1},{2,18},{18,2},{3,19},{19,3},{4,20},{20... | collective-permute-start | bytes 1511432 | tf_op jit(solution)/shard_map/ppermute | solution.py:354
  15.0 0.2 collective-permute-done.3.other_ref
  15.2 0.4 shard_map.58
  15.6 0.0 copy-start
  15.6 1.7 %collective-permute-start.4 = (bf16[4,2,64,128]{3,2,1,0:T(8,128)(2,1)S(1)}, bf16[4,2,64,128]{3,2,1,0:T(8,128)(2,1)S(1)}, u32[]{:S(2)}, u32[]{:S(2)}) collective-permute-start(bf16[4,2,64,128]{3,2,1,0:T(8,128)(2,1)S(1)} %get-tuple-element.51), channel_id=1, source_target_pairs={{0,2},{1,3},{2,0},{3,1},{4,6},{5,7},{6,4},{7,5},{8,10},{9,11},{10,... | collective-permute-start | bytes 393224 | tf_op jit(solution)/shard_map/ppermute | solution.py:351
  17.3 1.6 %collective-permute-start.5 = (bf16[4,2,64,128]{3,2,1,0:T(8,128)(2,1)S(1)}, bf16[4,2,64,128]{3,2,1,0:T(8,128)(2,1)S(1)}, u32[]{:S(2)}, u32[]{:S(2)}) collective-permute-start(bf16[4,2,64,128]{3,2,1,0:T(8,128)(2,1)S(1)} %get-tuple-element.52), channel_id=1, source_target_pairs={{0,4},{1,5},{2,6},{3,7},{4,0},{5,1},{6,2},{7,3},{8,12},{9,13},{10,... | collective-permute-start | bytes 393224 | tf_op jit(solution)/shard_map/ppermute | solution.py:351
  18.9 0.2 collective-permute-start.6
  19.1 2.7 %collective-permute-start.9 = (bf16[4,144,128]{2,1,0:T(8,128)(2,1)S(1)}, bf16[4,144,128]{2,1,0:T(8,128)(2,1)S(1)}, u32[]{:S(2)}, u32[]{:S(2)}) collective-permute-start(bf16[4,144,128]{2,1,0:T(8,128)(2,1)S(1)} %get-tuple-element.58), channel_id=1, source_target_pairs={{0,8},{1,9},{2,10},{3,11},{4,12},{5,13},{6,14},{7,15},{8,0},{9,1},... | collective-permute-start | bytes 442376 | tf_op jit(solution)/shard_map/ppermute | solution.py:351
  21.9 5.4 %collective-permute-done.7.refs_8_.refs_6_ = bf16[3,656,128]{2,1,0:T(8,128)(2,1)S(1)} collective-permute-done((bf16[3,656,128]{2,1,0:T(8,128)(2,1)S(1)}, bf16[3,656,128]{2,1,0:T(8,128)(2,1)S(1)}, u32[]{:S(2)}, u32[]{:S(2)}) %collective-permute-start.7) | collective-permute-done | bytes 503840 | tf_op jit(solution)/shard_map/ppermute | solution.py:354
  27.3 0.0 collective-permute-done.4.refs_1_
  27.3 1.1 %collective-permute-done.6.refs_3_ = bf16[4,2,64,128]{3,2,1,0:T(8,128)(2,1)S(1)} collective-permute-done((bf16[4,2,64,128]{3,2,1,0:T(8,128)(2,1)S(1)}, bf16[4,2,64,128]{3,2,1,0:T(8,128)(2,1)S(1)}, u32[]{:S(2)}, u32[]{:S(2)}) %collective-permute-start.6) | collective-permute-done | bytes 131104 | tf_op jit(solution)/shard_map/ppermute | solution.py:351
  28.4 0.8 %shard_map.59 = (bf16[4,4,64,128]{3,2,1,0:T(8,128)(2,1)S(1)}, bf16[4,4,64,128]{3,2,1,0:T(8,128)(2,1)S(1)}) custom-call(bf16[4,2,64,128]{3,2,1,0:T(8,128)(2,1)S(1)} %get-tuple-element.50.refs_0_, bf16[4,2,64,128]{3,2,1,0:T(8,128)(2,1)S(1)} %collective-permute-done.4.refs_1_, bf16[4,2,64,128]{3,2,1,0:T(8,128)(2,1)S(1)} %collective-permute-done.5.refs_2_, ...), custom_call_target="tpu_custom_call" | custom-call | flops 268435456 | bytes 2097152 | tf_op jit(solution)/shard_map/pallas_call | solution.py:325
  29.2 1.9 %collective-permute-start.8 = (bf16[4,4,64,128]{3,2,1,0:T(8,128)(2,1)S(1)}, bf16[4,4,64,128]{3,2,1,0:T(8,128)(2,1)S(1)}, u32[]{:S(2)}, u32[]{:S(2)}) collective-permute-start(bf16[4,4,64,128]{3,2,1,0:T(8,128)(2,1)S(1)} %get-tuple-element.56), channel_id=1, source_target_pairs={{0,8},{1,9},{2,10},{3,11},{4,12},{5,13},{6,14},{7,15},{8,0},{9,1},... | collective-permute-start | bytes 786440 | tf_op jit(solution)/shard_map/ppermute | solution.py:351
  31.1 1.4 %collective-permute-start.10 = (bf16[144,128]{1,0:T(8,128)(2,1)S(1)}, bf16[144,128]{1,0:T(8,128)(2,1)S(1)}, u32[]{:S(2)}, u32[]{:S(2)}) collective-permute-start(bf16[144,128]{1,0:T(8,128)(2,1)S(1)} %get-tuple-element.61), channel_id=1, source_target_pairs={{0,2},{1,3},{2,0},{3,1},{4,6},{5,7},{6,4},{7,5},{8,10},{9,11},{10,... | collective-permute-start | bytes 110600 | tf_op jit(solution)/shard_map/ppermute | solution.py:351
  32.5 2.6 %collective-permute-start.11 = (bf16[144,128]{1,0:T(8,128)(2,1)S(1)}, bf16[144,128]{1,0:T(8,128)(2,1)S(1)}, u32[]{:S(2)}, u32[]{:S(2)}) collective-permute-start(bf16[144,128]{1,0:T(8,128)(2,1)S(1)} %get-tuple-element.62), channel_id=1, source_target_pairs={{0,4},{1,5},{2,6},{3,7},{4,0},{5,1},{6,2},{7,3},{8,12},{9,13},{10,... | collective-permute-start | bytes 110600 | tf_op jit(solution)/shard_map/ppermute | solution.py:351
  35.1 2.5 %collective-permute-done.11.late2 = bf16[144,128]{1,0:T(8,128)(2,1)S(1)} collective-permute-done((bf16[144,128]{1,0:T(8,128)(2,1)S(1)}, bf16[144,128]{1,0:T(8,128)(2,1)S(1)}, u32[]{:S(2)}, u32[]{:S(2)}) %collective-permute-start.11) | collective-permute-done | bytes 36896 | tf_op jit(solution)/shard_map/ppermute | solution.py:351
  37.6 2.4 %collective-permute-done.12.late3 = bf16[144,128]{1,0:T(8,128)(2,1)S(1)} collective-permute-done((bf16[144,128]{1,0:T(8,128)(2,1)S(1)}, bf16[144,128]{1,0:T(8,128)(2,1)S(1)}, u32[]{:S(2)}, u32[]{:S(2)}) %collective-permute-start.12) | collective-permute-done | bytes 36896 | tf_op jit(solution)/shard_map/ppermute | solution.py:351
  40.0 1.6 %collective-permute-start.13 = (bf16[4,144,128]{2,1,0:T(8,128)(2,1)S(1)}, bf16[4,144,128]{2,1,0:T(8,128)(2,1)S(1)}, u32[]{:S(2)}, u32[]{:S(2)}) collective-permute-start(bf16[4,144,128]{2,1,0:T(8,128)(2,1)S(1)} %shard_map.61.refs_7_), channel_id=1, source_target_pairs={{0,16},{16,0},{1,17},{17,1},{2,18},{18,2},{3,19},{19,3},{4,20},{20... | collective-permute-start | bytes 442376 | tf_op jit(solution)/shard_map/ppermute | solution.py:354
  41.5 3.7 %collective-permute-done.13.refs_8_ = bf16[4,144,128]{2,1,0:T(8,128)(2,1)S(1)} collective-permute-done((bf16[4,144,128]{2,1,0:T(8,128)(2,1)S(1)}, bf16[4,144,128]{2,1,0:T(8,128)(2,1)S(1)}, u32[]{:S(2)}, u32[]{:S(2)}) %collective-permute-start.13) | collective-permute-done | bytes 147488 | tf_op jit(solution)/shard_map/ppermute | solution.py:354
  45.2 0.4 shard_map.62
  45.6 0.1 collective-permute-start.14
  45.7 1.3 %shard_map.63.refs_2_ = bf16[32,256,128]{2,1,0:T(8,128)(2,1)} custom-call(bf16[1040,128]{1,0:T(8,128)(2,1)S(1)} %get-tuple-element.66.refs_0_, bf16[32,64,256]{2,1,0:T(8,128)(2,1)S(1)} %copy-done), custom_call_target="tpu_custom_call" | custom-call | flops 134217728 | bytes 2097152 | tf_op jit(solution)/shard_map/pallas_call | solution.py:325
  47.0 0.2 collective-permute-done.14.refs_0_
  47.2 1.3 %shard_map.64 = bf16[32,256,128]{2,1,0:T(8,128)(2,1)} custom-call(bf16[1040,128]{1,0:T(8,128)(2,1)S(1)} %collective-permute-done.14.refs_0_, bf16[32,64,256]{2,1,0:T(8,128)(2,1)S(1)} %copy-done, bf16[32,256,128]{2,1,0:T(8,128)(2,1)} %shard_map.63.refs_2_), custom_call_target="tpu_custom_call", output_to_operand_aliasing={{}: (2, {})} | custom-call | flops 134217728 | bytes 2097152 | tf_op jit(solution)/shard_map/pallas_call | solution.py:325
  (10 shorter events, 0.1 us)
Async XLA Ops:
  1.1 9.6 %collective-permute-start = (bf16[656,128]{1,0:T(8,128)(2,1)S(1)}, bf16[656,128]{1,0:T(8,128)(2,1)S(1)}, u32[]{:S(2)}, u32[]{:S(2)}) collective-permute-start(bf16[656,128]{1,0:T(8,128)(2,1)S(1)} %get-tuple-element.41), channel_id=1, source_target_pairs={{0,2},{1,3},{2,0},{3,1},{4,6},{5,7},{6,4},{7,5},{8,10},{9,11},{10,... | collective-permute-start | bytes 503816 | tf_op jit(solution)/shard_map/ppermute | solution.py:351
  4.1 7.2 %collective-permute-start.1 = (bf16[656,128]{1,0:T(8,128)(2,1)S(1)}, bf16[656,128]{1,0:T(8,128)(2,1)S(1)}, u32[]{:S(2)}, u32[]{:S(2)}) collective-permute-start(bf16[656,128]{1,0:T(8,128)(2,1)S(1)} %get-tuple-element.42), channel_id=1, source_target_pairs={{0,4},{1,5},{2,6},{3,7},{4,0},{5,1},{6,2},{7,3},{8,12},{9,13},{10,... | collective-permute-start | bytes 503816 | tf_op jit(solution)/shard_map/ppermute | solution.py:351
  5.7 7.6 %collective-permute-start.2 = (bf16[656,128]{1,0:T(8,128)(2,1)S(1)}, bf16[656,128]{1,0:T(8,128)(2,1)S(1)}, u32[]{:S(2)}, u32[]{:S(2)}) collective-permute-start(bf16[656,128]{1,0:T(8,128)(2,1)S(1)} %get-tuple-element.43), channel_id=1, source_target_pairs={{0,6},{1,7},{2,4},{3,5},{4,2},{5,3},{6,0},{7,1},{8,14},{9,15},{10,... | collective-permute-start | bytes 503816 | tf_op jit(solution)/shard_map/ppermute | solution.py:351
  13.3 1.9 %collective-permute-start.3 = (bf16[32,64,128]{2,1,0:T(8,128)(2,1)S(1)}, bf16[32,64,128]{2,1,0:T(8,128)(2,1)S(1)}, u32[]{:S(2)}, u32[]{:S(2)}) collective-permute-start(bf16[32,64,128]{2,1,0:T(8,128)(2,1)S(1)} %get-tuple-element.44.own_ref), channel_id=1, source_target_pairs={{0,1},{1,0},{2,3},{3,2},{4,5},{5,4},{6,7},{7,6},{8,9},{9,8},{10,11... | collective-permute-start | bytes 1572872 | tf_op jit(solution)/shard_map/ppermute | solution.py:351
  13.3 14.0 %collective-permute-start.7 = (bf16[3,656,128]{2,1,0:T(8,128)(2,1)S(1)}, bf16[3,656,128]{2,1,0:T(8,128)(2,1)S(1)}, u32[]{:S(2)}, u32[]{:S(2)}) collective-permute-start(bf16[3,656,128]{2,1,0:T(8,128)(2,1)S(1)} %shard_map.57), channel_id=1, source_target_pairs={{0,16},{16,0},{1,17},{17,1},{2,18},{18,2},{3,19},{19,3},{4,20},{20... | collective-permute-start | bytes 1511432 | tf_op jit(solution)/shard_map/ppermute | solution.py:354
  15.6 30.1 %copy-start = (bf16[32,64,256]{2,1,0:T(8,128)(2,1)S(1)}, bf16[32,64,256]{2,1,0:T(8,128)(2,1)}, u32[]{:S(2)}) copy-start(bf16[32,64,256]{2,1,0:T(8,128)(2,1)} %refs_1_.5) | copy-start | bytes 3145732
  15.6 11.7 %collective-permute-start.4 = (bf16[4,2,64,128]{3,2,1,0:T(8,128)(2,1)S(1)}, bf16[4,2,64,128]{3,2,1,0:T(8,128)(2,1)S(1)}, u32[]{:S(2)}, u32[]{:S(2)}) collective-permute-start(bf16[4,2,64,128]{3,2,1,0:T(8,128)(2,1)S(1)} %get-tuple-element.51), channel_id=1, source_target_pairs={{0,2},{1,3},{2,0},{3,1},{4,6},{5,7},{6,4},{7,5},{8,10},{9,11},{10,... | collective-permute-start | bytes 393224 | tf_op jit(solution)/shard_map/ppermute | solution.py:351
  17.3 9.9 %collective-permute-start.5 = (bf16[4,2,64,128]{3,2,1,0:T(8,128)(2,1)S(1)}, bf16[4,2,64,128]{3,2,1,0:T(8,128)(2,1)S(1)}, u32[]{:S(2)}, u32[]{:S(2)}) collective-permute-start(bf16[4,2,64,128]{3,2,1,0:T(8,128)(2,1)S(1)} %get-tuple-element.52), channel_id=1, source_target_pairs={{0,4},{1,5},{2,6},{3,7},{4,0},{5,1},{6,2},{7,3},{8,12},{9,13},{10,... | collective-permute-start | bytes 393224 | tf_op jit(solution)/shard_map/ppermute | solution.py:351
  18.9 9.4 %collective-permute-start.6 = (bf16[4,2,64,128]{3,2,1,0:T(8,128)(2,1)S(1)}, bf16[4,2,64,128]{3,2,1,0:T(8,128)(2,1)S(1)}, u32[]{:S(2)}, u32[]{:S(2)}) collective-permute-start(bf16[4,2,64,128]{3,2,1,0:T(8,128)(2,1)S(1)} %get-tuple-element.53), channel_id=1, source_target_pairs={{0,6},{1,7},{2,4},{3,5},{4,2},{5,3},{6,0},{7,1},{8,14},{9,15},{10,... | collective-permute-start | bytes 393224 | tf_op jit(solution)/shard_map/ppermute | solution.py:351
  19.1 11.9 %collective-permute-start.9 = (bf16[4,144,128]{2,1,0:T(8,128)(2,1)S(1)}, bf16[4,144,128]{2,1,0:T(8,128)(2,1)S(1)}, u32[]{:S(2)}, u32[]{:S(2)}) collective-permute-start(bf16[4,144,128]{2,1,0:T(8,128)(2,1)S(1)} %get-tuple-element.58), channel_id=1, source_target_pairs={{0,8},{1,9},{2,10},{3,11},{4,12},{5,13},{6,14},{7,15},{8,0},{9,1},... | collective-permute-start | bytes 442376 | tf_op jit(solution)/shard_map/ppermute | solution.py:351
  29.2 16.0 %collective-permute-start.8 = (bf16[4,4,64,128]{3,2,1,0:T(8,128)(2,1)S(1)}, bf16[4,4,64,128]{3,2,1,0:T(8,128)(2,1)S(1)}, u32[]{:S(2)}, u32[]{:S(2)}) collective-permute-start(bf16[4,4,64,128]{3,2,1,0:T(8,128)(2,1)S(1)} %get-tuple-element.56), channel_id=1, source_target_pairs={{0,8},{1,9},{2,10},{3,11},{4,12},{5,13},{6,14},{7,15},{8,0},{9,1},... | collective-permute-start | bytes 786440 | tf_op jit(solution)/shard_map/ppermute | solution.py:351
  31.1 4.0 %collective-permute-start.10 = (bf16[144,128]{1,0:T(8,128)(2,1)S(1)}, bf16[144,128]{1,0:T(8,128)(2,1)S(1)}, u32[]{:S(2)}, u32[]{:S(2)}) collective-permute-start(bf16[144,128]{1,0:T(8,128)(2,1)S(1)} %get-tuple-element.61), channel_id=1, source_target_pairs={{0,2},{1,3},{2,0},{3,1},{4,6},{5,7},{6,4},{7,5},{8,10},{9,11},{10,... | collective-permute-start | bytes 110600 | tf_op jit(solution)/shard_map/ppermute | solution.py:351
  32.5 5.1 %collective-permute-start.11 = (bf16[144,128]{1,0:T(8,128)(2,1)S(1)}, bf16[144,128]{1,0:T(8,128)(2,1)S(1)}, u32[]{:S(2)}, u32[]{:S(2)}) collective-permute-start(bf16[144,128]{1,0:T(8,128)(2,1)S(1)} %get-tuple-element.62), channel_id=1, source_target_pairs={{0,4},{1,5},{2,6},{3,7},{4,0},{5,1},{6,2},{7,3},{8,12},{9,13},{10,... | collective-permute-start | bytes 110600 | tf_op jit(solution)/shard_map/ppermute | solution.py:351
  35.1 4.9 %collective-permute-start.12 = (bf16[144,128]{1,0:T(8,128)(2,1)S(1)}, bf16[144,128]{1,0:T(8,128)(2,1)S(1)}, u32[]{:S(2)}, u32[]{:S(2)}) collective-permute-start(bf16[144,128]{1,0:T(8,128)(2,1)S(1)} %get-tuple-element.63), channel_id=1, source_target_pairs={{0,6},{1,7},{2,4},{3,5},{4,2},{5,3},{6,0},{7,1},{8,14},{9,15},{10,... | collective-permute-start | bytes 110600 | tf_op jit(solution)/shard_map/ppermute | solution.py:351
  40.0 5.2 %collective-permute-start.13 = (bf16[4,144,128]{2,1,0:T(8,128)(2,1)S(1)}, bf16[4,144,128]{2,1,0:T(8,128)(2,1)S(1)}, u32[]{:S(2)}, u32[]{:S(2)}) collective-permute-start(bf16[4,144,128]{2,1,0:T(8,128)(2,1)S(1)} %shard_map.61.refs_7_), channel_id=1, source_target_pairs={{0,16},{16,0},{1,17},{17,1},{2,18},{18,2},{3,19},{19,3},{4,20},{20... | collective-permute-start | bytes 442376 | tf_op jit(solution)/shard_map/ppermute | solution.py:354
  45.6 1.6 %collective-permute-start.14 = (bf16[1040,128]{1,0:T(8,128)(2,1)S(1)}, bf16[1040,128]{1,0:T(8,128)(2,1)S(1)}, u32[]{:S(2)}, u32[]{:S(2)}) collective-permute-start(bf16[1040,128]{1,0:T(8,128)(2,1)S(1)} %get-tuple-element.65), channel_id=1, source_target_pairs={{0,1},{1,0},{2,3},{3,2},{4,5},{5,4},{6,7},{7,6},{8,9},{9,8},{10,11... | collective-permute-start | bytes 798728 | tf_op jit(solution)/shard_map/ppermute | solution.py:351

commit v4 on v3

--- a/solution.py
+++ b/solution.py
@@ -123,10 +123,14 @@
     return level_rows(trans_ref, rank, i4, own_place() ^ r, own_half() ^ side, 8, 1), slots
 
 
-def spot_tile(target, i4, r, side, columns):
-    first = lax.broadcasted_iota(jnp.int32, (TILE, columns), 0) == 0
-    box = i4 * 16 + first_box(own_place() ^ r) + (own_half() ^ side)
-    return jnp.where(first, target[box] % 32, target[box + 8] % 32).astype(jnp.float32).astype(BF16)
+def spot_tile(target, i4, r, columns):
+    row = lax.broadcasted_iota(jnp.int32, (TILE, columns), 0)
+    base = i4 * 16 + first_box(own_place() ^ r)
+    half = own_half()
+    spots = [target[base + (half ^ side) + i3 * 8] % 32 for side in range(2) for i3 in range(2)]
+    upper = jnp.where(row == 2, spots[2], spots[3])
+    tile = jnp.where(row < 2, jnp.where(row == 0, spots[0], spots[1]), upper)
+    return tile.astype(jnp.float32).astype(BF16)
 
 
 def pack_kernel(rank, target_ref, trans_ref, *refs):
@@ -139,18 +143,27 @@
         ref = out_refs[r - 1]
         slots = ref.at[pl.ds(0, 8 * rank)].reshape(2, 2, 2 * rank, columns)
         pairs.append((level_rows(trans_ref, rank, group, own_place() ^ r, BOTH, 6, 2), slots))
-        pairs.append(last_level(rank, trans_ref, group, r, 0, ref.at[pl.ds(8 * rank, 2 * rank)]))
+        for side in range(2):
+            rows = ref.at[pl.ds((8 + 2 * side) * rank, 2 * rank)]
+            pairs.append(last_level(rank, trans_ref, group, r, side, rows))
     copies = start_all(pairs, sem)
     target_copy.wait()
     for r in (3, 2, 1):
-        out_refs[r - 1][pl.ds(10 * rank, TILE), :] = spot_tile(target, group, r, 0, columns)
+        out_refs[r - 1][pl.ds(12 * rank, TILE), :] = spot_tile(target, group, r, columns)
     for copy in copies:
         copy.wait()
 
 
-def gather_kernel(near1, near2, near3, out_ref):
+def gather_kernel(rank, near1, near2, near3, out_ref):
     for index, ref in enumerate((near1, near2, near3)):
-        out_ref[index] = ref[...]
+        out_ref[index, pl.ds(0, 10 * rank), :] = ref[pl.ds(0, 10 * rank), :]
+        out_ref[index, pl.ds(10 * rank, TILE), :] = ref[pl.ds(12 * rank, TILE), :]
+
+
+def late_kernel(rank, late_ref, near1, near2, near3, out_ref):
+    out_ref[0] = late_ref[...]
+    for index, ref in enumerate((near1, near2, near3)):
+        out_ref[index + 1] = ref[pl.ds(10 * rank, 2 * rank + TILE), :]
 
 
 def local_kernel(
@@ -187,14 +200,13 @@
     rest = [(level_rows(grid_ref, rank, BOTH, own_place(), BOTH, 6, 2), pair_ref)]
     two = pl.ds(0, 2 * rank)
     rest += [last_level(rank, grid_ref, i4, 0, 0, stay_ref.at[i4, two]) for i4 in range(2)]
-    rest += [last_level(rank, grid_ref, group, r, 1, late_ref.at[r, two]) for r in range(4)]
+    rest.append(last_level(rank, grid_ref, group, 0, 1, late_ref.at[two]))
     rest = start_all(rest, rest_sem)
     target_copy.wait()
     tile = pl.ds(2 * rank, TILE)
     for i4 in range(2):
-        stay_ref[i4, tile, :] = spot_tile(target_smem, i4, 0, 0, columns)
-    for r in range(4):
-        late_ref[r, tile, :] = spot_tile(target_smem, group, r, 1, columns)
+        stay_ref[i4, tile, :] = spot_tile(target_smem, i4, 0, columns)
+    late_ref[tile, :] = spot_tile(target_smem, group, 0, columns)
     for part in range(4):
         for copy in loads[part]:
             copy.wait()
@@ -251,16 +263,6 @@
             out_ref[r, q] = product(matrix(r, h, i3, bit, 1), rows)
 
 
-def split_kernel(late_ref, *out_refs):
-    for r in range(4):
-        out_refs[r][...] = late_ref[r]
-
-
-def collect_kernel(late0, late1, late2, late3, out_ref):
-    for r, ref in enumerate((late0, late1, late2, late3)):
-        out_ref[r] = ref[...]
-
-
 def last_kernel(
     rank, keep_ref, recv_ref, stay_ref, near1, near2, near3, far_ref, here_ref, cross_ref, own_ref, send_ref
 ):
@@ -268,18 +270,20 @@
 
     def source(side, r, h):
         if side:
-            return (here_ref, cross_ref)[h].at[r], 0
+            return (here_ref, cross_ref)[h].at[r], 0, 2 * rank
         if r == 0:
-            return stay_ref.at[group ^ h], 0
-        return (far_ref.at[r - 1] if h else (near1, near2, near3)[r - 1]), 8 * rank
+            return stay_ref.at[group ^ h], 0, 2 * rank
+        if h:
+            return far_ref.at[r - 1], 8 * rank, 10 * rank
+        return (near1, near2, near3)[r - 1], 8 * rank, 12 * rank
 
     for out_ref, bit in ((send_ref, 1 - core), (own_ref, core)):
         tile = []
         for side in range(2):
             for r in range(4):
                 for h in range(2):
-                    ref, base = source(side, r, h)
-                    spots = ref[pl.ds(base + 2 * rank, TILE), :].astype(jnp.float32)
+                    ref, base, at = source(side, r, h)
+                    spots = ref[pl.ds(at, TILE), :].astype(jnp.float32)[2 * side : 2 * side + 2]
                     tile.append(jnp.where(bit == 0, spots[0:1], spots[1:2]))
                     q = (group ^ h) * 2 + bit
                     sides = (keep_ref[r, q], recv_ref[r, q])
@@ -355,7 +359,7 @@
 
     grid = translations.reshape(2, 2, 2, 2, 2, -1, width)
     part = shape(2 * rank + TILE, width)
-    near_part = shape(10 * rank + TILE, width)
+    near_part = shape(12 * rank + TILE, width)
     near = call(
         bind(pack_kernel, rank),
         (near_part,) * 3,
@@ -374,7 +378,7 @@
             shape(boxes, rank, width),
             shape(2, 2, 2, 2 * rank, width),
             shape(2, *part.shape),
-            shape(4, *part.shape),
+            part,
         ),
         (hbm,) * 5,
         (vmem,) * 5,
@@ -395,10 +399,9 @@
     )(
         right_sides.reshape(boxes, leaf_rows, columns), leaf_basis, translations, grid, node_target
     )
-    late = across(late, 8)
     coefficients, near = lax.optimization_barrier((coefficients, near))
     partner = across(coefficients, 1)
-    far = call(gather_kernel, shape(3, *near_part.shape), (vmem,) * 3, vmem, [], 0, 2**20)(*near)
+    far = call(bind(gather_kernel, rank), shape(3, 10 * rank + TILE, width), (vmem,) * 3, vmem, [], 0, 2**20)(*near)
     partner, _ = lax.optimization_barrier((partner, far))
     far = swapped(far)
     slots = call(
@@ -411,10 +414,11 @@
         2**21,
     )(coefficients, partner, chip_translations)
     slots = [slots[0]] + [across(slots[r], 2 * r) for r in (1, 2, 3)]
-    late, *_ = lax.optimization_barrier((late, slots[1]))
-    late = call(split_kernel, (part,) * 4, (vmem,), (vmem,) * 4, [], 0, 2**20)(late)
-    late = [late[0]] + [across(late[r], 2 * r) for r in (1, 2, 3)]
-    here = call(collect_kernel, shape(4, *part.shape), (vmem,) * 4, vmem, [], 0, 2**20)(*late)
+    _, late = lax.optimization_barrier((slots[1], late))
+    here = call(
+        bind(late_kernel, rank), shape(4, *part.shape), (vmem,) * 4, vmem, [], 0, 2**20
+    )(late, *near)
+    here = across(here, 8)
     keep, send = call(
         bind(quad_kernel, rank),
         (shape(4, 4, rank, columns), shape(4, 4, rank, columns)),

time: 48.7 us -> 47.7 us (0.979)
  starting transfers between devices: 20.1 us -> 17 us
  waiting for transfers between devices: 17.9 us -> 19.9 us
    ppermute x13 -> x10, waiting for transfers between devices: 8.83 us -> 16.7 us  [across(): return lax.ppermute(value, AXES, [(s, s ^ mask) for s in range(16)])]
    ppermute x2, waiting for transfers between devices: 9.04 us -> 3.26 us  [swapped(): return lax.ppermute(value, 'groups', [(0, 1), (1, 0)])]
    ppermute x13 -> x10, starting transfers between devices: 16.9 us -> 13.8 us  [across(): return lax.ppermute(value, AXES, [(s, s ^ mask) for s in range(16)])]
    pallas_call x10 -> x9, Pallas kernels: 10.4 us -> 10.4 us  [placed(): run(*(pltpu.with_memory_space_constraint(operand, space) if space == pltp...]
  transfers between devices with their start and end apart: 15 -> 12, of which waited for: 9 -> 7; matrix products, arithmetic and copies ran while one was open for 0% -> 0% of each run, Pallas kernels for 16% -> 16%
where the time goes in v4:
time: 47.7 us; the launch traced here: 47.5 us
  waiting for transfers between devices  19.9 us (42%)
  starting transfers between devices  17 us (36%)
  Pallas kernels  10.4 us (22%)
    ppermute x10, waiting for transfers between devices, across(): return lax.ppermute(value, AXES, [(s, s ^ mask) for s in range(16)])  16.7 us
    ppermute x10, starting transfers between devices, across(): return lax.ppermute(value, AXES, [(s, s ^ mask) for s in range(16)])  13.8 us
    pallas_call x9, Pallas kernels, placed(): run(*(pltpu.with_memory_space_constraint(operand, space) if space == pltp...  10.4 us
    ppermute x2, waiting for transfers between devices, swapped(): return lax.ppermute(value, 'groups', [(0, 1), (1, 0)])  3.26 us
    ppermute x2, starting transfers between devices, swapped(): return lax.ppermute(value, 'groups', [(0, 1), (1, 0)])  3.2 us
  transfers between devices with their start and end apart: 12, of which 7 were waited for; matrix products, arithmetic and copies ran while one was open for 0% of the time, Pallas kernels for 16%

profile of v4, /device:TPU:0, one launch (start us, length us, event | category | flops | bytes accessed | tf_op | source)
XLA Modules:
  0.0 47.5 jit_solution(8382846438460044020)
XLA Ops:
  0.0 1.1 %shard_map.55 = (bf16[784,128]{1,0:T(8,128)(2,1)S(1)}, bf16[784,128]{1,0:T(8,128)(2,1)S(1)}, bf16[784,128]{1,0:T(8,128)(2,1)S(1)}) custom-call(s32[32]{0:T(128)} %refs_4_.1, bf16[2,2,2,2,2,576,128]{6,5,4,3,2,1,0:T(8,128)(2,1)} %bitcast.3), custom_call_target="tpu_custom_call" | custom-call | bytes 1048576 | tf_op jit(solution)/shard_map/pallas_call | solution.py:329
  1.1 3.0 %collective-permute-start = (bf16[784,128]{1,0:T(8,128)(2,1)S(1)}, bf16[784,128]{1,0:T(8,128)(2,1)S(1)}, u32[]{:S(2)}, u32[]{:S(2)}) collective-permute-start(bf16[784,128]{1,0:T(8,128)(2,1)S(1)} %get-tuple-element.37), channel_id=1, source_target_pairs={{0,2},{1,3},{2,0},{3,1},{4,6},{5,7},{6,4},{7,5},{8,10},{9,11},{10,... | collective-permute-start | bytes 602120 | tf_op jit(solution)/shard_map/ppermute | solution.py:355
  4.2 1.6 %collective-permute-start.1 = (bf16[784,128]{1,0:T(8,128)(2,1)S(1)}, bf16[784,128]{1,0:T(8,128)(2,1)S(1)}, u32[]{:S(2)}, u32[]{:S(2)}) collective-permute-start(bf16[784,128]{1,0:T(8,128)(2,1)S(1)} %get-tuple-element.38), channel_id=1, source_target_pairs={{0,4},{1,5},{2,6},{3,7},{4,0},{5,1},{6,2},{7,3},{8,12},{9,13},{10,... | collective-permute-start | bytes 602120 | tf_op jit(solution)/shard_map/ppermute | solution.py:355
  5.7 0.0 collective-permute-start.2
  5.7 5.0 %shard_map.56 = (bf16[32,64,128]{2,1,0:T(8,128)(2,1)S(1)}, bf16[32,64,128]{2,1,0:T(8,128)(2,1)S(1)}, bf16[2,2,2,128,128]{4,3,2,1,0:T(8,128)(2,1)S(1)}, bf16[2,14...) custom-call(bf16[32,256,128]{2,1,0:T(8,128)(2,1)} %bitcast.5, bf16[32,64,256]{2,1,0:T(8,128)(2,1)} %refs_1_.3, ...), custom_call_target="tpu_custom_call" | custom-call | flops 469762048 | bytes 6291456 | tf_op jit(solution)/shard_map/pallas_call | solution.py:329
  10.8 0.0 collective-permute-done.refs_0_.refs_5_.refs_1_.refs_3_
  10.8 1.3 %collective-permute-done.1.refs_1_.refs_6_.refs_2_.refs_4_ = bf16[784,128]{1,0:T(8,128)(2,1)S(1)} collective-permute-done((bf16[784,128]{1,0:T(8,128)(2,1)S(1)}, bf16[784,128]{1,0:T(8,128)(2,1)S(1)}, u32[]{:S(2)}, u32[]{:S(2)}) %collective-permute-start.1) | collective-permute-done | bytes 200736 | tf_op jit(solution)/shard_map/ppermute | solution.py:355
  12.1 2.6 %collective-permute-done.2.refs_2_.refs_7_.refs_3_.refs_5_ = bf16[784,128]{1,0:T(8,128)(2,1)S(1)} collective-permute-done((bf16[784,128]{1,0:T(8,128)(2,1)S(1)}, bf16[784,128]{1,0:T(8,128)(2,1)S(1)}, u32[]{:S(2)}, u32[]{:S(2)}) %collective-permute-start.2) | collective-permute-done | bytes 200736 | tf_op jit(solution)/shard_map/ppermute | solution.py:355
  14.7 0.0 collective-permute-start.3
  14.7 1.7 %collective-permute-start.7 = (bf16[3,656,128]{2,1,0:T(8,128)(2,1)S(1)}, bf16[3,656,128]{2,1,0:T(8,128)(2,1)S(1)}, u32[]{:S(2)}, u32[]{:S(2)}) collective-permute-start(bf16[3,656,128]{2,1,0:T(8,128)(2,1)S(1)} %shard_map.57), channel_id=1, source_target_pairs={{0,16},{16,0},{1,17},{17,1},{2,18},{18,2},{3,19},{19,3},{4,20},{20... | collective-permute-start | bytes 1511432 | tf_op jit(solution)/shard_map/ppermute | solution.py:358
  16.5 0.2 collective-permute-done.3.other_ref
  16.6 0.4 shard_map.58
  17.0 1.7 %collective-permute-start.4 = (bf16[4,2,64,128]{3,2,1,0:T(8,128)(2,1)S(1)}, bf16[4,2,64,128]{3,2,1,0:T(8,128)(2,1)S(1)}, u32[]{:S(2)}, u32[]{:S(2)}) collective-permute-start(bf16[4,2,64,128]{3,2,1,0:T(8,128)(2,1)S(1)} %get-tuple-element.47), channel_id=1, source_target_pairs={{0,2},{1,3},{2,0},{3,1},{4,6},{5,7},{6,4},{7,5},{8,10},{9,11},{10,... | collective-permute-start | bytes 393224 | tf_op jit(solution)/shard_map/ppermute | solution.py:355
  18.8 1.6 %collective-permute-start.5 = (bf16[4,2,64,128]{3,2,1,0:T(8,128)(2,1)S(1)}, bf16[4,2,64,128]{3,2,1,0:T(8,128)(2,1)S(1)}, u32[]{:S(2)}, u32[]{:S(2)}) collective-permute-start(bf16[4,2,64,128]{3,2,1,0:T(8,128)(2,1)S(1)} %get-tuple-element.48), channel_id=1, source_target_pairs={{0,4},{1,5},{2,6},{3,7},{4,0},{5,1},{6,2},{7,3},{8,12},{9,13},{10,... | collective-permute-start | bytes 393224 | tf_op jit(solution)/shard_map/ppermute | solution.py:355
  20.3 0.2 collective-permute-start.6
  20.6 2.0 %collective-permute-done.4.refs_1_ = bf16[4,2,64,128]{3,2,1,0:T(8,128)(2,1)S(1)} collective-permute-done((bf16[4,2,64,128]{3,2,1,0:T(8,128)(2,1)S(1)}, bf16[4,2,64,128]{3,2,1,0:T(8,128)(2,1)S(1)}, u32[]{:S(2)}, u32[]{:S(2)}) %collective-permute-start.4) | collective-permute-done | bytes 131104 | tf_op jit(solution)/shard_map/ppermute | solution.py:355
  22.6 0.0 copy-start
  22.7 2.8 %collective-permute-start.9 = (bf16[4,144,128]{2,1,0:T(8,128)(2,1)S(1)}, bf16[4,144,128]{2,1,0:T(8,128)(2,1)S(1)}, u32[]{:S(2)}, u32[]{:S(2)}) collective-permute-start(bf16[4,144,128]{2,1,0:T(8,128)(2,1)S(1)} %shard_map.60), channel_id=1, source_target_pairs={{0,8},{1,9},{2,10},{3,11},{4,12},{5,13},{6,14},{7,15},{8,0},{9,1},... | collective-permute-start | bytes 442376 | tf_op jit(solution)/shard_map/ppermute | solution.py:355
  25.5 3.3 %collective-permute-done.7.refs_8_.refs_6_ = bf16[3,656,128]{2,1,0:T(8,128)(2,1)S(1)} collective-permute-done((bf16[3,656,128]{2,1,0:T(8,128)(2,1)S(1)}, bf16[3,656,128]{2,1,0:T(8,128)(2,1)S(1)}, u32[]{:S(2)}, u32[]{:S(2)}) %collective-permute-start.7) | collective-permute-done | bytes 503840 | tf_op jit(solution)/shard_map/ppermute | solution.py:358
  28.7 0.0 collective-permute-done.5.refs_2_
  28.7 0.0 collective-permute-done.6.refs_3_
  28.7 0.8 %shard_map.59 = (bf16[4,4,64,128]{3,2,1,0:T(8,128)(2,1)S(1)}, bf16[4,4,64,128]{3,2,1,0:T(8,128)(2,1)S(1)}) custom-call(bf16[4,2,64,128]{3,2,1,0:T(8,128)(2,1)S(1)} %get-tuple-element.46.refs_0_, bf16[4,2,64,128]{3,2,1,0:T(8,128)(2,1)S(1)} %collective-permute-done.4.refs_1_, bf16[4,2,64,128]{3,2,1,0:T(8,128)(2,1)S(1)} %collective-permute-done.5.refs_2_, ...), custom_call_target="tpu_custom_call" | custom-call | flops 268435456 | bytes 2097152 | tf_op jit(solution)/shard_map/pallas_call | solution.py:329
  29.5 2.8 %collective-permute-start.8 = (bf16[4,4,64,128]{3,2,1,0:T(8,128)(2,1)S(1)}, bf16[4,4,64,128]{3,2,1,0:T(8,128)(2,1)S(1)}, u32[]{:S(2)}, u32[]{:S(2)}) collective-permute-start(bf16[4,4,64,128]{3,2,1,0:T(8,128)(2,1)S(1)} %get-tuple-element.52), channel_id=1, source_target_pairs={{0,8},{1,9},{2,10},{3,11},{4,12},{5,13},{6,14},{7,15},{8,0},{9,1},... | collective-permute-start | bytes 786440 | tf_op jit(solution)/shard_map/ppermute | solution.py:355
  32.3 0.0 collective-permute-done.9.refs_7_
  32.3 1.5 %collective-permute-start.10 = (bf16[4,144,128]{2,1,0:T(8,128)(2,1)S(1)}, bf16[4,144,128]{2,1,0:T(8,128)(2,1)S(1)}, u32[]{:S(2)}, u32[]{:S(2)}) collective-permute-start(bf16[4,144,128]{2,1,0:T(8,128)(2,1)S(1)} %collective-permute-done.9.refs_7_), channel_id=1, source_target_pairs={{0,16},{16,0},{1,17},{17,1},{2,18},{18,2},{3,19},{19,3},{4,20},{20... | collective-permute-start | bytes 442376 | tf_op jit(solution)/shard_map/ppermute | solution.py:358
  33.8 10.3 %collective-permute-done.8.refs_1_ = bf16[4,4,64,128]{3,2,1,0:T(8,128)(2,1)S(1)} collective-permute-done((bf16[4,4,64,128]{3,2,1,0:T(8,128)(2,1)S(1)}, bf16[4,4,64,128]{3,2,1,0:T(8,128)(2,1)S(1)}, u32[]{:S(2)}, u32[]{:S(2)}) %collective-permute-start.8) | collective-permute-done | bytes 262176 | tf_op jit(solution)/shard_map/ppermute | solution.py:355
  44.2 0.0 collective-permute-done.10.refs_8_
  44.2 0.4 shard_map.61
  44.6 0.1 collective-permute-start.11
  44.7 1.3 %shard_map.62.refs_2_ = bf16[32,256,128]{2,1,0:T(8,128)(2,1)} custom-call(bf16[1040,128]{1,0:T(8,128)(2,1)S(1)} %get-tuple-element.58.refs_0_, bf16[32,64,256]{2,1,0:T(8,128)(2,1)S(1)} %copy-done), custom_call_target="tpu_custom_call" | custom-call | flops 134217728 | bytes 2097152 | tf_op jit(solution)/shard_map/pallas_call | solution.py:329
  46.0 0.2 collective-permute-done.11.refs_0_
  46.2 1.3 %shard_map.63 = bf16[32,256,128]{2,1,0:T(8,128)(2,1)} custom-call(bf16[1040,128]{1,0:T(8,128)(2,1)S(1)} %collective-permute-done.11.refs_0_, bf16[32,64,256]{2,1,0:T(8,128)(2,1)S(1)} %copy-done, bf16[32,256,128]{2,1,0:T(8,128)(2,1)} %shard_map.62.refs_2_), custom_call_target="tpu_custom_call", output_to_operand_aliasing={{}: (2, {})} | custom-call | flops 134217728 | bytes 2097152 | tf_op jit(solution)/shard_map/pallas_call | solution.py:329
  (3 shorter events, 0.0 us)
Async XLA Ops:
  1.1 9.6 %collective-permute-start = (bf16[784,128]{1,0:T(8,128)(2,1)S(1)}, bf16[784,128]{1,0:T(8,128)(2,1)S(1)}, u32[]{:S(2)}, u32[]{:S(2)}) collective-permute-start(bf16[784,128]{1,0:T(8,128)(2,1)S(1)} %get-tuple-element.37), channel_id=1, source_target_pairs={{0,2},{1,3},{2,0},{3,1},{4,6},{5,7},{6,4},{7,5},{8,10},{9,11},{10,... | collective-permute-start | bytes 602120 | tf_op jit(solution)/shard_map/ppermute | solution.py:355
  4.2 7.9 %collective-permute-start.1 = (bf16[784,128]{1,0:T(8,128)(2,1)S(1)}, bf16[784,128]{1,0:T(8,128)(2,1)S(1)}, u32[]{:S(2)}, u32[]{:S(2)}) collective-permute-start(bf16[784,128]{1,0:T(8,128)(2,1)S(1)} %get-tuple-element.38), channel_id=1, source_target_pairs={{0,4},{1,5},{2,6},{3,7},{4,0},{5,1},{6,2},{7,3},{8,12},{9,13},{10,... | collective-permute-start | bytes 602120 | tf_op jit(solution)/shard_map/ppermute | solution.py:355
  5.7 9.0 %collective-permute-start.2 = (bf16[784,128]{1,0:T(8,128)(2,1)S(1)}, bf16[784,128]{1,0:T(8,128)(2,1)S(1)}, u32[]{:S(2)}, u32[]{:S(2)}) collective-permute-start(bf16[784,128]{1,0:T(8,128)(2,1)S(1)} %get-tuple-element.39), channel_id=1, source_target_pairs={{0,6},{1,7},{2,4},{3,5},{4,2},{5,3},{6,0},{7,1},{8,14},{9,15},{10,... | collective-permute-start | bytes 602120 | tf_op jit(solution)/shard_map/ppermute | solution.py:355
  14.7 1.9 %collective-permute-start.3 = (bf16[32,64,128]{2,1,0:T(8,128)(2,1)S(1)}, bf16[32,64,128]{2,1,0:T(8,128)(2,1)S(1)}, u32[]{:S(2)}, u32[]{:S(2)}) collective-permute-start(bf16[32,64,128]{2,1,0:T(8,128)(2,1)S(1)} %get-tuple-element.40.own_ref), channel_id=1, source_target_pairs={{0,1},{1,0},{2,3},{3,2},{4,5},{5,4},{6,7},{7,6},{8,9},{9,8},{10,11... | collective-permute-start | bytes 1572872 | tf_op jit(solution)/shard_map/ppermute | solution.py:355
  14.7 14.0 %collective-permute-start.7 = (bf16[3,656,128]{2,1,0:T(8,128)(2,1)S(1)}, bf16[3,656,128]{2,1,0:T(8,128)(2,1)S(1)}, u32[]{:S(2)}, u32[]{:S(2)}) collective-permute-start(bf16[3,656,128]{2,1,0:T(8,128)(2,1)S(1)} %shard_map.57), channel_id=1, source_target_pairs={{0,16},{16,0},{1,17},{17,1},{2,18},{18,2},{3,19},{19,3},{4,20},{20... | collective-permute-start | bytes 1511432 | tf_op jit(solution)/shard_map/ppermute | solution.py:358
  17.0 5.6 %collective-permute-start.4 = (bf16[4,2,64,128]{3,2,1,0:T(8,128)(2,1)S(1)}, bf16[4,2,64,128]{3,2,1,0:T(8,128)(2,1)S(1)}, u32[]{:S(2)}, u32[]{:S(2)}) collective-permute-start(bf16[4,2,64,128]{3,2,1,0:T(8,128)(2,1)S(1)} %get-tuple-element.47), channel_id=1, source_target_pairs={{0,2},{1,3},{2,0},{3,1},{4,6},{5,7},{6,4},{7,5},{8,10},{9,11},{10,... | collective-permute-start | bytes 393224 | tf_op jit(solution)/shard_map/ppermute | solution.py:355
  18.8 10.0 %collective-permute-start.5 = (bf16[4,2,64,128]{3,2,1,0:T(8,128)(2,1)S(1)}, bf16[4,2,64,128]{3,2,1,0:T(8,128)(2,1)S(1)}, u32[]{:S(2)}, u32[]{:S(2)}) collective-permute-start(bf16[4,2,64,128]{3,2,1,0:T(8,128)(2,1)S(1)} %get-tuple-element.48), channel_id=1, source_target_pairs={{0,4},{1,5},{2,6},{3,7},{4,0},{5,1},{6,2},{7,3},{8,12},{9,13},{10,... | collective-permute-start | bytes 393224 | tf_op jit(solution)/shard_map/ppermute | solution.py:355
  20.3 8.4 %collective-permute-start.6 = (bf16[4,2,64,128]{3,2,1,0:T(8,128)(2,1)S(1)}, bf16[4,2,64,128]{3,2,1,0:T(8,128)(2,1)S(1)}, u32[]{:S(2)}, u32[]{:S(2)}) collective-permute-start(bf16[4,2,64,128]{3,2,1,0:T(8,128)(2,1)S(1)} %get-tuple-element.49), channel_id=1, source_target_pairs={{0,6},{1,7},{2,4},{3,5},{4,2},{5,3},{6,0},{7,1},{8,14},{9,15},{10,... | collective-permute-start | bytes 393224 | tf_op jit(solution)/shard_map/ppermute | solution.py:355
  22.6 22.0 %copy-start = (bf16[32,64,256]{2,1,0:T(8,128)(2,1)S(1)}, bf16[32,64,256]{2,1,0:T(8,128)(2,1)}, u32[]{:S(2)}) copy-start(bf16[32,64,256]{2,1,0:T(8,128)(2,1)} %refs_1_.5) | copy-start | bytes 3145732
  22.7 9.7 %collective-permute-start.9 = (bf16[4,144,128]{2,1,0:T(8,128)(2,1)S(1)}, bf16[4,144,128]{2,1,0:T(8,128)(2,1)S(1)}, u32[]{:S(2)}, u32[]{:S(2)}) collective-permute-start(bf16[4,144,128]{2,1,0:T(8,128)(2,1)S(1)} %shard_map.60), channel_id=1, source_target_pairs={{0,8},{1,9},{2,10},{3,11},{4,12},{5,13},{6,14},{7,15},{8,0},{9,1},... | collective-permute-start | bytes 442376 | tf_op jit(solution)/shard_map/ppermute | solution.py:355
  29.5 14.6 %collective-permute-start.8 = (bf16[4,4,64,128]{3,2,1,0:T(8,128)(2,1)S(1)}, bf16[4,4,64,128]{3,2,1,0:T(8,128)(2,1)S(1)}, u32[]{:S(2)}, u32[]{:S(2)}) collective-permute-start(bf16[4,4,64,128]{3,2,1,0:T(8,128)(2,1)S(1)} %get-tuple-element.52), channel_id=1, source_target_pairs={{0,8},{1,9},{2,10},{3,11},{4,12},{5,13},{6,14},{7,15},{8,0},{9,1},... | collective-permute-start | bytes 786440 | tf_op jit(solution)/shard_map/ppermute | solution.py:355
  32.3 11.8 %collective-permute-start.10 = (bf16[4,144,128]{2,1,0:T(8,128)(2,1)S(1)}, bf16[4,144,128]{2,1,0:T(8,128)(2,1)S(1)}, u32[]{:S(2)}, u32[]{:S(2)}) collective-permute-start(bf16[4,144,128]{2,1,0:T(8,128)(2,1)S(1)} %collective-permute-done.9.refs_7_), channel_id=1, source_target_pairs={{0,16},{16,0},{1,17},{17,1},{2,18},{18,2},{3,19},{19,3},{4,20},{20... | collective-permute-start | bytes 442376 | tf_op jit(solution)/shard_map/ppermute | solution.py:358
  44.6 1.6 %collective-permute-start.11 = (bf16[1040,128]{1,0:T(8,128)(2,1)S(1)}, bf16[1040,128]{1,0:T(8,128)(2,1)S(1)}, u32[]{:S(2)}, u32[]{:S(2)}) collective-permute-start(bf16[1040,128]{1,0:T(8,128)(2,1)S(1)} %get-tuple-element.57), channel_id=1, source_target_pairs={{0,1},{1,0},{2,3},{3,2},{4,5},{5,4},{6,7},{7,6},{8,9},{9,8},{10,11... | collective-permute-start | bytes 798728 | tf_op jit(solution)/shard_map/ppermute | solution.py:355

commit v5 on v4

--- a/solution.py
+++ b/solution.py
@@ -154,16 +154,20 @@
         copy.wait()
 
 
-def gather_kernel(rank, near1, near2, near3, out_ref):
+def gather_kernel(rank, near1, near2, near3, pair_ref, stay_ref):
     for index, ref in enumerate((near1, near2, near3)):
-        out_ref[index, pl.ds(0, 10 * rank), :] = ref[pl.ds(0, 10 * rank), :]
-        out_ref[index, pl.ds(10 * rank, TILE), :] = ref[pl.ds(12 * rank, TILE), :]
+        pair_ref[index] = ref[pl.ds(0, 8 * rank), :]
+        stay_ref[index, pl.ds(0, 2 * rank), :] = ref[pl.ds(8 * rank, 2 * rank), :]
+        stay_ref[index, pl.ds(2 * rank, TILE), :] = ref[pl.ds(12 * rank, TILE), :]
 
 
 def late_kernel(rank, late_ref, near1, near2, near3, out_ref):
-    out_ref[0] = late_ref[...]
-    for index, ref in enumerate((near1, near2, near3)):
-        out_ref[index + 1] = ref[pl.ds(10 * rank, 2 * rank + TILE), :]
+    tile = []
+    for r, (ref, at) in enumerate(((late_ref, 0), (near1, 10), (near2, 10), (near3, 10))):
+        out_ref[pl.ds(2 * r * rank, 2 * rank), :] = ref[pl.ds(at * rank, 2 * rank), :]
+        tile.append(ref[pl.ds((at + 2) * rank, TILE), :].astype(jnp.float32)[2:4])
+    pad = jnp.zeros((TILE - 8, out_ref.shape[-1]), jnp.float32)
+    out_ref[pl.ds(8 * rank, TILE), :] = jnp.concatenate([*tile, pad], axis=0).astype(BF16)
 
 
 def local_kernel(
@@ -263,52 +267,76 @@
             out_ref[r, q] = product(matrix(r, h, i3, bit, 1), rows)
 
 
-def last_kernel(
-    rank, keep_ref, recv_ref, stay_ref, near1, near2, near3, far_ref, here_ref, cross_ref, own_ref, send_ref
-):
-    group, core = lax.axis_index("groups"), lax.axis_index("rhs")
+def last_matrices(rank, bit, stay_ref, near1, near2, near3, far_ref, here_ref, cross_ref):
+    group = lax.axis_index("groups")
 
     def source(side, r, h):
         if side:
-            return (here_ref, cross_ref)[h].at[r], 0, 2 * rank
+            return (here_ref, cross_ref)[h], 2 * r * rank, 8 * rank, 2 * r
         if r == 0:
-            return stay_ref.at[group ^ h], 0, 2 * rank
+            return stay_ref.at[group ^ h], 0, 2 * rank, 0
         if h:
-            return far_ref.at[r - 1], 8 * rank, 10 * rank
-        return (near1, near2, near3)[r - 1], 8 * rank, 12 * rank
-
-    for out_ref, bit in ((send_ref, 1 - core), (own_ref, core)):
-        tile = []
-        for side in range(2):
-            for r in range(4):
-                for h in range(2):
-                    ref, base, at = source(side, r, h)
-                    spots = ref[pl.ds(at, TILE), :].astype(jnp.float32)[2 * side : 2 * side + 2]
-                    tile.append(jnp.where(bit == 0, spots[0:1], spots[1:2]))
-                    q = (group ^ h) * 2 + bit
-                    sides = (keep_ref[r, q], recv_ref[r, q])
-                    rows = stacked(sides[side], sides[1 - side])
-                    start = pl.multiple_of(base + bit * rank, TILE)
-                    index = side * 8 + r * 2 + h
-                    out_ref[pl.ds(index * rank, rank), :] = product(ref[pl.ds(start, rank), :], rows)
-        out_ref[pl.ds(16 * rank, TILE), :] = jnp.concatenate(tile, axis=0).astype(BF16)
+            return far_ref.at[r - 1], 0, 2 * rank, 0
+        return (near1, near2, near3)[r - 1], 8 * rank, 12 * rank, 0
+
+    boxes = []
+    for side in range(2):
+        for r in range(4):
+            for h in range(2):
+                ref, base, tile, row = source(side, r, h)
+                spots = ref[pl.ds(tile, TILE), :].astype(jnp.float32)[row : row + 2]
+                matrix = ref[pl.ds(pl.multiple_of(base + bit * rank, TILE), rank), :]
+                boxes.append((side, r, h, matrix, jnp.where(bit == 0, spots[0:1], spots[1:2])))
+    return boxes
+
+
+def both_halves(side, r, q, keep_ref, recv_ref):
+    sides = (keep_ref[r, q], recv_ref[r, q])
+    return stacked(sides[side], sides[1 - side])
+
+
+def send_kernel(rank, keep_ref, recv_ref, *refs):
+    group, bit = lax.axis_index("groups"), 1 - lax.axis_index("rhs")
+    out_ref, tile = refs[-1], []
+    for index, (side, r, h, matrix, spot) in enumerate(last_matrices(rank, bit, *refs[:-1])):
+        rows = both_halves(side, r, (group ^ h) * 2 + bit, keep_ref, recv_ref)
+        out_ref[pl.ds(index * rank, rank), :] = product(matrix, rows)
+        tile.append(spot)
+    out_ref[pl.ds(16 * rank, TILE), :] = jnp.concatenate(tile, axis=0).astype(BF16)
+
+
+def write_rows(box, spot, slot, basis_ref, result, out_ref, sem):
+    result[slot] = lax.dot_general(
+        basis_ref[spot], box, (((0,), (0,)), ((), ())), preferred_element_type=jnp.float32
+    ).astype(BF16)
+    copy = pltpu.make_async_copy(result.at[slot], out_ref.at[spot], sem)
+    copy.start()
+    return copy
+
+
+def own_kernel(rank, keep_ref, recv_ref, *refs):
+    *matrix_refs, basis_ref, out_ref, result, sem, final = refs
+    group, bit = lax.axis_index("groups"), lax.axis_index("rhs")
+    copies = []
+    boxes = last_matrices(rank, bit, *matrix_refs)
+    spots = [jnp.max(spot).astype(jnp.int32) for *_, spot in boxes]
+    for slot, (side, r, h, matrix, _) in enumerate(boxes):
+        rows = both_halves(side, r, (group ^ h) * 2 + bit, keep_ref, recv_ref)
+        final[slot] = product(matrix, rows)
+    for slot, spot in enumerate(spots):
+        copies.append(write_rows(final[slot], spot, slot, basis_ref, result, out_ref, sem))
+    for copy in copies:
+        copy.wait()
 
 
 def output_kernel(rank, box_ref, basis_ref, *refs):
     out_ref, result, sem = refs[-3:]
-    spots = box_ref[pl.ds(16 * rank, TILE), :].astype(jnp.float32)
+    tile = box_ref[pl.ds(16 * rank, TILE), :].astype(jnp.float32)
+    spots = [jnp.max(tile[slot : slot + 1]).astype(jnp.int32) for slot in range(16)]
     copies = []
-    for index in range(16):
-        spot = jnp.max(spots[index : index + 1]).astype(jnp.int32)
-        result[index] = lax.dot_general(
-            basis_ref[spot],
-            box_ref[pl.ds(index * rank, rank), :],
-            (((0,), (0,)), ((), ())),
-            preferred_element_type=jnp.float32,
-        ).astype(BF16)
-        copy = pltpu.make_async_copy(result.at[index], out_ref.at[spot], sem)
-        copy.start()
-        copies.append(copy)
+    for slot in range(16):
+        box = box_ref[pl.ds(slot * rank, rank), :]
+        copies.append(write_rows(box, spots[slot], slot, basis_ref, result, out_ref, sem))
     for copy in copies:
         copy.wait()
 
@@ -401,7 +429,15 @@
     )
     coefficients, near = lax.optimization_barrier((coefficients, near))
     partner = across(coefficients, 1)
-    far = call(bind(gather_kernel, rank), shape(3, 10 * rank + TILE, width), (vmem,) * 3, vmem, [], 0, 2**20)(*near)
+    far, far_stay = call(
+        bind(gather_kernel, rank),
+        (shape(3, 8 * rank, width), shape(3, *part.shape)),
+        (vmem,) * 3,
+        (vmem,) * 2,
+        [],
+        0,
+        2**20,
+    )(*near)
     partner, _ = lax.optimization_barrier((partner, far))
     far = swapped(far)
     slots = call(
@@ -415,8 +451,9 @@
     )(coefficients, partner, chip_translations)
     slots = [slots[0]] + [across(slots[r], 2 * r) for r in (1, 2, 3)]
     _, late = lax.optimization_barrier((slots[1], late))
+    far_stay = swapped(far_stay)
     here = call(
-        bind(late_kernel, rank), shape(4, *part.shape), (vmem,) * 4, vmem, [], 0, 2**20
+        bind(late_kernel, rank), shape(8 * rank + TILE, width), (vmem,) * 4, vmem, [], 0, 2**20
     )(late, *near)
     here = across(here, 8)
     keep, send = call(
@@ -431,29 +468,39 @@
     received = across(send, 8)
     here, _ = lax.optimization_barrier((here, send))
     cross = swapped(here)
-    own, send = call(
-        bind(last_kernel, rank),
-        (shape(16 * rank + TILE, columns),) * 2,
+    basis = out_basis
+    matrices = (stay, *near, far_stay, here, cross)
+    send = call(
+        bind(send_kernel, rank),
+        shape(16 * rank + TILE, columns),
         (vmem,) * 9,
-        (vmem,) * 2,
+        vmem,
         [],
+        boxes * block * width // 2,
+        2**20,
+    )(keep, received, *matrices)
+    partner = across(send, 1)
+    rows = shape(boxes, leaf_rows, columns)
+    scratch = [vmem((16, leaf_rows, columns), BF16), dma]
+    applied = call(
+        bind(own_kernel, rank),
+        rows,
+        (vmem,) * 10,
+        hbm,
+        [*scratch, vmem((16, rank, columns), BF16)],
         boxes * block * width,
         2**21,
-    )(keep, received, stay, *near, far, here, cross)
-    partner = across(send, 1)
-    applied = None
-    for part in (own, partner):
-        before = () if applied is None else (applied,)
-        applied = call(
-            bind(output_kernel, rank),
-            shape(boxes, leaf_rows, columns),
-            (vmem, vmem) + (hbm,) * len(before),
-            hbm,
-            [vmem((16, leaf_rows, columns), BF16), dma],
-            boxes * block * width,
-            2**21,
-            {2: 0} if before else None,
-        )(part, out_basis, *before)
+    )(keep, received, *matrices, basis)
+    applied = call(
+        bind(output_kernel, rank),
+        rows,
+        (vmem, vmem, hbm),
+        hbm,
+        scratch,
+        boxes * block * width,
+        2**21,
+        {2: 0},
+    )(partner, basis, applied)
     return applied.reshape(boxes * leaf_rows, columns)
 
 

time: 47.7 us -> 47.2 us (0.990)
  the two profiles are of different devices: /device:TPU:0 before, /device:TPU:31 now
where the time goes in v5:
time: 47.2 us; the launch traced here: 47.1 us
  waiting for transfers between devices  25.6 us (54%)
  starting transfers between devices  11 us (23%)
  Pallas kernels  10.4 us (22%)
    ppermute x10, waiting for transfers between devices, across(): return lax.ppermute(value, AXES, [(s, s ^ mask) for s in range(16)])  16.3 us
    pallas_call x9, Pallas kernels, placed(): run(*(pltpu.with_memory_space_constraint(operand, space) if space == pltp...  10.4 us
    ppermute x3, waiting for transfers between devices, swapped(): return lax.ppermute(value, 'groups', [(0, 1), (1, 0)])  9.25 us
    ppermute x10, starting transfers between devices, across(): return lax.ppermute(value, AXES, [(s, s ^ mask) for s in range(16)])  9.25 us
    ppermute x3, starting transfers between devices, swapped(): return lax.ppermute(value, 'groups', [(0, 1), (1, 0)])  1.79 us
  transfers between devices with their start and end apart: 13, of which 6 were waited for; matrix products, arithmetic and copies ran while one was open for 0% of the time, Pallas kernels for 16%

profile of v5, /device:TPU:31, one launch (start us, length us, event | category | flops | bytes accessed | tf_op | source)
XLA Modules:
  0.0 47.1 jit_solution(8925280256616733089)
XLA Ops:
  0.0 1.1 %shard_map.55 = (bf16[784,128]{1,0:T(8,128)(2,1)S(1)}, bf16[784,128]{1,0:T(8,128)(2,1)S(1)}, bf16[784,128]{1,0:T(8,128)(2,1)S(1)}) custom-call(s32[32]{0:T(128)} %refs_4_.1, bf16[2,2,2,2,2,576,128]{6,5,4,3,2,1,0:T(8,128)(2,1)} %bitcast.3), custom_call_target="tpu_custom_call" | custom-call | bytes 1048576 | tf_op jit(solution)/shard_map/pallas_call | solution.py:357
  1.1 0.3 collective-permute-start
  1.4 0.2 collective-permute-start.1
  1.6 2.3 %collective-permute-start.2 = (bf16[784,128]{1,0:T(8,128)(2,1)S(1)}, bf16[784,128]{1,0:T(8,128)(2,1)S(1)}, u32[]{:S(2)}, u32[]{:S(2)}) collective-permute-start(bf16[784,128]{1,0:T(8,128)(2,1)S(1)} %get-tuple-element.39), channel_id=1, source_target_pairs={{0,6},{1,7},{2,4},{3,5},{4,2},{5,3},{6,0},{7,1},{8,14},{9,15},{10,... | collective-permute-start | bytes 602120 | tf_op jit(solution)/shard_map/ppermute | solution.py:383
  3.8 5.0 %shard_map.56 = (bf16[32,64,128]{2,1,0:T(8,128)(2,1)S(1)}, bf16[32,64,128]{2,1,0:T(8,128)(2,1)S(1)}, bf16[2,2,2,128,128]{4,3,2,1,0:T(8,128)(2,1)S(1)}, bf16[2,14...) custom-call(bf16[32,256,128]{2,1,0:T(8,128)(2,1)} %bitcast.5, bf16[32,64,256]{2,1,0:T(8,128)(2,1)} %refs_1_.2, ...), custom_call_target="tpu_custom_call" | custom-call | flops 469762048 | bytes 6291456 | tf_op jit(solution)/shard_map/pallas_call | solution.py:357
  8.9 0.0 collective-permute-done.refs_0_.refs_5_.refs_1_.refs_3_
  8.9 0.0 collective-permute-done.1.refs_1_.refs_6_.refs_2_.refs_4_
  8.9 3.3 %collective-permute-done.2.refs_2_.refs_7_.refs_3_.refs_5_ = bf16[784,128]{1,0:T(8,128)(2,1)S(1)} collective-permute-done((bf16[784,128]{1,0:T(8,128)(2,1)S(1)}, bf16[784,128]{1,0:T(8,128)(2,1)S(1)}, u32[]{:S(2)}, u32[]{:S(2)}) %collective-permute-start.2) | collective-permute-done | bytes 200736 | tf_op jit(solution)/shard_map/ppermute | solution.py:383
  12.2 1.9 %collective-permute-start.3 = (bf16[32,64,128]{2,1,0:T(8,128)(2,1)S(1)}, bf16[32,64,128]{2,1,0:T(8,128)(2,1)S(1)}, u32[]{:S(2)}, u32[]{:S(2)}) collective-permute-start(bf16[32,64,128]{2,1,0:T(8,128)(2,1)S(1)} %get-tuple-element.40.own_ref), channel_id=1, source_target_pairs={{0,1},{1,0},{2,3},{3,2},{4,5},{5,4},{6,7},{7,6},{8,9},{9,8},{10,11... | collective-permute-start | bytes 1572872 | tf_op jit(solution)/shard_map/ppermute | solution.py:383
  14.1 0.3 collective-permute-start.7
  14.4 1.2 %collective-permute-done.3.other_ref = bf16[32,64,128]{2,1,0:T(8,128)(2,1)S(1)} collective-permute-done((bf16[32,64,128]{2,1,0:T(8,128)(2,1)S(1)}, bf16[32,64,128]{2,1,0:T(8,128)(2,1)S(1)}, u32[]{:S(2)}, u32[]{:S(2)}) %collective-permute-start.3) | collective-permute-done | bytes 524320 | tf_op jit(solution)/shard_map/ppermute | solution.py:383
  15.6 0.4 shard_map.58
  16.0 0.3 collective-permute-start.4
  16.3 0.2 collective-permute-start.5
  16.5 2.3 %collective-permute-start.6 = (bf16[4,2,64,128]{3,2,1,0:T(8,128)(2,1)S(1)}, bf16[4,2,64,128]{3,2,1,0:T(8,128)(2,1)S(1)}, u32[]{:S(2)}, u32[]{:S(2)}) collective-permute-start(bf16[4,2,64,128]{3,2,1,0:T(8,128)(2,1)S(1)} %get-tuple-element.50), channel_id=1, source_target_pairs={{0,6},{1,7},{2,4},{3,5},{4,2},{5,3},{6,0},{7,1},{8,14},{9,15},{10,... | collective-permute-start | bytes 393224 | tf_op jit(solution)/shard_map/ppermute | solution.py:383
  18.7 2.1 %collective-permute-done.4.refs_1_ = bf16[4,2,64,128]{3,2,1,0:T(8,128)(2,1)S(1)} collective-permute-done((bf16[4,2,64,128]{3,2,1,0:T(8,128)(2,1)S(1)}, bf16[4,2,64,128]{3,2,1,0:T(8,128)(2,1)S(1)}, u32[]{:S(2)}, u32[]{:S(2)}) %collective-permute-start.4) | collective-permute-done | bytes 131104 | tf_op jit(solution)/shard_map/ppermute | solution.py:383
  20.8 0.1 collective-permute-start.10
  20.9 4.0 %collective-permute-done.7.refs_8_ = bf16[3,512,128]{2,1,0:T(8,128)(2,1)S(1)} collective-permute-done((bf16[3,512,128]{2,1,0:T(8,128)(2,1)S(1)}, bf16[3,512,128]{2,1,0:T(8,128)(2,1)S(1)}, u32[]{:S(2)}, u32[]{:S(2)}) %collective-permute-start.7) | collective-permute-done | bytes 393248 | tf_op jit(solution)/shard_map/ppermute | solution.py:386
  24.9 0.0 collective-permute-done.5.refs_2_
  24.9 0.0 collective-permute-done.6.refs_3_
  24.9 0.8 %shard_map.59 = (bf16[4,4,64,128]{3,2,1,0:T(8,128)(2,1)S(1)}, bf16[4,4,64,128]{3,2,1,0:T(8,128)(2,1)S(1)}) custom-call(bf16[4,2,64,128]{3,2,1,0:T(8,128)(2,1)S(1)} %get-tuple-element.47.refs_0_, bf16[4,2,64,128]{3,2,1,0:T(8,128)(2,1)S(1)} %collective-permute-done.4.refs_1_, bf16[4,2,64,128]{3,2,1,0:T(8,128)(2,1)S(1)} %collective-permute-done.5.refs_2_, ...), custom_call_target="tpu_custom_call" | custom-call | flops 268435456 | bytes 2097152 | tf_op jit(solution)/shard_map/pallas_call | solution.py:357
  25.8 0.1 collective-permute-start.8
  25.9 9.8 %collective-permute-done.10.refs_7_ = bf16[528,128]{1,0:T(8,128)(2,1)S(1)} collective-permute-done((bf16[528,128]{1,0:T(8,128)(2,1)S(1)}, bf16[528,128]{1,0:T(8,128)(2,1)S(1)}, u32[]{:S(2)}, u32[]{:S(2)}) %collective-permute-start.10) | collective-permute-done | bytes 135200 | tf_op jit(solution)/shard_map/ppermute | solution.py:383
  35.7 0.3 collective-permute-start.11
  35.9 1.2 %collective-permute-start.9 = (bf16[3,144,128]{2,1,0:T(8,128)(2,1)S(1)}, bf16[3,144,128]{2,1,0:T(8,128)(2,1)S(1)}, u32[]{:S(2)}, u32[]{:S(2)}) collective-permute-start(bf16[3,144,128]{2,1,0:T(8,128)(2,1)S(1)} %get-tuple-element.55), channel_id=1, source_target_pairs={{0,16},{16,0},{1,17},{17,1},{2,18},{18,2},{3,19},{19,3},{4,20},{20... | collective-permute-start | bytes 331784 | tf_op jit(solution)/shard_map/ppermute | solution.py:386
  37.1 5.3 %collective-permute-done.9.refs_6_ = bf16[3,144,128]{2,1,0:T(8,128)(2,1)S(1)} collective-permute-done((bf16[3,144,128]{2,1,0:T(8,128)(2,1)S(1)}, bf16[3,144,128]{2,1,0:T(8,128)(2,1)S(1)}, u32[]{:S(2)}, u32[]{:S(2)}) %collective-permute-start.9) | collective-permute-done | bytes 110624 | tf_op jit(solution)/shard_map/ppermute | solution.py:386
  42.4 0.0 collective-permute-done.8.refs_1_
  42.4 0.0 collective-permute-done.11.refs_8_
  42.4 0.3 shard_map.61
  42.7 1.7 %collective-permute-start.12 = (bf16[1040,128]{1,0:T(8,128)(2,1)S(1)}, bf16[1040,128]{1,0:T(8,128)(2,1)S(1)}, u32[]{:S(2)}, u32[]{:S(2)}) collective-permute-start(bf16[1040,128]{1,0:T(8,128)(2,1)S(1)} %shard_map.61), channel_id=1, source_target_pairs={{0,1},{1,0},{2,3},{3,2},{4,5},{5,4},{6,7},{7,6},{8,9},{9,8},{10,11... | collective-permute-start | bytes 798728 | tf_op jit(solution)/shard_map/ppermute | solution.py:383
  44.4 1.4 %shard_map.62.refs_2_ = bf16[32,256,128]{2,1,0:T(8,128)(2,1)} custom-call(bf16[4,4,64,128]{3,2,1,0:T(8,128)(2,1)S(1)} %get-tuple-element.52.refs_0_, bf16[4,4,64,128]{3,2,1,0:T(8,128)(2,1)S(1)} %collective-permute-done.8.refs_1_, bf16[2,144,128]{2,1,0:T(8,128)(2,1)S(1)} %get-tuple-element.54.refs_2_, ...), custom_call_target="tpu_custom_call" | custom-call | flops 134217728 | bytes 2097152 | tf_op jit(solution)/shard_map/pallas_call | solution.py:357
  45.8 1.3 %shard_map.63 = bf16[32,256,128]{2,1,0:T(8,128)(2,1)} custom-call(bf16[1040,128]{1,0:T(8,128)(2,1)S(1)} %collective-permute-done.12.refs_0_, bf16[32,64,256]{2,1,0:T(8,128)(2,1)S(1)} %copy-done, bf16[32,256,128]{2,1,0:T(8,128)(2,1)} %shard_map.62.refs_2_), custom_call_target="tpu_custom_call", output_to_operand_aliasing={{}: (2, {})} | custom-call | flops 134217728 | bytes 2097152 | tf_op jit(solution)/shard_map/pallas_call | solution.py:357
  (5 shorter events, 0.1 us)
Async XLA Ops:
  1.1 7.8 %collective-permute-start = (bf16[784,128]{1,0:T(8,128)(2,1)S(1)}, bf16[784,128]{1,0:T(8,128)(2,1)S(1)}, u32[]{:S(2)}, u32[]{:S(2)}) collective-permute-start(bf16[784,128]{1,0:T(8,128)(2,1)S(1)} %get-tuple-element.37), channel_id=1, source_target_pairs={{0,2},{1,3},{2,0},{3,1},{4,6},{5,7},{6,4},{7,5},{8,10},{9,11},{10,... | collective-permute-start | bytes 602120 | tf_op jit(solution)/shard_map/ppermute | solution.py:383
  1.4 7.5 %collective-permute-start.1 = (bf16[784,128]{1,0:T(8,128)(2,1)S(1)}, bf16[784,128]{1,0:T(8,128)(2,1)S(1)}, u32[]{:S(2)}, u32[]{:S(2)}) collective-permute-start(bf16[784,128]{1,0:T(8,128)(2,1)S(1)} %get-tuple-element.38), channel_id=1, source_target_pairs={{0,4},{1,5},{2,6},{3,7},{4,0},{5,1},{6,2},{7,3},{8,12},{9,13},{10,... | collective-permute-start | bytes 602120 | tf_op jit(solution)/shard_map/ppermute | solution.py:383
  1.6 10.6 %collective-permute-start.2 = (bf16[784,128]{1,0:T(8,128)(2,1)S(1)}, bf16[784,128]{1,0:T(8,128)(2,1)S(1)}, u32[]{:S(2)}, u32[]{:S(2)}) collective-permute-start(bf16[784,128]{1,0:T(8,128)(2,1)S(1)} %get-tuple-element.39), channel_id=1, source_target_pairs={{0,6},{1,7},{2,4},{3,5},{4,2},{5,3},{6,0},{7,1},{8,14},{9,15},{10,... | collective-permute-start | bytes 602120 | tf_op jit(solution)/shard_map/ppermute | solution.py:383
  12.2 3.4 %collective-permute-start.3 = (bf16[32,64,128]{2,1,0:T(8,128)(2,1)S(1)}, bf16[32,64,128]{2,1,0:T(8,128)(2,1)S(1)}, u32[]{:S(2)}, u32[]{:S(2)}) collective-permute-start(bf16[32,64,128]{2,1,0:T(8,128)(2,1)S(1)} %get-tuple-element.40.own_ref), channel_id=1, source_target_pairs={{0,1},{1,0},{2,3},{3,2},{4,5},{5,4},{6,7},{7,6},{8,9},{9,8},{10,11... | collective-permute-start | bytes 1572872 | tf_op jit(solution)/shard_map/ppermute | solution.py:383
  14.1 10.8 %collective-permute-start.7 = (bf16[3,512,128]{2,1,0:T(8,128)(2,1)S(1)}, bf16[3,512,128]{2,1,0:T(8,128)(2,1)S(1)}, u32[]{:S(2)}, u32[]{:S(2)}) collective-permute-start(bf16[3,512,128]{2,1,0:T(8,128)(2,1)S(1)} %get-tuple-element.44), channel_id=1, source_target_pairs={{0,16},{16,0},{1,17},{17,1},{2,18},{18,2},{3,19},{19,3},{4,20},{20... | collective-permute-start | bytes 1179656 | tf_op jit(solution)/shard_map/ppermute | solution.py:386
  16.0 4.8 %collective-permute-start.4 = (bf16[4,2,64,128]{3,2,1,0:T(8,128)(2,1)S(1)}, bf16[4,2,64,128]{3,2,1,0:T(8,128)(2,1)S(1)}, u32[]{:S(2)}, u32[]{:S(2)}) collective-permute-start(bf16[4,2,64,128]{3,2,1,0:T(8,128)(2,1)S(1)} %get-tuple-element.48), channel_id=1, source_target_pairs={{0,2},{1,3},{2,0},{3,1},{4,6},{5,7},{6,4},{7,5},{8,10},{9,11},{10,... | collective-permute-start | bytes 393224 | tf_op jit(solution)/shard_map/ppermute | solution.py:383
  16.3 8.6 %collective-permute-start.5 = (bf16[4,2,64,128]{3,2,1,0:T(8,128)(2,1)S(1)}, bf16[4,2,64,128]{3,2,1,0:T(8,128)(2,1)S(1)}, u32[]{:S(2)}, u32[]{:S(2)}) collective-permute-start(bf16[4,2,64,128]{3,2,1,0:T(8,128)(2,1)S(1)} %get-tuple-element.49), channel_id=1, source_target_pairs={{0,4},{1,5},{2,6},{3,7},{4,0},{5,1},{6,2},{7,3},{8,12},{9,13},{10,... | collective-permute-start | bytes 393224 | tf_op jit(solution)/shard_map/ppermute | solution.py:383
  16.5 8.4 %collective-permute-start.6 = (bf16[4,2,64,128]{3,2,1,0:T(8,128)(2,1)S(1)}, bf16[4,2,64,128]{3,2,1,0:T(8,128)(2,1)S(1)}, u32[]{:S(2)}, u32[]{:S(2)}) collective-permute-start(bf16[4,2,64,128]{3,2,1,0:T(8,128)(2,1)S(1)} %get-tuple-element.50), channel_id=1, source_target_pairs={{0,6},{1,7},{2,4},{3,5},{4,2},{5,3},{6,0},{7,1},{8,14},{9,15},{10,... | collective-permute-start | bytes 393224 | tf_op jit(solution)/shard_map/ppermute | solution.py:383
  20.8 23.6 %copy-start = (bf16[32,64,256]{2,1,0:T(8,128)(2,1)S(1)}, bf16[32,64,256]{2,1,0:T(8,128)(2,1)}, u32[]{:S(2)}) copy-start(bf16[32,64,256]{2,1,0:T(8,128)(2,1)} %refs_1_.3) | copy-start | bytes 3145732
  20.8 14.8 %collective-permute-start.10 = (bf16[528,128]{1,0:T(8,128)(2,1)S(1)}, bf16[528,128]{1,0:T(8,128)(2,1)S(1)}, u32[]{:S(2)}, u32[]{:S(2)}) collective-permute-start(bf16[528,128]{1,0:T(8,128)(2,1)S(1)} %shard_map.60), channel_id=1, source_target_pairs={{0,8},{1,9},{2,10},{3,11},{4,12},{5,13},{6,14},{7,15},{8,0},{9,1},... | collective-permute-start | bytes 405512 | tf_op jit(solution)/shard_map/ppermute | solution.py:383
  25.8 16.6 %collective-permute-start.8 = (bf16[4,4,64,128]{3,2,1,0:T(8,128)(2,1)S(1)}, bf16[4,4,64,128]{3,2,1,0:T(8,128)(2,1)S(1)}, u32[]{:S(2)}, u32[]{:S(2)}) collective-permute-start(bf16[4,4,64,128]{3,2,1,0:T(8,128)(2,1)S(1)} %get-tuple-element.53), channel_id=1, source_target_pairs={{0,8},{1,9},{2,10},{3,11},{4,12},{5,13},{6,14},{7,15},{8,0},{9,1},... | collective-permute-start | bytes 786440 | tf_op jit(solution)/shard_map/ppermute | solution.py:383
  35.7 6.7 %collective-permute-start.11 = (bf16[528,128]{1,0:T(8,128)(2,1)S(1)}, bf16[528,128]{1,0:T(8,128)(2,1)S(1)}, u32[]{:S(2)}, u32[]{:S(2)}) collective-permute-start(bf16[528,128]{1,0:T(8,128)(2,1)S(1)} %collective-permute-done.10.refs_7_), channel_id=1, source_target_pairs={{0,16},{16,0},{1,17},{17,1},{2,18},{18,2},{3,19},{19,3},{4,20},{20... | collective-permute-start | bytes 405512 | tf_op jit(solution)/shard_map/ppermute | solution.py:386
  35.9 6.5 %collective-permute-start.9 = (bf16[3,144,128]{2,1,0:T(8,128)(2,1)S(1)}, bf16[3,144,128]{2,1,0:T(8,128)(2,1)S(1)}, u32[]{:S(2)}, u32[]{:S(2)}) collective-permute-start(bf16[3,144,128]{2,1,0:T(8,128)(2,1)S(1)} %get-tuple-element.55), channel_id=1, source_target_pairs={{0,16},{16,0},{1,17},{17,1},{2,18},{18,2},{3,19},{19,3},{4,20},{20... | collective-permute-start | bytes 331784 | tf_op jit(solution)/shard_map/ppermute | solution.py:386
  42.7 3.1 %collective-permute-start.12 = (bf16[1040,128]{1,0:T(8,128)(2,1)S(1)}, bf16[1040,128]{1,0:T(8,128)(2,1)S(1)}, u32[]{:S(2)}, u32[]{:S(2)}) collective-permute-start(bf16[1040,128]{1,0:T(8,128)(2,1)S(1)} %shard_map.61), channel_id=1, source_target_pairs={{0,1},{1,0},{2,3},{3,2},{4,5},{5,4},{6,7},{7,6},{8,9},{9,8},{10,11... | collective-permute-start | bytes 798728 | tf_op jit(solution)/shard_map/ppermute | solution.py:383

commit v6 on v5

--- a/solution.py
+++ b/solution.py
@@ -123,14 +123,17 @@
     return level_rows(trans_ref, rank, i4, own_place() ^ r, own_half() ^ side, 8, 1), slots
 
 
-def spot_tile(target, i4, r, columns):
+def spot_tile(target, boxes, columns):
     row = lax.broadcasted_iota(jnp.int32, (TILE, columns), 0)
-    base = i4 * 16 + first_box(own_place() ^ r)
-    half = own_half()
-    spots = [target[base + (half ^ side) + i3 * 8] % 32 for side in range(2) for i3 in range(2)]
-    upper = jnp.where(row == 2, spots[2], spots[3])
-    tile = jnp.where(row < 2, jnp.where(row == 0, spots[0], spots[1]), upper)
+    tile = target[boxes[-1]] % 32
+    for index, box in enumerate(boxes[:-1]):
+        tile = jnp.where(row == index, target[box] % 32, tile)
     return tile.astype(jnp.float32).astype(BF16)
+
+
+def late_tile(target, i4, r, columns):
+    base = i4 * 16 + first_box(own_place() ^ r) + 1 - own_half()
+    return spot_tile(target, (base, base + 8), columns)
 
 
 def pack_kernel(rank, target_ref, trans_ref, *refs):
@@ -143,35 +146,31 @@
         ref = out_refs[r - 1]
         slots = ref.at[pl.ds(0, 8 * rank)].reshape(2, 2, 2 * rank, columns)
         pairs.append((level_rows(trans_ref, rank, group, own_place() ^ r, BOTH, 6, 2), slots))
-        for side in range(2):
-            rows = ref.at[pl.ds((8 + 2 * side) * rank, 2 * rank)]
-            pairs.append(last_level(rank, trans_ref, group, r, side, rows))
+        pairs.append(last_level(rank, trans_ref, group, r, 1, ref.at[pl.ds(8 * rank, 2 * rank)]))
     copies = start_all(pairs, sem)
     target_copy.wait()
     for r in (3, 2, 1):
-        out_refs[r - 1][pl.ds(12 * rank, TILE), :] = spot_tile(target, group, r, columns)
+        out_refs[r - 1][pl.ds(10 * rank, TILE), :] = late_tile(target, group, r, columns)
     for copy in copies:
         copy.wait()
 
 
-def gather_kernel(rank, near1, near2, near3, pair_ref, stay_ref):
+def gather_kernel(rank, near1, near2, near3, out_ref):
     for index, ref in enumerate((near1, near2, near3)):
-        pair_ref[index] = ref[pl.ds(0, 8 * rank), :]
-        stay_ref[index, pl.ds(0, 2 * rank), :] = ref[pl.ds(8 * rank, 2 * rank), :]
-        stay_ref[index, pl.ds(2 * rank, TILE), :] = ref[pl.ds(12 * rank, TILE), :]
+        out_ref[index] = ref[pl.ds(0, 8 * rank), :]
 
 
 def late_kernel(rank, late_ref, near1, near2, near3, out_ref):
     tile = []
-    for r, (ref, at) in enumerate(((late_ref, 0), (near1, 10), (near2, 10), (near3, 10))):
+    for r, (ref, at) in enumerate(((late_ref, 0), (near1, 8), (near2, 8), (near3, 8))):
         out_ref[pl.ds(2 * r * rank, 2 * rank), :] = ref[pl.ds(at * rank, 2 * rank), :]
-        tile.append(ref[pl.ds((at + 2) * rank, TILE), :].astype(jnp.float32)[2:4])
+        tile.append(ref[pl.ds((at + 2) * rank, TILE), :].astype(jnp.float32)[0:2])
     pad = jnp.zeros((TILE - 8, out_ref.shape[-1]), jnp.float32)
     out_ref[pl.ds(8 * rank, TILE), :] = jnp.concatenate([*tile, pad], axis=0).astype(BF16)
 
 
 def local_kernel(
-    levels, rs_ref, leaf_ref, trans_ref, grid_ref, target_ref, out_ref, next_ref, pair_ref, stay_ref, late_ref,
+    levels, rs_ref, leaf_ref, trans_ref, grid_ref, target_ref, out_ref, next_ref, pair_ref, stay0, stay1, stay2, stay3, late_ref,
     rs, leaf, trans, ping, pong, target_smem, sem, trans_sem, rest_sem, target_sem
 ):
     rank = leaf_ref.shape[1]
@@ -203,14 +202,19 @@
     group, columns = lax.axis_index("groups"), grid_ref.shape[-1]
     rest = [(level_rows(grid_ref, rank, BOTH, own_place(), BOTH, 6, 2), pair_ref)]
     two = pl.ds(0, 2 * rank)
-    rest += [last_level(rank, grid_ref, i4, 0, 0, stay_ref.at[i4, two]) for i4 in range(2)]
+    stay_refs = (stay0, stay1, stay2, stay3)
+    for r, ref in enumerate(stay_refs):
+        for i4 in range(2):
+            rows = ref.at[pl.ds(2 * i4 * rank, 2 * rank)]
+            rest.append(last_level(rank, grid_ref, i4, r, 0, rows))
     rest.append(last_level(rank, grid_ref, group, 0, 1, late_ref.at[two]))
     rest = start_all(rest, rest_sem)
     target_copy.wait()
-    tile = pl.ds(2 * rank, TILE)
-    for i4 in range(2):
-        stay_ref[i4, tile, :] = spot_tile(target_smem, i4, 0, columns)
-    late_ref[tile, :] = spot_tile(target_smem, group, 0, columns)
+    for r, ref in enumerate(stay_refs):
+        base = first_box(own_place() ^ r) + own_half()
+        spots = [base + q * 8 for q in range(4)]
+        ref[pl.ds(4 * rank, TILE), :] = spot_tile(target_smem, spots, columns)
+    late_ref[pl.ds(2 * rank, TILE), :] = late_tile(target_smem, group, 0, columns)
     for part in range(4):
         for copy in loads[part]:
             copy.wait()
@@ -267,25 +271,23 @@
             out_ref[r, q] = product(matrix(r, h, i3, bit, 1), rows)
 
 
-def last_matrices(rank, bit, stay_ref, near1, near2, near3, far_ref, here_ref, cross_ref):
+def last_matrices(rank, bit, stay0, stay1, stay2, stay3, here_ref, cross_ref):
     group = lax.axis_index("groups")
 
     def source(side, r, h):
         if side:
-            return (here_ref, cross_ref)[h], 2 * r * rank, 8 * rank, 2 * r
-        if r == 0:
-            return stay_ref.at[group ^ h], 0, 2 * rank, 0
-        if h:
-            return far_ref.at[r - 1], 0, 2 * rank, 0
-        return (near1, near2, near3)[r - 1], 8 * rank, 12 * rank, 0
+            return (here_ref, cross_ref)[h], 2 * r, 8 * rank, 2 * r, 2 * r
+        i4 = group ^ h
+        return (stay0, stay1, stay2, stay3)[r], 2 * i4, 4 * rank, i4, None
 
     boxes = []
     for side in range(2):
         for r in range(4):
             for h in range(2):
-                ref, base, tile, row = source(side, r, h)
-                spots = ref[pl.ds(tile, TILE), :].astype(jnp.float32)[row : row + 2]
-                matrix = ref[pl.ds(pl.multiple_of(base + bit * rank, TILE), rank), :]
+                ref, first, tile, i4, row = source(side, r, h)
+                spots = ref[pl.ds(tile, TILE), :].astype(jnp.float32)
+                spots = jnp.where(i4 == 0, spots[0:2], spots[2:4]) if row is None else spots[row : row + 2]
+                matrix = ref[pl.ds(pl.multiple_of((first + bit) * rank, TILE), rank), :]
                 boxes.append((side, r, h, matrix, jnp.where(bit == 0, spots[0:1], spots[1:2])))
     return boxes
 
@@ -387,7 +389,8 @@
 
     grid = translations.reshape(2, 2, 2, 2, 2, -1, width)
     part = shape(2 * rank + TILE, width)
-    near_part = shape(12 * rank + TILE, width)
+    near_part = shape(10 * rank + TILE, width)
+    stay_part = shape(4 * rank + TILE, width)
     near = call(
         bind(pack_kernel, rank),
         (near_part,) * 3,
@@ -399,17 +402,17 @@
     )(node_target, grid)
     right_sides, near = lax.optimization_barrier((right_sides, near))
     near = [across(near[r - 1], 2 * r) for r in (1, 2, 3)]
-    coefficients, chip_translations, own_pair, stay, late = call(
+    coefficients, chip_translations, own_pair, *stay, late = call(
         bind(local_kernel, local_levels),
         (
             shape(boxes, rank, columns),
             shape(boxes, rank, width),
             shape(2, 2, 2, 2 * rank, width),
-            shape(2, *part.shape),
-            part,
-        ),
+        )
+        + (stay_part,) * 4
+        + (part,),
         (hbm,) * 5,
-        (vmem,) * 5,
+        (vmem,) * 8,
         [
             vmem((boxes, leaf_rows, columns), BF16),
             vmem((boxes, rank, leaf_rows), BF16),
@@ -429,15 +432,7 @@
     )
     coefficients, near = lax.optimization_barrier((coefficients, near))
     partner = across(coefficients, 1)
-    far, far_stay = call(
-        bind(gather_kernel, rank),
-        (shape(3, 8 * rank, width), shape(3, *part.shape)),
-        (vmem,) * 3,
-        (vmem,) * 2,
-        [],
-        0,
-        2**20,
-    )(*near)
+    far = call(bind(gather_kernel, rank), shape(3, 8 * rank, width), (vmem,) * 3, vmem, [], 0, 2**20)(*near)
     partner, _ = lax.optimization_barrier((partner, far))
     far = swapped(far)
     slots = call(
@@ -451,7 +446,6 @@
     )(coefficients, partner, chip_translations)
     slots = [slots[0]] + [across(slots[r], 2 * r) for r in (1, 2, 3)]
     _, late = lax.optimization_barrier((slots[1], late))
-    far_stay = swapped(far_stay)
     here = call(
         bind(late_kernel, rank), shape(8 * rank + TILE, width), (vmem,) * 4, vmem, [], 0, 2**20
     )(late, *near)
@@ -466,14 +460,16 @@
         2**21,
     )(*slots, own_pair, *near, far)
     received = across(send, 8)
-    here, _ = lax.optimization_barrier((here, send))
+    stay, _ = lax.optimization_barrier((stay, send))
+    stay = [stay[0]] + [across(stay[r], 2 * r) for r in (1, 2, 3)]
+    here, stay[1], stay[2], stay[3] = lax.optimization_barrier((here, stay[1], stay[2], stay[3]))
     cross = swapped(here)
     basis = out_basis
-    matrices = (stay, *near, far_stay, here, cross)
+    matrices = (*stay, here, cross)
     send = call(
         bind(send_kernel, rank),
         shape(16 * rank + TILE, columns),
-        (vmem,) * 9,
+        (vmem,) * 8,
         vmem,
         [],
         boxes * block * width // 2,
@@ -485,7 +481,7 @@
     applied = call(
         bind(own_kernel, rank),
         rows,
-        (vmem,) * 10,
+        (vmem,) * 9,
         hbm,
         [*scratch, vmem((16, rank, columns), BF16)],
         boxes * block * width,

time: 47.2 us -> 46.6 us (0.987)
  the two profiles are of different devices: /device:TPU:31 before, /device:TPU:0 now
where the time goes in v6:
time: 46.6 us; the launch traced here: 46.4 us
  starting transfers between devices  21.1 us (45%)
  waiting for transfers between devices  14.9 us (32%)
  Pallas kernels  10.3 us (22%)
    ppermute x13, starting transfers between devices, across(): return lax.ppermute(value, AXES, [(s, s ^ mask) for s in range(16)])  17.9 us
    ppermute x13, waiting for transfers between devices, across(): return lax.ppermute(value, AXES, [(s, s ^ mask) for s in range(16)])  12.3 us
    pallas_call x9, Pallas kernels, placed(): run(*(pltpu.with_memory_space_constraint(operand, space) if space == pltp...  10.3 us
    ppermute x2, starting transfers between devices, swapped(): return lax.ppermute(value, 'groups', [(0, 1), (1, 0)])  3.19 us
    ppermute x2, waiting for transfers between devices, swapped(): return lax.ppermute(value, 'groups', [(0, 1), (1, 0)])  2.52 us
  transfers between devices with their start and end apart: 15, of which 12 were waited for; matrix products, arithmetic and copies ran while one was open for 0% of the time, Pallas kernels for 17%

profile of v6, /device:TPU:0, one launch (start us, length us, event | category | flops | bytes accessed | tf_op | source)
XLA Modules:
  0.0 46.4 jit_solution(4715647227948837464)
XLA Ops:
  0.0 1.1 %shard_map.55 = (bf16[656,128]{1,0:T(8,128)(2,1)S(1)}, bf16[656,128]{1,0:T(8,128)(2,1)S(1)}, bf16[656,128]{1,0:T(8,128)(2,1)S(1)}) custom-call(s32[32]{0:T(128)} %refs_4_.1, bf16[2,2,2,2,2,576,128]{6,5,4,3,2,1,0:T(8,128)(2,1)} %bitcast.3), custom_call_target="tpu_custom_call" | custom-call | bytes 1048576 | tf_op jit(solution)/shard_map/pallas_call | solution.py:359
  1.1 3.0 %collective-permute-start = (bf16[656,128]{1,0:T(8,128)(2,1)S(1)}, bf16[656,128]{1,0:T(8,128)(2,1)S(1)}, u32[]{:S(2)}, u32[]{:S(2)}) collective-permute-start(bf16[656,128]{1,0:T(8,128)(2,1)S(1)} %get-tuple-element.45), channel_id=1, source_target_pairs={{0,2},{1,3},{2,0},{3,1},{4,6},{5,7},{6,4},{7,5},{8,10},{9,11},{10,... | collective-permute-start | bytes 503816 | tf_op jit(solution)/shard_map/ppermute | solution.py:385
  4.1 1.6 %collective-permute-start.1 = (bf16[656,128]{1,0:T(8,128)(2,1)S(1)}, bf16[656,128]{1,0:T(8,128)(2,1)S(1)}, u32[]{:S(2)}, u32[]{:S(2)}) collective-permute-start(bf16[656,128]{1,0:T(8,128)(2,1)S(1)} %get-tuple-element.46), channel_id=1, source_target_pairs={{0,4},{1,5},{2,6},{3,7},{4,0},{5,1},{6,2},{7,3},{8,12},{9,13},{10,... | collective-permute-start | bytes 503816 | tf_op jit(solution)/shard_map/ppermute | solution.py:385
  5.7 5.0 %shard_map.56 = (bf16[32,64,128]{2,1,0:T(8,128)(2,1)S(1)}, bf16[32,64,128]{2,1,0:T(8,128)(2,1)S(1)}, bf16[2,2,2,128,128]{4,3,2,1,0:T(8,128)(2,1)S(1)}, bf16[272,...) custom-call(bf16[32,256,128]{2,1,0:T(8,128)(2,1)} %bitcast.5, ...), custom_call_target="tpu_custom_call" | custom-call | flops 469762048 | bytes 6291456 | tf_op jit(solution)/shard_map/pallas_call | solution.py:359
  10.7 0.6 %collective-permute-done.1.refs_1_.refs_6_.refs_2_ = bf16[656,128]{1,0:T(8,128)(2,1)S(1)} collective-permute-done((bf16[656,128]{1,0:T(8,128)(2,1)S(1)}, bf16[656,128]{1,0:T(8,128)(2,1)S(1)}, u32[]{:S(2)}, u32[]{:S(2)}) %collective-permute-start.1) | collective-permute-done | bytes 167968 | tf_op jit(solution)/shard_map/ppermute | solution.py:385
  11.3 1.9 %collective-permute-done.2.refs_2_.refs_7_.refs_3_ = bf16[656,128]{1,0:T(8,128)(2,1)S(1)} collective-permute-done((bf16[656,128]{1,0:T(8,128)(2,1)S(1)}, bf16[656,128]{1,0:T(8,128)(2,1)S(1)}, u32[]{:S(2)}, u32[]{:S(2)}) %collective-permute-start.2) | collective-permute-done | bytes 167968 | tf_op jit(solution)/shard_map/ppermute | solution.py:385
  13.3 1.7 %collective-permute-start.7 = (bf16[3,512,128]{2,1,0:T(8,128)(2,1)S(1)}, bf16[3,512,128]{2,1,0:T(8,128)(2,1)S(1)}, u32[]{:S(2)}, u32[]{:S(2)}) collective-permute-start(bf16[3,512,128]{2,1,0:T(8,128)(2,1)S(1)} %shard_map.57), channel_id=1, source_target_pairs={{0,16},{16,0},{1,17},{17,1},{2,18},{18,2},{3,19},{19,3},{4,20},{20... | collective-permute-start | bytes 1179656 | tf_op jit(solution)/shard_map/ppermute | solution.py:388
  15.0 0.2 collective-permute-done.3.other_ref
  15.2 0.4 shard_map.58
  15.6 1.7 %collective-permute-start.4 = (bf16[4,2,64,128]{3,2,1,0:T(8,128)(2,1)S(1)}, bf16[4,2,64,128]{3,2,1,0:T(8,128)(2,1)S(1)}, u32[]{:S(2)}, u32[]{:S(2)}) collective-permute-start(bf16[4,2,64,128]{3,2,1,0:T(8,128)(2,1)S(1)} %get-tuple-element.55), channel_id=1, source_target_pairs={{0,2},{1,3},{2,0},{3,1},{4,6},{5,7},{6,4},{7,5},{8,10},{9,11},{10,... | collective-permute-start | bytes 393224 | tf_op jit(solution)/shard_map/ppermute | solution.py:385
  17.3 1.6 %collective-permute-start.5 = (bf16[4,2,64,128]{3,2,1,0:T(8,128)(2,1)S(1)}, bf16[4,2,64,128]{3,2,1,0:T(8,128)(2,1)S(1)}, u32[]{:S(2)}, u32[]{:S(2)}) collective-permute-start(bf16[4,2,64,128]{3,2,1,0:T(8,128)(2,1)S(1)} %get-tuple-element.56), channel_id=1, source_target_pairs={{0,4},{1,5},{2,6},{3,7},{4,0},{5,1},{6,2},{7,3},{8,12},{9,13},{10,... | collective-permute-start | bytes 393224 | tf_op jit(solution)/shard_map/ppermute | solution.py:385
  18.9 0.2 collective-permute-start.6
  19.2 2.0 %collective-permute-done.4.refs_1_ = bf16[4,2,64,128]{3,2,1,0:T(8,128)(2,1)S(1)} collective-permute-done((bf16[4,2,64,128]{3,2,1,0:T(8,128)(2,1)S(1)}, bf16[4,2,64,128]{3,2,1,0:T(8,128)(2,1)S(1)}, u32[]{:S(2)}, u32[]{:S(2)}) %collective-permute-start.4) | collective-permute-done | bytes 131104 | tf_op jit(solution)/shard_map/ppermute | solution.py:385
  21.2 2.8 %collective-permute-start.9 = (bf16[528,128]{1,0:T(8,128)(2,1)S(1)}, bf16[528,128]{1,0:T(8,128)(2,1)S(1)}, u32[]{:S(2)}, u32[]{:S(2)}) collective-permute-start(bf16[528,128]{1,0:T(8,128)(2,1)S(1)} %shard_map.60), channel_id=1, source_target_pairs={{0,8},{1,9},{2,10},{3,11},{4,12},{5,13},{6,14},{7,15},{8,0},{9,1},... | collective-permute-start | bytes 405512 | tf_op jit(solution)/shard_map/ppermute | solution.py:385
  24.0 0.9 %collective-permute-done.7.refs_8_ = bf16[3,512,128]{2,1,0:T(8,128)(2,1)S(1)} collective-permute-done((bf16[3,512,128]{2,1,0:T(8,128)(2,1)S(1)}, bf16[3,512,128]{2,1,0:T(8,128)(2,1)S(1)}, u32[]{:S(2)}, u32[]{:S(2)}) %collective-permute-start.7) | collective-permute-done | bytes 393248 | tf_op jit(solution)/shard_map/ppermute | solution.py:388
  24.9 0.6 %collective-permute-done.6.refs_3_ = bf16[4,2,64,128]{3,2,1,0:T(8,128)(2,1)S(1)} collective-permute-done((bf16[4,2,64,128]{3,2,1,0:T(8,128)(2,1)S(1)}, bf16[4,2,64,128]{3,2,1,0:T(8,128)(2,1)S(1)}, u32[]{:S(2)}, u32[]{:S(2)}) %collective-permute-start.6) | collective-permute-done | bytes 131104 | tf_op jit(solution)/shard_map/ppermute | solution.py:385
  25.5 0.8 %shard_map.59 = (bf16[4,4,64,128]{3,2,1,0:T(8,128)(2,1)S(1)}, bf16[4,4,64,128]{3,2,1,0:T(8,128)(2,1)S(1)}) custom-call(bf16[4,2,64,128]{3,2,1,0:T(8,128)(2,1)S(1)} %get-tuple-element.54.refs_0_, bf16[4,2,64,128]{3,2,1,0:T(8,128)(2,1)S(1)} %collective-permute-done.4.refs_1_, bf16[4,2,64,128]{3,2,1,0:T(8,128)(2,1)S(1)} %collective-permute-done.5.refs_2_, ...), custom_call_target="tpu_custom_call" | custom-call | flops 268435456 | bytes 2097152 | tf_op jit(solution)/shard_map/pallas_call | solution.py:359
  26.3 3.4 %collective-permute-start.8 = (bf16[4,4,64,128]{3,2,1,0:T(8,128)(2,1)S(1)}, bf16[4,4,64,128]{3,2,1,0:T(8,128)(2,1)S(1)}, u32[]{:S(2)}, u32[]{:S(2)}) collective-permute-start(bf16[4,4,64,128]{3,2,1,0:T(8,128)(2,1)S(1)} %get-tuple-element.60), channel_id=1, source_target_pairs={{0,8},{1,9},{2,10},{3,11},{4,12},{5,13},{6,14},{7,15},{8,0},{9,1},... | collective-permute-start | bytes 786440 | tf_op jit(solution)/shard_map/ppermute | solution.py:385
  29.7 1.8 %collective-permute-start.10 = (bf16[272,128]{1,0:T(8,128)(2,1)S(1)}, bf16[272,128]{1,0:T(8,128)(2,1)S(1)}, u32[]{:S(2)}, u32[]{:S(2)}) collective-permute-start(bf16[272,128]{1,0:T(8,128)(2,1)S(1)} %get-tuple-element.68), channel_id=1, source_target_pairs={{0,2},{1,3},{2,0},{3,1},{4,6},{5,7},{6,4},{7,5},{8,10},{9,11},{10,... | collective-permute-start | bytes 208904 | tf_op jit(solution)/shard_map/ppermute | solution.py:385
  31.5 1.5 %collective-permute-start.11 = (bf16[272,128]{1,0:T(8,128)(2,1)S(1)}, bf16[272,128]{1,0:T(8,128)(2,1)S(1)}, u32[]{:S(2)}, u32[]{:S(2)}) collective-permute-start(bf16[272,128]{1,0:T(8,128)(2,1)S(1)} %get-tuple-element.69), channel_id=1, source_target_pairs={{0,4},{1,5},{2,6},{3,7},{4,0},{5,1},{6,2},{7,3},{8,12},{9,13},{10,... | collective-permute-start | bytes 208904 | tf_op jit(solution)/shard_map/ppermute | solution.py:385
  33.0 0.2 collective-permute-start.12
  33.2 0.8 %collective-permute-done.10.refs_3_ = bf16[272,128]{1,0:T(8,128)(2,1)S(1)} collective-permute-done((bf16[272,128]{1,0:T(8,128)(2,1)S(1)}, bf16[272,128]{1,0:T(8,128)(2,1)S(1)}, u32[]{:S(2)}, u32[]{:S(2)}) %collective-permute-start.10) | collective-permute-done | bytes 69664 | tf_op jit(solution)/shard_map/ppermute | solution.py:385
  34.0 2.5 %collective-permute-done.11.refs_4_ = bf16[272,128]{1,0:T(8,128)(2,1)S(1)} collective-permute-done((bf16[272,128]{1,0:T(8,128)(2,1)S(1)}, bf16[272,128]{1,0:T(8,128)(2,1)S(1)}, u32[]{:S(2)}, u32[]{:S(2)}) %collective-permute-start.11) | collective-permute-done | bytes 69664 | tf_op jit(solution)/shard_map/ppermute | solution.py:385
  36.5 1.7 %collective-permute-done.12.refs_5_ = bf16[272,128]{1,0:T(8,128)(2,1)S(1)} collective-permute-done((bf16[272,128]{1,0:T(8,128)(2,1)S(1)}, bf16[272,128]{1,0:T(8,128)(2,1)S(1)}, u32[]{:S(2)}, u32[]{:S(2)}) %collective-permute-start.12) | collective-permute-done | bytes 69664 | tf_op jit(solution)/shard_map/ppermute | solution.py:385
  38.2 1.5 %collective-permute-start.13 = (bf16[528,128]{1,0:T(8,128)(2,1)S(1)}, bf16[528,128]{1,0:T(8,128)(2,1)S(1)}, u32[]{:S(2)}, u32[]{:S(2)}) collective-permute-start(bf16[528,128]{1,0:T(8,128)(2,1)S(1)} %collective-permute-done.9.refs_6_), channel_id=1, source_target_pairs={{0,16},{16,0},{1,17},{17,1},{2,18},{18,2},{3,19},{19,3},{4,20},{20... | collective-permute-start | bytes 405512 | tf_op jit(solution)/shard_map/ppermute | solution.py:388
  39.7 1.9 %collective-permute-done.8.refs_1_ = bf16[4,4,64,128]{3,2,1,0:T(8,128)(2,1)S(1)} collective-permute-done((bf16[4,4,64,128]{3,2,1,0:T(8,128)(2,1)S(1)}, bf16[4,4,64,128]{3,2,1,0:T(8,128)(2,1)S(1)}, u32[]{:S(2)}, u32[]{:S(2)}) %collective-permute-start.8) | collective-permute-done | bytes 262176 | tf_op jit(solution)/shard_map/ppermute | solution.py:385
  41.6 1.7 %collective-permute-done.13.refs_7_ = bf16[528,128]{1,0:T(8,128)(2,1)S(1)} collective-permute-done((bf16[528,128]{1,0:T(8,128)(2,1)S(1)}, bf16[528,128]{1,0:T(8,128)(2,1)S(1)}, u32[]{:S(2)}, u32[]{:S(2)}) %collective-permute-start.13) | collective-permute-done | bytes 135200 | tf_op jit(solution)/shard_map/ppermute | solution.py:388
  43.2 0.3 shard_map.61
  43.5 0.1 collective-permute-start.14
  43.6 1.4 %shard_map.62.refs_2_ = bf16[32,256,128]{2,1,0:T(8,128)(2,1)} custom-call(bf16[4,4,64,128]{3,2,1,0:T(8,128)(2,1)S(1)} %get-tuple-element.59.refs_0_, bf16[4,4,64,128]{3,2,1,0:T(8,128)(2,1)S(1)} %collective-permute-done.8.refs_1_, bf16[272,128]{1,0:T(8,128)(2,1)S(1)} %get-tuple-element.65.refs_2_, bf16[272,128]{1,0:T(8,128)(2,1)S(1)} %collective-permute-done.10.refs_3_, ...), custom_call_target="tpu_custom_call" | custom-call | flops 134217728 | bytes 2097152 | tf_op jit(solution)/shard_map/pallas_call | solution.py:359
  45.0 0.1 collective-permute-done.14.refs_0_
  45.1 1.3 %shard_map.63 = bf16[32,256,128]{2,1,0:T(8,128)(2,1)} custom-call(bf16[1040,128]{1,0:T(8,128)(2,1)S(1)} %collective-permute-done.14.refs_0_, bf16[32,64,256]{2,1,0:T(8,128)(2,1)S(1)} %copy-done, bf16[32,256,128]{2,1,0:T(8,128)(2,1)} %shard_map.62.refs_2_), custom_call_target="tpu_custom_call", output_to_operand_aliasing={{}: (2, {})} | custom-call | flops 134217728 | bytes 2097152 | tf_op jit(solution)/shard_map/pallas_call | solution.py:359
  (9 shorter events, 0.1 us)
Async XLA Ops:
  1.1 9.6 %collective-permute-start = (bf16[656,128]{1,0:T(8,128)(2,1)S(1)}, bf16[656,128]{1,0:T(8,128)(2,1)S(1)}, u32[]{:S(2)}, u32[]{:S(2)}) collective-permute-start(bf16[656,128]{1,0:T(8,128)(2,1)S(1)} %get-tuple-element.45), channel_id=1, source_target_pairs={{0,2},{1,3},{2,0},{3,1},{4,6},{5,7},{6,4},{7,5},{8,10},{9,11},{10,... | collective-permute-start | bytes 503816 | tf_op jit(solution)/shard_map/ppermute | solution.py:385
  4.1 7.2 %collective-permute-start.1 = (bf16[656,128]{1,0:T(8,128)(2,1)S(1)}, bf16[656,128]{1,0:T(8,128)(2,1)S(1)}, u32[]{:S(2)}, u32[]{:S(2)}) collective-permute-start(bf16[656,128]{1,0:T(8,128)(2,1)S(1)} %get-tuple-element.46), channel_id=1, source_target_pairs={{0,4},{1,5},{2,6},{3,7},{4,0},{5,1},{6,2},{7,3},{8,12},{9,13},{10,... | collective-permute-start | bytes 503816 | tf_op jit(solution)/shard_map/ppermute | solution.py:385
  5.7 7.6 %collective-permute-start.2 = (bf16[656,128]{1,0:T(8,128)(2,1)S(1)}, bf16[656,128]{1,0:T(8,128)(2,1)S(1)}, u32[]{:S(2)}, u32[]{:S(2)}) collective-permute-start(bf16[656,128]{1,0:T(8,128)(2,1)S(1)} %get-tuple-element.47), channel_id=1, source_target_pairs={{0,6},{1,7},{2,4},{3,5},{4,2},{5,3},{6,0},{7,1},{8,14},{9,15},{10,... | collective-permute-start | bytes 503816 | tf_op jit(solution)/shard_map/ppermute | solution.py:385
  13.3 1.9 %collective-permute-start.3 = (bf16[32,64,128]{2,1,0:T(8,128)(2,1)S(1)}, bf16[32,64,128]{2,1,0:T(8,128)(2,1)S(1)}, u32[]{:S(2)}, u32[]{:S(2)}) collective-permute-start(bf16[32,64,128]{2,1,0:T(8,128)(2,1)S(1)} %get-tuple-element.48.own_ref), channel_id=1, source_target_pairs={{0,1},{1,0},{2,3},{3,2},{4,5},{5,4},{6,7},{7,6},{8,9},{9,8},{10,11... | collective-permute-start | bytes 1572872 | tf_op jit(solution)/shard_map/ppermute | solution.py:385
  13.3 11.6 %collective-permute-start.7 = (bf16[3,512,128]{2,1,0:T(8,128)(2,1)S(1)}, bf16[3,512,128]{2,1,0:T(8,128)(2,1)S(1)}, u32[]{:S(2)}, u32[]{:S(2)}) collective-permute-start(bf16[3,512,128]{2,1,0:T(8,128)(2,1)S(1)} %shard_map.57), channel_id=1, source_target_pairs={{0,16},{16,0},{1,17},{17,1},{2,18},{18,2},{3,19},{19,3},{4,20},{20... | collective-permute-start | bytes 1179656 | tf_op jit(solution)/shard_map/ppermute | solution.py:388
  15.6 28.0 %copy-start = (bf16[32,64,256]{2,1,0:T(8,128)(2,1)S(1)}, bf16[32,64,256]{2,1,0:T(8,128)(2,1)}, u32[]{:S(2)}) copy-start(bf16[32,64,256]{2,1,0:T(8,128)(2,1)} %refs_1_.3) | copy-start | bytes 3145732
  15.6 5.6 %collective-permute-start.4 = (bf16[4,2,64,128]{3,2,1,0:T(8,128)(2,1)S(1)}, bf16[4,2,64,128]{3,2,1,0:T(8,128)(2,1)S(1)}, u32[]{:S(2)}, u32[]{:S(2)}) collective-permute-start(bf16[4,2,64,128]{3,2,1,0:T(8,128)(2,1)S(1)} %get-tuple-element.55), channel_id=1, source_target_pairs={{0,2},{1,3},{2,0},{3,1},{4,6},{5,7},{6,4},{7,5},{8,10},{9,11},{10,... | collective-permute-start | bytes 393224 | tf_op jit(solution)/shard_map/ppermute | solution.py:385
  17.3 7.6 %collective-permute-start.5 = (bf16[4,2,64,128]{3,2,1,0:T(8,128)(2,1)S(1)}, bf16[4,2,64,128]{3,2,1,0:T(8,128)(2,1)S(1)}, u32[]{:S(2)}, u32[]{:S(2)}) collective-permute-start(bf16[4,2,64,128]{3,2,1,0:T(8,128)(2,1)S(1)} %get-tuple-element.56), channel_id=1, source_target_pairs={{0,4},{1,5},{2,6},{3,7},{4,0},{5,1},{6,2},{7,3},{8,12},{9,13},{10,... | collective-permute-start | bytes 393224 | tf_op jit(solution)/shard_map/ppermute | solution.py:385
  18.9 6.6 %collective-permute-start.6 = (bf16[4,2,64,128]{3,2,1,0:T(8,128)(2,1)S(1)}, bf16[4,2,64,128]{3,2,1,0:T(8,128)(2,1)S(1)}, u32[]{:S(2)}, u32[]{:S(2)}) collective-permute-start(bf16[4,2,64,128]{3,2,1,0:T(8,128)(2,1)S(1)} %get-tuple-element.57), channel_id=1, source_target_pairs={{0,6},{1,7},{2,4},{3,5},{4,2},{5,3},{6,0},{7,1},{8,14},{9,15},{10,... | collective-permute-start | bytes 393224 | tf_op jit(solution)/shard_map/ppermute | solution.py:385
  21.2 17.0 %collective-permute-start.9 = (bf16[528,128]{1,0:T(8,128)(2,1)S(1)}, bf16[528,128]{1,0:T(8,128)(2,1)S(1)}, u32[]{:S(2)}, u32[]{:S(2)}) collective-permute-start(bf16[528,128]{1,0:T(8,128)(2,1)S(1)} %shard_map.60), channel_id=1, source_target_pairs={{0,8},{1,9},{2,10},{3,11},{4,12},{5,13},{6,14},{7,15},{8,0},{9,1},... | collective-permute-start | bytes 405512 | tf_op jit(solution)/shard_map/ppermute | solution.py:385
  26.3 15.2 %collective-permute-start.8 = (bf16[4,4,64,128]{3,2,1,0:T(8,128)(2,1)S(1)}, bf16[4,4,64,128]{3,2,1,0:T(8,128)(2,1)S(1)}, u32[]{:S(2)}, u32[]{:S(2)}) collective-permute-start(bf16[4,4,64,128]{3,2,1,0:T(8,128)(2,1)S(1)} %get-tuple-element.60), channel_id=1, source_target_pairs={{0,8},{1,9},{2,10},{3,11},{4,12},{5,13},{6,14},{7,15},{8,0},{9,1},... | collective-permute-start | bytes 786440 | tf_op jit(solution)/shard_map/ppermute | solution.py:385
  29.7 4.3 %collective-permute-start.10 = (bf16[272,128]{1,0:T(8,128)(2,1)S(1)}, bf16[272,128]{1,0:T(8,128)(2,1)S(1)}, u32[]{:S(2)}, u32[]{:S(2)}) collective-permute-start(bf16[272,128]{1,0:T(8,128)(2,1)S(1)} %get-tuple-element.68), channel_id=1, source_target_pairs={{0,2},{1,3},{2,0},{3,1},{4,6},{5,7},{6,4},{7,5},{8,10},{9,11},{10,... | collective-permute-start | bytes 208904 | tf_op jit(solution)/shard_map/ppermute | solution.py:385
  31.5 5.1 %collective-permute-start.11 = (bf16[272,128]{1,0:T(8,128)(2,1)S(1)}, bf16[272,128]{1,0:T(8,128)(2,1)S(1)}, u32[]{:S(2)}, u32[]{:S(2)}) collective-permute-start(bf16[272,128]{1,0:T(8,128)(2,1)S(1)} %get-tuple-element.69), channel_id=1, source_target_pairs={{0,4},{1,5},{2,6},{3,7},{4,0},{5,1},{6,2},{7,3},{8,12},{9,13},{10,... | collective-permute-start | bytes 208904 | tf_op jit(solution)/shard_map/ppermute | solution.py:385
  33.0 5.2 %collective-permute-start.12 = (bf16[272,128]{1,0:T(8,128)(2,1)S(1)}, bf16[272,128]{1,0:T(8,128)(2,1)S(1)}, u32[]{:S(2)}, u32[]{:S(2)}) collective-permute-start(bf16[272,128]{1,0:T(8,128)(2,1)S(1)} %get-tuple-element.70), channel_id=1, source_target_pairs={{0,6},{1,7},{2,4},{3,5},{4,2},{5,3},{6,0},{7,1},{8,14},{9,15},{10,... | collective-permute-start | bytes 208904 | tf_op jit(solution)/shard_map/ppermute | solution.py:385
  38.2 5.0 %collective-permute-start.13 = (bf16[528,128]{1,0:T(8,128)(2,1)S(1)}, bf16[528,128]{1,0:T(8,128)(2,1)S(1)}, u32[]{:S(2)}, u32[]{:S(2)}) collective-permute-start(bf16[528,128]{1,0:T(8,128)(2,1)S(1)} %collective-permute-done.9.refs_6_), channel_id=1, source_target_pairs={{0,16},{16,0},{1,17},{17,1},{2,18},{18,2},{3,19},{19,3},{4,20},{20... | collective-permute-start | bytes 405512 | tf_op jit(solution)/shard_map/ppermute | solution.py:388
  43.5 1.6 %collective-permute-start.14 = (bf16[1040,128]{1,0:T(8,128)(2,1)S(1)}, bf16[1040,128]{1,0:T(8,128)(2,1)S(1)}, u32[]{:S(2)}, u32[]{:S(2)}) collective-permute-start(bf16[1040,128]{1,0:T(8,128)(2,1)S(1)} %shard_map.61), channel_id=1, source_target_pairs={{0,1},{1,0},{2,3},{3,2},{4,5},{5,4},{6,7},{7,6},{8,9},{9,8},{10,11... | collective-permute-start | bytes 798728 | tf_op jit(solution)/shard_map/ppermute | solution.py:385

commit v7 on v6

--- a/solution.py
+++ b/solution.py
@@ -90,6 +90,13 @@
 
 def stacked(first, second):
     return jnp.concatenate([first, second], axis=0)
+
+
+def products(first, second, own, other):
+    width = own.shape[0]
+    turned = jnp.concatenate([second[:, width:], second[:, :width]], axis=1)
+    both = product(stacked(first, turned), stacked(own, other))
+    return both[:width], both[width:]
 
 
 def own_half():
@@ -258,17 +265,21 @@
         start = pl.multiple_of(((i3 * 2 + i0) * 2 + level) * rank, TILE)
         return ref[pl.ds(start, rank), :]
 
-    order = [(r, h, i3) for r in range(4) for h in range(2) for i3 in range(2)]
-    for r, h, i3 in order:
-        q = (group ^ h) * 2 + i3
-        for i0 in range(2):
-            rows = stacked(boxes[r][q, i0], boxes[r ^ 1][q, i0])
-            middle[r, q, i0] = product(matrix(r, h, i3, i0, 0), rows)
+    slots = [(h, i3) for h in range(2) for i3 in range(2)]
+    for r in (0, 2):
+        for h, i3 in slots:
+            q = (group ^ h) * 2 + i3
+            for i0 in range(2):
+                pair = matrix(r, h, i3, i0, 0), matrix(r + 1, h, i3, i0, 0)
+                both = products(*pair, boxes[r][q, i0], boxes[r + 1][q, i0])
+                middle[r, q, i0], middle[r + 1, q, i0] = both
     for out_ref, bit in ((send_ref, 1 - half), (keep_ref, half)):
-        for r, h, i3 in order:
-            q = (group ^ h) * 2 + i3
-            rows = stacked(middle[r, q, bit], middle[r ^ 2, q, bit])
-            out_ref[r, q] = product(matrix(r, h, i3, bit, 1), rows)
+        for r in (0, 1):
+            for h, i3 in slots:
+                q = (group ^ h) * 2 + i3
+                pair = matrix(r, h, i3, bit, 1), matrix(r + 2, h, i3, bit, 1)
+                both = products(*pair, middle[r, q, bit], middle[r + 2, q, bit])
+                out_ref[r, q], out_ref[r + 2, q] = both
 
 
 def last_matrices(rank, bit, stay0, stay1, stay2, stay3, here_ref, cross_ref):

time: 46.6 us -> 46.4 us (level)
  transfers between devices with their start and end apart: 15 -> 15, of which waited for: 12 -> 12; matrix products, arithmetic and copies ran while one was open for 0% -> 0% of each run, Pallas kernels for 17% -> 16%
where the time goes in v7:
time: 46.4 us; the launch traced here: 46.2 us
  starting transfers between devices  21.1 us (45%)
  waiting for transfers between devices  14.8 us (32%)
  Pallas kernels  10.2 us (22%)
    ppermute x13, starting transfers between devices, across(): return lax.ppermute(value, AXES, [(s, s ^ mask) for s in range(16)])  17.9 us
    ppermute x13, waiting for transfers between devices, across(): return lax.ppermute(value, AXES, [(s, s ^ mask) for s in range(16)])  12.5 us
    pallas_call x9, Pallas kernels, placed(): run(*(pltpu.with_memory_space_constraint(operand, space) if space == pltp...  10.2 us
    ppermute x2, starting transfers between devices, swapped(): return lax.ppermute(value, 'groups', [(0, 1), (1, 0)])  3.2 us
    ppermute x2, waiting for transfers between devices, swapped(): return lax.ppermute(value, 'groups', [(0, 1), (1, 0)])  2.34 us
  transfers between devices with their start and end apart: 15, of which 12 were waited for; matrix products, arithmetic and copies ran while one was open for 0% of the time, Pallas kernels for 16%

profile of v7, /device:TPU:0, one launch (start us, length us, event | category | flops | bytes accessed | tf_op | source)
XLA Modules:
  0.0 46.2 jit_solution(3535554207008306373)
XLA Ops:
  0.0 1.1 %shard_map.55 = (bf16[656,128]{1,0:T(8,128)(2,1)S(1)}, bf16[656,128]{1,0:T(8,128)(2,1)S(1)}, bf16[656,128]{1,0:T(8,128)(2,1)S(1)}) custom-call(s32[32]{0:T(128)} %refs_4_.1, bf16[2,2,2,2,2,576,128]{6,5,4,3,2,1,0:T(8,128)(2,1)} %bitcast.3), custom_call_target="tpu_custom_call" | custom-call | bytes 1048576 | tf_op jit(solution)/shard_map/pallas_call | solution.py:370
  1.1 3.0 %collective-permute-start = (bf16[656,128]{1,0:T(8,128)(2,1)S(1)}, bf16[656,128]{1,0:T(8,128)(2,1)S(1)}, u32[]{:S(2)}, u32[]{:S(2)}) collective-permute-start(bf16[656,128]{1,0:T(8,128)(2,1)S(1)} %get-tuple-element.45), channel_id=1, source_target_pairs={{0,2},{1,3},{2,0},{3,1},{4,6},{5,7},{6,4},{7,5},{8,10},{9,11},{10,... | collective-permute-start | bytes 503816 | tf_op jit(solution)/shard_map/ppermute | solution.py:396
  4.1 1.6 %collective-permute-start.1 = (bf16[656,128]{1,0:T(8,128)(2,1)S(1)}, bf16[656,128]{1,0:T(8,128)(2,1)S(1)}, u32[]{:S(2)}, u32[]{:S(2)}) collective-permute-start(bf16[656,128]{1,0:T(8,128)(2,1)S(1)} %get-tuple-element.46), channel_id=1, source_target_pairs={{0,4},{1,5},{2,6},{3,7},{4,0},{5,1},{6,2},{7,3},{8,12},{9,13},{10,... | collective-permute-start | bytes 503816 | tf_op jit(solution)/shard_map/ppermute | solution.py:396
  5.7 5.0 %shard_map.56 = (bf16[32,64,128]{2,1,0:T(8,128)(2,1)S(1)}, bf16[32,64,128]{2,1,0:T(8,128)(2,1)S(1)}, bf16[2,2,2,128,128]{4,3,2,1,0:T(8,128)(2,1)S(1)}, bf16[272,...) custom-call(bf16[32,256,128]{2,1,0:T(8,128)(2,1)} %bitcast.5, ...), custom_call_target="tpu_custom_call" | custom-call | flops 469762048 | bytes 6291456 | tf_op jit(solution)/shard_map/pallas_call | solution.py:370
  10.7 0.6 %collective-permute-done.1.refs_1_.refs_6_.refs_2_ = bf16[656,128]{1,0:T(8,128)(2,1)S(1)} collective-permute-done((bf16[656,128]{1,0:T(8,128)(2,1)S(1)}, bf16[656,128]{1,0:T(8,128)(2,1)S(1)}, u32[]{:S(2)}, u32[]{:S(2)}) %collective-permute-start.1) | collective-permute-done | bytes 167968 | tf_op jit(solution)/shard_map/ppermute | solution.py:396
  11.3 1.9 %collective-permute-done.2.refs_2_.refs_7_.refs_3_ = bf16[656,128]{1,0:T(8,128)(2,1)S(1)} collective-permute-done((bf16[656,128]{1,0:T(8,128)(2,1)S(1)}, bf16[656,128]{1,0:T(8,128)(2,1)S(1)}, u32[]{:S(2)}, u32[]{:S(2)}) %collective-permute-start.2) | collective-permute-done | bytes 167968 | tf_op jit(solution)/shard_map/ppermute | solution.py:396
  13.3 1.7 %collective-permute-start.7 = (bf16[3,512,128]{2,1,0:T(8,128)(2,1)S(1)}, bf16[3,512,128]{2,1,0:T(8,128)(2,1)S(1)}, u32[]{:S(2)}, u32[]{:S(2)}) collective-permute-start(bf16[3,512,128]{2,1,0:T(8,128)(2,1)S(1)} %shard_map.57), channel_id=1, source_target_pairs={{0,16},{16,0},{1,17},{17,1},{2,18},{18,2},{3,19},{19,3},{4,20},{20... | collective-permute-start | bytes 1179656 | tf_op jit(solution)/shard_map/ppermute | solution.py:399
  15.0 0.2 collective-permute-done.3.other_ref
  15.2 0.4 shard_map.58
  15.6 1.7 %collective-permute-start.4 = (bf16[4,2,64,128]{3,2,1,0:T(8,128)(2,1)S(1)}, bf16[4,2,64,128]{3,2,1,0:T(8,128)(2,1)S(1)}, u32[]{:S(2)}, u32[]{:S(2)}) collective-permute-start(bf16[4,2,64,128]{3,2,1,0:T(8,128)(2,1)S(1)} %get-tuple-element.55), channel_id=1, source_target_pairs={{0,2},{1,3},{2,0},{3,1},{4,6},{5,7},{6,4},{7,5},{8,10},{9,11},{10,... | collective-permute-start | bytes 393224 | tf_op jit(solution)/shard_map/ppermute | solution.py:396
  17.3 1.6 %collective-permute-start.5 = (bf16[4,2,64,128]{3,2,1,0:T(8,128)(2,1)S(1)}, bf16[4,2,64,128]{3,2,1,0:T(8,128)(2,1)S(1)}, u32[]{:S(2)}, u32[]{:S(2)}) collective-permute-start(bf16[4,2,64,128]{3,2,1,0:T(8,128)(2,1)S(1)} %get-tuple-element.56), channel_id=1, source_target_pairs={{0,4},{1,5},{2,6},{3,7},{4,0},{5,1},{6,2},{7,3},{8,12},{9,13},{10,... | collective-permute-start | bytes 393224 | tf_op jit(solution)/shard_map/ppermute | solution.py:396
  18.9 0.2 collective-permute-start.6
  19.2 2.0 %collective-permute-done.4.refs_1_ = bf16[4,2,64,128]{3,2,1,0:T(8,128)(2,1)S(1)} collective-permute-done((bf16[4,2,64,128]{3,2,1,0:T(8,128)(2,1)S(1)}, bf16[4,2,64,128]{3,2,1,0:T(8,128)(2,1)S(1)}, u32[]{:S(2)}, u32[]{:S(2)}) %collective-permute-start.4) | collective-permute-done | bytes 131104 | tf_op jit(solution)/shard_map/ppermute | solution.py:396
  21.2 2.8 %collective-permute-start.9 = (bf16[528,128]{1,0:T(8,128)(2,1)S(1)}, bf16[528,128]{1,0:T(8,128)(2,1)S(1)}, u32[]{:S(2)}, u32[]{:S(2)}) collective-permute-start(bf16[528,128]{1,0:T(8,128)(2,1)S(1)} %shard_map.60), channel_id=1, source_target_pairs={{0,8},{1,9},{2,10},{3,11},{4,12},{5,13},{6,14},{7,15},{8,0},{9,1},... | collective-permute-start | bytes 405512 | tf_op jit(solution)/shard_map/ppermute | solution.py:396
  24.0 0.9 %collective-permute-done.7.refs_8_ = bf16[3,512,128]{2,1,0:T(8,128)(2,1)S(1)} collective-permute-done((bf16[3,512,128]{2,1,0:T(8,128)(2,1)S(1)}, bf16[3,512,128]{2,1,0:T(8,128)(2,1)S(1)}, u32[]{:S(2)}, u32[]{:S(2)}) %collective-permute-start.7) | collective-permute-done | bytes 393248 | tf_op jit(solution)/shard_map/ppermute | solution.py:399
  24.9 0.6 %collective-permute-done.6.refs_3_ = bf16[4,2,64,128]{3,2,1,0:T(8,128)(2,1)S(1)} collective-permute-done((bf16[4,2,64,128]{3,2,1,0:T(8,128)(2,1)S(1)}, bf16[4,2,64,128]{3,2,1,0:T(8,128)(2,1)S(1)}, u32[]{:S(2)}, u32[]{:S(2)}) %collective-permute-start.6) | collective-permute-done | bytes 131104 | tf_op jit(solution)/shard_map/ppermute | solution.py:396
  25.5 0.7 %shard_map.59 = (bf16[4,4,64,128]{3,2,1,0:T(8,128)(2,1)S(1)}, bf16[4,4,64,128]{3,2,1,0:T(8,128)(2,1)S(1)}) custom-call(bf16[4,2,64,128]{3,2,1,0:T(8,128)(2,1)S(1)} %get-tuple-element.54.refs_0_, bf16[4,2,64,128]{3,2,1,0:T(8,128)(2,1)S(1)} %collective-permute-done.4.refs_1_, bf16[4,2,64,128]{3,2,1,0:T(8,128)(2,1)S(1)} %collective-permute-done.5.refs_2_, ...), custom_call_target="tpu_custom_call" | custom-call | flops 268435456 | bytes 2097152 | tf_op jit(solution)/shard_map/pallas_call | solution.py:370
  26.1 3.4 %collective-permute-start.8 = (bf16[4,4,64,128]{3,2,1,0:T(8,128)(2,1)S(1)}, bf16[4,4,64,128]{3,2,1,0:T(8,128)(2,1)S(1)}, u32[]{:S(2)}, u32[]{:S(2)}) collective-permute-start(bf16[4,4,64,128]{3,2,1,0:T(8,128)(2,1)S(1)} %get-tuple-element.60), channel_id=1, source_target_pairs={{0,8},{1,9},{2,10},{3,11},{4,12},{5,13},{6,14},{7,15},{8,0},{9,1},... | collective-permute-start | bytes 786440 | tf_op jit(solution)/shard_map/ppermute | solution.py:396
  29.6 1.7 %collective-permute-start.10 = (bf16[272,128]{1,0:T(8,128)(2,1)S(1)}, bf16[272,128]{1,0:T(8,128)(2,1)S(1)}, u32[]{:S(2)}, u32[]{:S(2)}) collective-permute-start(bf16[272,128]{1,0:T(8,128)(2,1)S(1)} %get-tuple-element.68), channel_id=1, source_target_pairs={{0,2},{1,3},{2,0},{3,1},{4,6},{5,7},{6,4},{7,5},{8,10},{9,11},{10,... | collective-permute-start | bytes 208904 | tf_op jit(solution)/shard_map/ppermute | solution.py:396
  31.3 1.5 %collective-permute-start.11 = (bf16[272,128]{1,0:T(8,128)(2,1)S(1)}, bf16[272,128]{1,0:T(8,128)(2,1)S(1)}, u32[]{:S(2)}, u32[]{:S(2)}) collective-permute-start(bf16[272,128]{1,0:T(8,128)(2,1)S(1)} %get-tuple-element.69), channel_id=1, source_target_pairs={{0,4},{1,5},{2,6},{3,7},{4,0},{5,1},{6,2},{7,3},{8,12},{9,13},{10,... | collective-permute-start | bytes 208904 | tf_op jit(solution)/shard_map/ppermute | solution.py:396
  32.8 0.2 collective-permute-start.12
  33.0 0.8 %collective-permute-done.10.refs_3_ = bf16[272,128]{1,0:T(8,128)(2,1)S(1)} collective-permute-done((bf16[272,128]{1,0:T(8,128)(2,1)S(1)}, bf16[272,128]{1,0:T(8,128)(2,1)S(1)}, u32[]{:S(2)}, u32[]{:S(2)}) %collective-permute-start.10) | collective-permute-done | bytes 69664 | tf_op jit(solution)/shard_map/ppermute | solution.py:396
  33.9 2.5 %collective-permute-done.11.refs_4_ = bf16[272,128]{1,0:T(8,128)(2,1)S(1)} collective-permute-done((bf16[272,128]{1,0:T(8,128)(2,1)S(1)}, bf16[272,128]{1,0:T(8,128)(2,1)S(1)}, u32[]{:S(2)}, u32[]{:S(2)}) %collective-permute-start.11) | collective-permute-done | bytes 69664 | tf_op jit(solution)/shard_map/ppermute | solution.py:396
  36.4 1.7 %collective-permute-done.12.refs_5_ = bf16[272,128]{1,0:T(8,128)(2,1)S(1)} collective-permute-done((bf16[272,128]{1,0:T(8,128)(2,1)S(1)}, bf16[272,128]{1,0:T(8,128)(2,1)S(1)}, u32[]{:S(2)}, u32[]{:S(2)}) %collective-permute-start.12) | collective-permute-done | bytes 69664 | tf_op jit(solution)/shard_map/ppermute | solution.py:396
  38.0 1.5 %collective-permute-start.13 = (bf16[528,128]{1,0:T(8,128)(2,1)S(1)}, bf16[528,128]{1,0:T(8,128)(2,1)S(1)}, u32[]{:S(2)}, u32[]{:S(2)}) collective-permute-start(bf16[528,128]{1,0:T(8,128)(2,1)S(1)} %collective-permute-done.9.refs_6_), channel_id=1, source_target_pairs={{0,16},{16,0},{1,17},{17,1},{2,18},{18,2},{3,19},{19,3},{4,20},{20... | collective-permute-start | bytes 405512 | tf_op jit(solution)/shard_map/ppermute | solution.py:399
  39.5 2.0 %collective-permute-done.8.refs_1_ = bf16[4,4,64,128]{3,2,1,0:T(8,128)(2,1)S(1)} collective-permute-done((bf16[4,4,64,128]{3,2,1,0:T(8,128)(2,1)S(1)}, bf16[4,4,64,128]{3,2,1,0:T(8,128)(2,1)S(1)}, u32[]{:S(2)}, u32[]{:S(2)}) %collective-permute-start.8) | collective-permute-done | bytes 262176 | tf_op jit(solution)/shard_map/ppermute | solution.py:396
  41.6 1.5 %collective-permute-done.13.refs_7_ = bf16[528,128]{1,0:T(8,128)(2,1)S(1)} collective-permute-done((bf16[528,128]{1,0:T(8,128)(2,1)S(1)}, bf16[528,128]{1,0:T(8,128)(2,1)S(1)}, u32[]{:S(2)}, u32[]{:S(2)}) %collective-permute-start.13) | collective-permute-done | bytes 135200 | tf_op jit(solution)/shard_map/ppermute | solution.py:399
  43.0 0.3 shard_map.61
  43.3 0.1 collective-permute-start.14
  43.4 1.4 %shard_map.62.refs_2_ = bf16[32,256,128]{2,1,0:T(8,128)(2,1)} custom-call(bf16[4,4,64,128]{3,2,1,0:T(8,128)(2,1)S(1)} %get-tuple-element.59.refs_0_, bf16[4,4,64,128]{3,2,1,0:T(8,128)(2,1)S(1)} %collective-permute-done.8.refs_1_, bf16[272,128]{1,0:T(8,128)(2,1)S(1)} %get-tuple-element.65.refs_2_, bf16[272,128]{1,0:T(8,128)(2,1)S(1)} %collective-permute-done.10.refs_3_, ...), custom_call_target="tpu_custom_call" | custom-call | flops 134217728 | bytes 2097152 | tf_op jit(solution)/shard_map/pallas_call | solution.py:370
  44.8 0.1 collective-permute-done.14.refs_0_
  44.9 1.3 %shard_map.63 = bf16[32,256,128]{2,1,0:T(8,128)(2,1)} custom-call(bf16[1040,128]{1,0:T(8,128)(2,1)S(1)} %collective-permute-done.14.refs_0_, bf16[32,64,256]{2,1,0:T(8,128)(2,1)S(1)} %copy-done, bf16[32,256,128]{2,1,0:T(8,128)(2,1)} %shard_map.62.refs_2_), custom_call_target="tpu_custom_call", output_to_operand_aliasing={{}: (2, {})} | custom-call | flops 134217728 | bytes 2097152 | tf_op jit(solution)/shard_map/pallas_call | solution.py:370
  (9 shorter events, 0.1 us)
Async XLA Ops:
  1.1 9.6 %collective-permute-start = (bf16[656,128]{1,0:T(8,128)(2,1)S(1)}, bf16[656,128]{1,0:T(8,128)(2,1)S(1)}, u32[]{:S(2)}, u32[]{:S(2)}) collective-permute-start(bf16[656,128]{1,0:T(8,128)(2,1)S(1)} %get-tuple-element.45), channel_id=1, source_target_pairs={{0,2},{1,3},{2,0},{3,1},{4,6},{5,7},{6,4},{7,5},{8,10},{9,11},{10,... | collective-permute-start | bytes 503816 | tf_op jit(solution)/shard_map/ppermute | solution.py:396
  4.1 7.2 %collective-permute-start.1 = (bf16[656,128]{1,0:T(8,128)(2,1)S(1)}, bf16[656,128]{1,0:T(8,128)(2,1)S(1)}, u32[]{:S(2)}, u32[]{:S(2)}) collective-permute-start(bf16[656,128]{1,0:T(8,128)(2,1)S(1)} %get-tuple-element.46), channel_id=1, source_target_pairs={{0,4},{1,5},{2,6},{3,7},{4,0},{5,1},{6,2},{7,3},{8,12},{9,13},{10,... | collective-permute-start | bytes 503816 | tf_op jit(solution)/shard_map/ppermute | solution.py:396
  5.7 7.6 %collective-permute-start.2 = (bf16[656,128]{1,0:T(8,128)(2,1)S(1)}, bf16[656,128]{1,0:T(8,128)(2,1)S(1)}, u32[]{:S(2)}, u32[]{:S(2)}) collective-permute-start(bf16[656,128]{1,0:T(8,128)(2,1)S(1)} %get-tuple-element.47), channel_id=1, source_target_pairs={{0,6},{1,7},{2,4},{3,5},{4,2},{5,3},{6,0},{7,1},{8,14},{9,15},{10,... | collective-permute-start | bytes 503816 | tf_op jit(solution)/shard_map/ppermute | solution.py:396
  13.3 1.9 %collective-permute-start.3 = (bf16[32,64,128]{2,1,0:T(8,128)(2,1)S(1)}, bf16[32,64,128]{2,1,0:T(8,128)(2,1)S(1)}, u32[]{:S(2)}, u32[]{:S(2)}) collective-permute-start(bf16[32,64,128]{2,1,0:T(8,128)(2,1)S(1)} %get-tuple-element.48.own_ref), channel_id=1, source_target_pairs={{0,1},{1,0},{2,3},{3,2},{4,5},{5,4},{6,7},{7,6},{8,9},{9,8},{10,11... | collective-permute-start | bytes 1572872 | tf_op jit(solution)/shard_map/ppermute | solution.py:396
  13.3 11.6 %collective-permute-start.7 = (bf16[3,512,128]{2,1,0:T(8,128)(2,1)S(1)}, bf16[3,512,128]{2,1,0:T(8,128)(2,1)S(1)}, u32[]{:S(2)}, u32[]{:S(2)}) collective-permute-start(bf16[3,512,128]{2,1,0:T(8,128)(2,1)S(1)} %shard_map.57), channel_id=1, source_target_pairs={{0,16},{16,0},{1,17},{17,1},{2,18},{18,2},{3,19},{19,3},{4,20},{20... | collective-permute-start | bytes 1179656 | tf_op jit(solution)/shard_map/ppermute | solution.py:399
  15.6 27.8 %copy-start = (bf16[32,64,256]{2,1,0:T(8,128)(2,1)S(1)}, bf16[32,64,256]{2,1,0:T(8,128)(2,1)}, u32[]{:S(2)}) copy-start(bf16[32,64,256]{2,1,0:T(8,128)(2,1)} %refs_1_.3) | copy-start | bytes 3145732
  15.6 5.6 %collective-permute-start.4 = (bf16[4,2,64,128]{3,2,1,0:T(8,128)(2,1)S(1)}, bf16[4,2,64,128]{3,2,1,0:T(8,128)(2,1)S(1)}, u32[]{:S(2)}, u32[]{:S(2)}) collective-permute-start(bf16[4,2,64,128]{3,2,1,0:T(8,128)(2,1)S(1)} %get-tuple-element.55), channel_id=1, source_target_pairs={{0,2},{1,3},{2,0},{3,1},{4,6},{5,7},{6,4},{7,5},{8,10},{9,11},{10,... | collective-permute-start | bytes 393224 | tf_op jit(solution)/shard_map/ppermute | solution.py:396
  17.3 7.6 %collective-permute-start.5 = (bf16[4,2,64,128]{3,2,1,0:T(8,128)(2,1)S(1)}, bf16[4,2,64,128]{3,2,1,0:T(8,128)(2,1)S(1)}, u32[]{:S(2)}, u32[]{:S(2)}) collective-permute-start(bf16[4,2,64,128]{3,2,1,0:T(8,128)(2,1)S(1)} %get-tuple-element.56), channel_id=1, source_target_pairs={{0,4},{1,5},{2,6},{3,7},{4,0},{5,1},{6,2},{7,3},{8,12},{9,13},{10,... | collective-permute-start | bytes 393224 | tf_op jit(solution)/shard_map/ppermute | solution.py:396
  18.9 6.6 %collective-permute-start.6 = (bf16[4,2,64,128]{3,2,1,0:T(8,128)(2,1)S(1)}, bf16[4,2,64,128]{3,2,1,0:T(8,128)(2,1)S(1)}, u32[]{:S(2)}, u32[]{:S(2)}) collective-permute-start(bf16[4,2,64,128]{3,2,1,0:T(8,128)(2,1)S(1)} %get-tuple-element.57), channel_id=1, source_target_pairs={{0,6},{1,7},{2,4},{3,5},{4,2},{5,3},{6,0},{7,1},{8,14},{9,15},{10,... | collective-permute-start | bytes 393224 | tf_op jit(solution)/shard_map/ppermute | solution.py:396
  21.2 16.8 %collective-permute-start.9 = (bf16[528,128]{1,0:T(8,128)(2,1)S(1)}, bf16[528,128]{1,0:T(8,128)(2,1)S(1)}, u32[]{:S(2)}, u32[]{:S(2)}) collective-permute-start(bf16[528,128]{1,0:T(8,128)(2,1)S(1)} %shard_map.60), channel_id=1, source_target_pairs={{0,8},{1,9},{2,10},{3,11},{4,12},{5,13},{6,14},{7,15},{8,0},{9,1},... | collective-permute-start | bytes 405512 | tf_op jit(solution)/shard_map/ppermute | solution.py:396
  26.1 15.4 %collective-permute-start.8 = (bf16[4,4,64,128]{3,2,1,0:T(8,128)(2,1)S(1)}, bf16[4,4,64,128]{3,2,1,0:T(8,128)(2,1)S(1)}, u32[]{:S(2)}, u32[]{:S(2)}) collective-permute-start(bf16[4,4,64,128]{3,2,1,0:T(8,128)(2,1)S(1)} %get-tuple-element.60), channel_id=1, source_target_pairs={{0,8},{1,9},{2,10},{3,11},{4,12},{5,13},{6,14},{7,15},{8,0},{9,1},... | collective-permute-start | bytes 786440 | tf_op jit(solution)/shard_map/ppermute | solution.py:396
  29.6 4.3 %collective-permute-start.10 = (bf16[272,128]{1,0:T(8,128)(2,1)S(1)}, bf16[272,128]{1,0:T(8,128)(2,1)S(1)}, u32[]{:S(2)}, u32[]{:S(2)}) collective-permute-start(bf16[272,128]{1,0:T(8,128)(2,1)S(1)} %get-tuple-element.68), channel_id=1, source_target_pairs={{0,2},{1,3},{2,0},{3,1},{4,6},{5,7},{6,4},{7,5},{8,10},{9,11},{10,... | collective-permute-start | bytes 208904 | tf_op jit(solution)/shard_map/ppermute | solution.py:396
  31.3 5.0 %collective-permute-start.11 = (bf16[272,128]{1,0:T(8,128)(2,1)S(1)}, bf16[272,128]{1,0:T(8,128)(2,1)S(1)}, u32[]{:S(2)}, u32[]{:S(2)}) collective-permute-start(bf16[272,128]{1,0:T(8,128)(2,1)S(1)} %get-tuple-element.69), channel_id=1, source_target_pairs={{0,4},{1,5},{2,6},{3,7},{4,0},{5,1},{6,2},{7,3},{8,12},{9,13},{10,... | collective-permute-start | bytes 208904 | tf_op jit(solution)/shard_map/ppermute | solution.py:396
  32.8 5.2 %collective-permute-start.12 = (bf16[272,128]{1,0:T(8,128)(2,1)S(1)}, bf16[272,128]{1,0:T(8,128)(2,1)S(1)}, u32[]{:S(2)}, u32[]{:S(2)}) collective-permute-start(bf16[272,128]{1,0:T(8,128)(2,1)S(1)} %get-tuple-element.70), channel_id=1, source_target_pairs={{0,6},{1,7},{2,4},{3,5},{4,2},{5,3},{6,0},{7,1},{8,14},{9,15},{10,... | collective-permute-start | bytes 208904 | tf_op jit(solution)/shard_map/ppermute | solution.py:396
  38.0 5.0 %collective-permute-start.13 = (bf16[528,128]{1,0:T(8,128)(2,1)S(1)}, bf16[528,128]{1,0:T(8,128)(2,1)S(1)}, u32[]{:S(2)}, u32[]{:S(2)}) collective-permute-start(bf16[528,128]{1,0:T(8,128)(2,1)S(1)} %collective-permute-done.9.refs_6_), channel_id=1, source_target_pairs={{0,16},{16,0},{1,17},{17,1},{2,18},{18,2},{3,19},{19,3},{4,20},{20... | collective-permute-start | bytes 405512 | tf_op jit(solution)/shard_map/ppermute | solution.py:399
  43.3 1.6 %collective-permute-start.14 = (bf16[1040,128]{1,0:T(8,128)(2,1)S(1)}, bf16[1040,128]{1,0:T(8,128)(2,1)S(1)}, u32[]{:S(2)}, u32[]{:S(2)}) collective-permute-start(bf16[1040,128]{1,0:T(8,128)(2,1)S(1)} %shard_map.61), channel_id=1, source_target_pairs={{0,1},{1,0},{2,3},{3,2},{4,5},{5,4},{6,7},{7,6},{8,9},{9,8},{10,11... | collective-permute-start | bytes 798728 | tf_op jit(solution)/shard_map/ppermute | solution.py:396

commit v8 on v7

--- a/solution.py
+++ b/solution.py
@@ -444,7 +444,6 @@
     coefficients, near = lax.optimization_barrier((coefficients, near))
     partner = across(coefficients, 1)
     far = call(bind(gather_kernel, rank), shape(3, 8 * rank, width), (vmem,) * 3, vmem, [], 0, 2**20)(*near)
-    partner, _ = lax.optimization_barrier((partner, far))
     far = swapped(far)
     slots = call(
         chip_kernel,

time: 46.4 us -> 46.4 us (level)
  no operation moved by 1% of the time
where the time goes in v8:
time: 46.4 us; the launch traced here: 46.2 us
  starting transfers between devices  21.1 us (45%)
  waiting for transfers between devices  14.8 us (32%)
  Pallas kernels  10.2 us (22%)
    ppermute x13, starting transfers between devices, across(): return lax.ppermute(value, AXES, [(s, s ^ mask) for s in range(16)])  17.9 us
    ppermute x13, waiting for transfers between devices, across(): return lax.ppermute(value, AXES, [(s, s ^ mask) for s in range(16)])  12.5 us
    pallas_call x9, Pallas kernels, placed(): run(*(pltpu.with_memory_space_constraint(operand, space) if space == pltp...  10.2 us
    ppermute x2, starting transfers between devices, swapped(): return lax.ppermute(value, 'groups', [(0, 1), (1, 0)])  3.2 us
    ppermute x2, waiting for transfers between devices, swapped(): return lax.ppermute(value, 'groups', [(0, 1), (1, 0)])  2.34 us
  transfers between devices with their start and end apart: 15, of which 12 were waited for; matrix products, arithmetic and copies ran while one was open for 0% of the time, Pallas kernels for 16%

profile of v8, /device:TPU:0, one launch (start us, length us, event | category | flops | bytes accessed | tf_op | source)
XLA Modules:
  0.0 46.2 jit_solution(3535554207008306373)
XLA Ops:
  0.0 1.1 %shard_map.55 = (bf16[656,128]{1,0:T(8,128)(2,1)S(1)}, bf16[656,128]{1,0:T(8,128)(2,1)S(1)}, bf16[656,128]{1,0:T(8,128)(2,1)S(1)}) custom-call(s32[32]{0:T(128)} %refs_4_.1, bf16[2,2,2,2,2,576,128]{6,5,4,3,2,1,0:T(8,128)(2,1)} %bitcast.3), custom_call_target="tpu_custom_call" | custom-call | bytes 1048576 | tf_op jit(solution)/shard_map/pallas_call | solution.py:370
  1.1 3.0 %collective-permute-start = (bf16[656,128]{1,0:T(8,128)(2,1)S(1)}, bf16[656,128]{1,0:T(8,128)(2,1)S(1)}, u32[]{:S(2)}, u32[]{:S(2)}) collective-permute-start(bf16[656,128]{1,0:T(8,128)(2,1)S(1)} %get-tuple-element.44), channel_id=1, source_target_pairs={{0,2},{1,3},{2,0},{3,1},{4,6},{5,7},{6,4},{7,5},{8,10},{9,11},{10,... | collective-permute-start | bytes 503816 | tf_op jit(solution)/shard_map/ppermute | solution.py:396
  4.1 1.6 %collective-permute-start.1 = (bf16[656,128]{1,0:T(8,128)(2,1)S(1)}, bf16[656,128]{1,0:T(8,128)(2,1)S(1)}, u32[]{:S(2)}, u32[]{:S(2)}) collective-permute-start(bf16[656,128]{1,0:T(8,128)(2,1)S(1)} %get-tuple-element.45), channel_id=1, source_target_pairs={{0,4},{1,5},{2,6},{3,7},{4,0},{5,1},{6,2},{7,3},{8,12},{9,13},{10,... | collective-permute-start | bytes 503816 | tf_op jit(solution)/shard_map/ppermute | solution.py:396
  5.7 5.0 %shard_map.56 = (bf16[32,64,128]{2,1,0:T(8,128)(2,1)S(1)}, bf16[32,64,128]{2,1,0:T(8,128)(2,1)S(1)}, bf16[2,2,2,128,128]{4,3,2,1,0:T(8,128)(2,1)S(1)}, bf16[272,...) custom-call(bf16[32,256,128]{2,1,0:T(8,128)(2,1)} %bitcast.5, ...), custom_call_target="tpu_custom_call" | custom-call | flops 469762048 | bytes 6291456 | tf_op jit(solution)/shard_map/pallas_call | solution.py:370
  10.7 0.6 %collective-permute-done.1.refs_1_.refs_6_.refs_2_ = bf16[656,128]{1,0:T(8,128)(2,1)S(1)} collective-permute-done((bf16[656,128]{1,0:T(8,128)(2,1)S(1)}, bf16[656,128]{1,0:T(8,128)(2,1)S(1)}, u32[]{:S(2)}, u32[]{:S(2)}) %collective-permute-start.1) | collective-permute-done | bytes 167968 | tf_op jit(solution)/shard_map/ppermute | solution.py:396
  11.3 1.9 %collective-permute-done.2.refs_2_.refs_7_.refs_3_ = bf16[656,128]{1,0:T(8,128)(2,1)S(1)} collective-permute-done((bf16[656,128]{1,0:T(8,128)(2,1)S(1)}, bf16[656,128]{1,0:T(8,128)(2,1)S(1)}, u32[]{:S(2)}, u32[]{:S(2)}) %collective-permute-start.2) | collective-permute-done | bytes 167968 | tf_op jit(solution)/shard_map/ppermute | solution.py:396
  13.3 1.7 %collective-permute-start.7 = (bf16[3,512,128]{2,1,0:T(8,128)(2,1)S(1)}, bf16[3,512,128]{2,1,0:T(8,128)(2,1)S(1)}, u32[]{:S(2)}, u32[]{:S(2)}) collective-permute-start(bf16[3,512,128]{2,1,0:T(8,128)(2,1)S(1)} %shard_map.58), channel_id=1, source_target_pairs={{0,16},{16,0},{1,17},{17,1},{2,18},{18,2},{3,19},{19,3},{4,20},{20... | collective-permute-start | bytes 1179656 | tf_op jit(solution)/shard_map/ppermute | solution.py:399
  15.0 0.2 collective-permute-done.3.other_ref
  15.2 0.4 shard_map.57
  15.6 1.7 %collective-permute-start.4 = (bf16[4,2,64,128]{3,2,1,0:T(8,128)(2,1)S(1)}, bf16[4,2,64,128]{3,2,1,0:T(8,128)(2,1)S(1)}, u32[]{:S(2)}, u32[]{:S(2)}) collective-permute-start(bf16[4,2,64,128]{3,2,1,0:T(8,128)(2,1)S(1)} %get-tuple-element.50), channel_id=1, source_target_pairs={{0,2},{1,3},{2,0},{3,1},{4,6},{5,7},{6,4},{7,5},{8,10},{9,11},{10,... | collective-permute-start | bytes 393224 | tf_op jit(solution)/shard_map/ppermute | solution.py:396
  17.3 1.6 %collective-permute-start.5 = (bf16[4,2,64,128]{3,2,1,0:T(8,128)(2,1)S(1)}, bf16[4,2,64,128]{3,2,1,0:T(8,128)(2,1)S(1)}, u32[]{:S(2)}, u32[]{:S(2)}) collective-permute-start(bf16[4,2,64,128]{3,2,1,0:T(8,128)(2,1)S(1)} %get-tuple-element.51), channel_id=1, source_target_pairs={{0,4},{1,5},{2,6},{3,7},{4,0},{5,1},{6,2},{7,3},{8,12},{9,13},{10,... | collective-permute-start | bytes 393224 | tf_op jit(solution)/shard_map/ppermute | solution.py:396
  18.9 0.2 collective-permute-start.6
  19.2 2.0 %collective-permute-done.4.refs_1_ = bf16[4,2,64,128]{3,2,1,0:T(8,128)(2,1)S(1)} collective-permute-done((bf16[4,2,64,128]{3,2,1,0:T(8,128)(2,1)S(1)}, bf16[4,2,64,128]{3,2,1,0:T(8,128)(2,1)S(1)}, u32[]{:S(2)}, u32[]{:S(2)}) %collective-permute-start.4) | collective-permute-done | bytes 131104 | tf_op jit(solution)/shard_map/ppermute | solution.py:396
  21.2 2.8 %collective-permute-start.9 = (bf16[528,128]{1,0:T(8,128)(2,1)S(1)}, bf16[528,128]{1,0:T(8,128)(2,1)S(1)}, u32[]{:S(2)}, u32[]{:S(2)}) collective-permute-start(bf16[528,128]{1,0:T(8,128)(2,1)S(1)} %shard_map.60), channel_id=1, source_target_pairs={{0,8},{1,9},{2,10},{3,11},{4,12},{5,13},{6,14},{7,15},{8,0},{9,1},... | collective-permute-start | bytes 405512 | tf_op jit(solution)/shard_map/ppermute | solution.py:396
  24.0 0.9 %collective-permute-done.7.refs_8_ = bf16[3,512,128]{2,1,0:T(8,128)(2,1)S(1)} collective-permute-done((bf16[3,512,128]{2,1,0:T(8,128)(2,1)S(1)}, bf16[3,512,128]{2,1,0:T(8,128)(2,1)S(1)}, u32[]{:S(2)}, u32[]{:S(2)}) %collective-permute-start.7) | collective-permute-done | bytes 393248 | tf_op jit(solution)/shard_map/ppermute | solution.py:399
  24.9 0.6 %collective-permute-done.6.refs_3_ = bf16[4,2,64,128]{3,2,1,0:T(8,128)(2,1)S(1)} collective-permute-done((bf16[4,2,64,128]{3,2,1,0:T(8,128)(2,1)S(1)}, bf16[4,2,64,128]{3,2,1,0:T(8,128)(2,1)S(1)}, u32[]{:S(2)}, u32[]{:S(2)}) %collective-permute-start.6) | collective-permute-done | bytes 131104 | tf_op jit(solution)/shard_map/ppermute | solution.py:396
  25.5 0.7 %shard_map.59 = (bf16[4,4,64,128]{3,2,1,0:T(8,128)(2,1)S(1)}, bf16[4,4,64,128]{3,2,1,0:T(8,128)(2,1)S(1)}) custom-call(bf16[4,2,64,128]{3,2,1,0:T(8,128)(2,1)S(1)} %get-tuple-element.49.refs_0_, bf16[4,2,64,128]{3,2,1,0:T(8,128)(2,1)S(1)} %collective-permute-done.4.refs_1_, bf16[4,2,64,128]{3,2,1,0:T(8,128)(2,1)S(1)} %collective-permute-done.5.refs_2_, ...), custom_call_target="tpu_custom_call" | custom-call | flops 268435456 | bytes 2097152 | tf_op jit(solution)/shard_map/pallas_call | solution.py:370
  26.1 3.4 %collective-permute-start.8 = (bf16[4,4,64,128]{3,2,1,0:T(8,128)(2,1)S(1)}, bf16[4,4,64,128]{3,2,1,0:T(8,128)(2,1)S(1)}, u32[]{:S(2)}, u32[]{:S(2)}) collective-permute-start(bf16[4,4,64,128]{3,2,1,0:T(8,128)(2,1)S(1)} %get-tuple-element.58), channel_id=1, source_target_pairs={{0,8},{1,9},{2,10},{3,11},{4,12},{5,13},{6,14},{7,15},{8,0},{9,1},... | collective-permute-start | bytes 786440 | tf_op jit(solution)/shard_map/ppermute | solution.py:396
  29.6 1.7 %collective-permute-start.10 = (bf16[272,128]{1,0:T(8,128)(2,1)S(1)}, bf16[272,128]{1,0:T(8,128)(2,1)S(1)}, u32[]{:S(2)}, u32[]{:S(2)}) collective-permute-start(bf16[272,128]{1,0:T(8,128)(2,1)S(1)} %get-tuple-element.66), channel_id=1, source_target_pairs={{0,2},{1,3},{2,0},{3,1},{4,6},{5,7},{6,4},{7,5},{8,10},{9,11},{10,... | collective-permute-start | bytes 208904 | tf_op jit(solution)/shard_map/ppermute | solution.py:396
  31.3 1.5 %collective-permute-start.11 = (bf16[272,128]{1,0:T(8,128)(2,1)S(1)}, bf16[272,128]{1,0:T(8,128)(2,1)S(1)}, u32[]{:S(2)}, u32[]{:S(2)}) collective-permute-start(bf16[272,128]{1,0:T(8,128)(2,1)S(1)} %get-tuple-element.67), channel_id=1, source_target_pairs={{0,4},{1,5},{2,6},{3,7},{4,0},{5,1},{6,2},{7,3},{8,12},{9,13},{10,... | collective-permute-start | bytes 208904 | tf_op jit(solution)/shard_map/ppermute | solution.py:396
  32.8 0.2 collective-permute-start.12
  33.0 0.8 %collective-permute-done.10.refs_3_ = bf16[272,128]{1,0:T(8,128)(2,1)S(1)} collective-permute-done((bf16[272,128]{1,0:T(8,128)(2,1)S(1)}, bf16[272,128]{1,0:T(8,128)(2,1)S(1)}, u32[]{:S(2)}, u32[]{:S(2)}) %collective-permute-start.10) | collective-permute-done | bytes 69664 | tf_op jit(solution)/shard_map/ppermute | solution.py:396
  33.9 2.5 %collective-permute-done.11.refs_4_ = bf16[272,128]{1,0:T(8,128)(2,1)S(1)} collective-permute-done((bf16[272,128]{1,0:T(8,128)(2,1)S(1)}, bf16[272,128]{1,0:T(8,128)(2,1)S(1)}, u32[]{:S(2)}, u32[]{:S(2)}) %collective-permute-start.11) | collective-permute-done | bytes 69664 | tf_op jit(solution)/shard_map/ppermute | solution.py:396
  36.4 1.7 %collective-permute-done.12.refs_5_ = bf16[272,128]{1,0:T(8,128)(2,1)S(1)} collective-permute-done((bf16[272,128]{1,0:T(8,128)(2,1)S(1)}, bf16[272,128]{1,0:T(8,128)(2,1)S(1)}, u32[]{:S(2)}, u32[]{:S(2)}) %collective-permute-start.12) | collective-permute-done | bytes 69664 | tf_op jit(solution)/shard_map/ppermute | solution.py:396
  38.0 1.5 %collective-permute-start.13 = (bf16[528,128]{1,0:T(8,128)(2,1)S(1)}, bf16[528,128]{1,0:T(8,128)(2,1)S(1)}, u32[]{:S(2)}, u32[]{:S(2)}) collective-permute-start(bf16[528,128]{1,0:T(8,128)(2,1)S(1)} %collective-permute-done.9.refs_6_), channel_id=1, source_target_pairs={{0,16},{16,0},{1,17},{17,1},{2,18},{18,2},{3,19},{19,3},{4,20},{20... | collective-permute-start | bytes 405512 | tf_op jit(solution)/shard_map/ppermute | solution.py:399
  39.5 2.0 %collective-permute-done.8.refs_1_ = bf16[4,4,64,128]{3,2,1,0:T(8,128)(2,1)S(1)} collective-permute-done((bf16[4,4,64,128]{3,2,1,0:T(8,128)(2,1)S(1)}, bf16[4,4,64,128]{3,2,1,0:T(8,128)(2,1)S(1)}, u32[]{:S(2)}, u32[]{:S(2)}) %collective-permute-start.8) | collective-permute-done | bytes 262176 | tf_op jit(solution)/shard_map/ppermute | solution.py:396
  41.6 1.5 %collective-permute-done.13.refs_7_ = bf16[528,128]{1,0:T(8,128)(2,1)S(1)} collective-permute-done((bf16[528,128]{1,0:T(8,128)(2,1)S(1)}, bf16[528,128]{1,0:T(8,128)(2,1)S(1)}, u32[]{:S(2)}, u32[]{:S(2)}) %collective-permute-start.13) | collective-permute-done | bytes 135200 | tf_op jit(solution)/shard_map/ppermute | solution.py:399
  43.0 0.3 shard_map.61
  43.3 0.1 collective-permute-start.14
  43.4 1.4 %shard_map.62.refs_2_ = bf16[32,256,128]{2,1,0:T(8,128)(2,1)} custom-call(bf16[4,4,64,128]{3,2,1,0:T(8,128)(2,1)S(1)} %get-tuple-element.57.refs_0_, bf16[4,4,64,128]{3,2,1,0:T(8,128)(2,1)S(1)} %collective-permute-done.8.refs_1_, bf16[272,128]{1,0:T(8,128)(2,1)S(1)} %get-tuple-element.63.refs_2_, bf16[272,128]{1,0:T(8,128)(2,1)S(1)} %collective-permute-done.10.refs_3_, ...), custom_call_target="tpu_custom_call" | custom-call | flops 134217728 | bytes 2097152 | tf_op jit(solution)/shard_map/pallas_call | solution.py:370
  44.8 0.1 collective-permute-done.14.refs_0_
  44.9 1.3 %shard_map.63 = bf16[32,256,128]{2,1,0:T(8,128)(2,1)} custom-call(bf16[1040,128]{1,0:T(8,128)(2,1)S(1)} %collective-permute-done.14.refs_0_, bf16[32,64,256]{2,1,0:T(8,128)(2,1)S(1)} %copy-done, bf16[32,256,128]{2,1,0:T(8,128)(2,1)} %shard_map.62.refs_2_), custom_call_target="tpu_custom_call", output_to_operand_aliasing={{}: (2, {})} | custom-call | flops 134217728 | bytes 2097152 | tf_op jit(solution)/shard_map/pallas_call | solution.py:370
  (9 shorter events, 0.1 us)
Async XLA Ops:
  1.1 9.6 %collective-permute-start = (bf16[656,128]{1,0:T(8,128)(2,1)S(1)}, bf16[656,128]{1,0:T(8,128)(2,1)S(1)}, u32[]{:S(2)}, u32[]{:S(2)}) collective-permute-start(bf16[656,128]{1,0:T(8,128)(2,1)S(1)} %get-tuple-element.44), channel_id=1, source_target_pairs={{0,2},{1,3},{2,0},{3,1},{4,6},{5,7},{6,4},{7,5},{8,10},{9,11},{10,... | collective-permute-start | bytes 503816 | tf_op jit(solution)/shard_map/ppermute | solution.py:396
  4.1 7.2 %collective-permute-start.1 = (bf16[656,128]{1,0:T(8,128)(2,1)S(1)}, bf16[656,128]{1,0:T(8,128)(2,1)S(1)}, u32[]{:S(2)}, u32[]{:S(2)}) collective-permute-start(bf16[656,128]{1,0:T(8,128)(2,1)S(1)} %get-tuple-element.45), channel_id=1, source_target_pairs={{0,4},{1,5},{2,6},{3,7},{4,0},{5,1},{6,2},{7,3},{8,12},{9,13},{10,... | collective-permute-start | bytes 503816 | tf_op jit(solution)/shard_map/ppermute | solution.py:396
  5.7 7.6 %collective-permute-start.2 = (bf16[656,128]{1,0:T(8,128)(2,1)S(1)}, bf16[656,128]{1,0:T(8,128)(2,1)S(1)}, u32[]{:S(2)}, u32[]{:S(2)}) collective-permute-start(bf16[656,128]{1,0:T(8,128)(2,1)S(1)} %get-tuple-element.46), channel_id=1, source_target_pairs={{0,6},{1,7},{2,4},{3,5},{4,2},{5,3},{6,0},{7,1},{8,14},{9,15},{10,... | collective-permute-start | bytes 503816 | tf_op jit(solution)/shard_map/ppermute | solution.py:396
  13.3 1.9 %collective-permute-start.3 = (bf16[32,64,128]{2,1,0:T(8,128)(2,1)S(1)}, bf16[32,64,128]{2,1,0:T(8,128)(2,1)S(1)}, u32[]{:S(2)}, u32[]{:S(2)}) collective-permute-start(bf16[32,64,128]{2,1,0:T(8,128)(2,1)S(1)} %get-tuple-element.47.own_ref), channel_id=1, source_target_pairs={{0,1},{1,0},{2,3},{3,2},{4,5},{5,4},{6,7},{7,6},{8,9},{9,8},{10,11... | collective-permute-start | bytes 1572872 | tf_op jit(solution)/shard_map/ppermute | solution.py:396
  13.3 11.6 %collective-permute-start.7 = (bf16[3,512,128]{2,1,0:T(8,128)(2,1)S(1)}, bf16[3,512,128]{2,1,0:T(8,128)(2,1)S(1)}, u32[]{:S(2)}, u32[]{:S(2)}) collective-permute-start(bf16[3,512,128]{2,1,0:T(8,128)(2,1)S(1)} %shard_map.58), channel_id=1, source_target_pairs={{0,16},{16,0},{1,17},{17,1},{2,18},{18,2},{3,19},{19,3},{4,20},{20... | collective-permute-start | bytes 1179656 | tf_op jit(solution)/shard_map/ppermute | solution.py:399
  15.6 27.8 %copy-start = (bf16[32,64,256]{2,1,0:T(8,128)(2,1)S(1)}, bf16[32,64,256]{2,1,0:T(8,128)(2,1)}, u32[]{:S(2)}) copy-start(bf16[32,64,256]{2,1,0:T(8,128)(2,1)} %refs_1_.3) | copy-start | bytes 3145732
  15.6 5.6 %collective-permute-start.4 = (bf16[4,2,64,128]{3,2,1,0:T(8,128)(2,1)S(1)}, bf16[4,2,64,128]{3,2,1,0:T(8,128)(2,1)S(1)}, u32[]{:S(2)}, u32[]{:S(2)}) collective-permute-start(bf16[4,2,64,128]{3,2,1,0:T(8,128)(2,1)S(1)} %get-tuple-element.50), channel_id=1, source_target_pairs={{0,2},{1,3},{2,0},{3,1},{4,6},{5,7},{6,4},{7,5},{8,10},{9,11},{10,... | collective-permute-start | bytes 393224 | tf_op jit(solution)/shard_map/ppermute | solution.py:396
  17.3 7.6 %collective-permute-start.5 = (bf16[4,2,64,128]{3,2,1,0:T(8,128)(2,1)S(1)}, bf16[4,2,64,128]{3,2,1,0:T(8,128)(2,1)S(1)}, u32[]{:S(2)}, u32[]{:S(2)}) collective-permute-start(bf16[4,2,64,128]{3,2,1,0:T(8,128)(2,1)S(1)} %get-tuple-element.51), channel_id=1, source_target_pairs={{0,4},{1,5},{2,6},{3,7},{4,0},{5,1},{6,2},{7,3},{8,12},{9,13},{10,... | collective-permute-start | bytes 393224 | tf_op jit(solution)/shard_map/ppermute | solution.py:396
  18.9 6.6 %collective-permute-start.6 = (bf16[4,2,64,128]{3,2,1,0:T(8,128)(2,1)S(1)}, bf16[4,2,64,128]{3,2,1,0:T(8,128)(2,1)S(1)}, u32[]{:S(2)}, u32[]{:S(2)}) collective-permute-start(bf16[4,2,64,128]{3,2,1,0:T(8,128)(2,1)S(1)} %get-tuple-element.52), channel_id=1, source_target_pairs={{0,6},{1,7},{2,4},{3,5},{4,2},{5,3},{6,0},{7,1},{8,14},{9,15},{10,... | collective-permute-start | bytes 393224 | tf_op jit(solution)/shard_map/ppermute | solution.py:396
  21.2 16.8 %collective-permute-start.9 = (bf16[528,128]{1,0:T(8,128)(2,1)S(1)}, bf16[528,128]{1,0:T(8,128)(2,1)S(1)}, u32[]{:S(2)}, u32[]{:S(2)}) collective-permute-start(bf16[528,128]{1,0:T(8,128)(2,1)S(1)} %shard_map.60), channel_id=1, source_target_pairs={{0,8},{1,9},{2,10},{3,11},{4,12},{5,13},{6,14},{7,15},{8,0},{9,1},... | collective-permute-start | bytes 405512 | tf_op jit(solution)/shard_map/ppermute | solution.py:396
  26.1 15.4 %collective-permute-start.8 = (bf16[4,4,64,128]{3,2,1,0:T(8,128)(2,1)S(1)}, bf16[4,4,64,128]{3,2,1,0:T(8,128)(2,1)S(1)}, u32[]{:S(2)}, u32[]{:S(2)}) collective-permute-start(bf16[4,4,64,128]{3,2,1,0:T(8,128)(2,1)S(1)} %get-tuple-element.58), channel_id=1, source_target_pairs={{0,8},{1,9},{2,10},{3,11},{4,12},{5,13},{6,14},{7,15},{8,0},{9,1},... | collective-permute-start | bytes 786440 | tf_op jit(solution)/shard_map/ppermute | solution.py:396
  29.6 4.3 %collective-permute-start.10 = (bf16[272,128]{1,0:T(8,128)(2,1)S(1)}, bf16[272,128]{1,0:T(8,128)(2,1)S(1)}, u32[]{:S(2)}, u32[]{:S(2)}) collective-permute-start(bf16[272,128]{1,0:T(8,128)(2,1)S(1)} %get-tuple-element.66), channel_id=1, source_target_pairs={{0,2},{1,3},{2,0},{3,1},{4,6},{5,7},{6,4},{7,5},{8,10},{9,11},{10,... | collective-permute-start | bytes 208904 | tf_op jit(solution)/shard_map/ppermute | solution.py:396
  31.3 5.0 %collective-permute-start.11 = (bf16[272,128]{1,0:T(8,128)(2,1)S(1)}, bf16[272,128]{1,0:T(8,128)(2,1)S(1)}, u32[]{:S(2)}, u32[]{:S(2)}) collective-permute-start(bf16[272,128]{1,0:T(8,128)(2,1)S(1)} %get-tuple-element.67), channel_id=1, source_target_pairs={{0,4},{1,5},{2,6},{3,7},{4,0},{5,1},{6,2},{7,3},{8,12},{9,13},{10,... | collective-permute-start | bytes 208904 | tf_op jit(solution)/shard_map/ppermute | solution.py:396
  32.8 5.2 %collective-permute-start.12 = (bf16[272,128]{1,0:T(8,128)(2,1)S(1)}, bf16[272,128]{1,0:T(8,128)(2,1)S(1)}, u32[]{:S(2)}, u32[]{:S(2)}) collective-permute-start(bf16[272,128]{1,0:T(8,128)(2,1)S(1)} %get-tuple-element.68), channel_id=1, source_target_pairs={{0,6},{1,7},{2,4},{3,5},{4,2},{5,3},{6,0},{7,1},{8,14},{9,15},{10,... | collective-permute-start | bytes 208904 | tf_op jit(solution)/shard_map/ppermute | solution.py:396
  38.0 5.0 %collective-permute-start.13 = (bf16[528,128]{1,0:T(8,128)(2,1)S(1)}, bf16[528,128]{1,0:T(8,128)(2,1)S(1)}, u32[]{:S(2)}, u32[]{:S(2)}) collective-permute-start(bf16[528,128]{1,0:T(8,128)(2,1)S(1)} %collective-permute-done.9.refs_6_), channel_id=1, source_target_pairs={{0,16},{16,0},{1,17},{17,1},{2,18},{18,2},{3,19},{19,3},{4,20},{20... | collective-permute-start | bytes 405512 | tf_op jit(solution)/shard_map/ppermute | solution.py:399
  43.3 1.6 %collective-permute-start.14 = (bf16[1040,128]{1,0:T(8,128)(2,1)S(1)}, bf16[1040,128]{1,0:T(8,128)(2,1)S(1)}, u32[]{:S(2)}, u32[]{:S(2)}) collective-permute-start(bf16[1040,128]{1,0:T(8,128)(2,1)S(1)} %shard_map.61), channel_id=1, source_target_pairs={{0,1},{1,0},{2,3},{3,2},{4,5},{5,4},{6,7},{7,6},{8,9},{9,8},{10,11... | collective-permute-start | bytes 798728 | tf_op jit(solution)/shard_map/ppermute | solution.py:396

commit v9 on v8

--- a/solution.py
+++ b/solution.py
@@ -472,7 +472,7 @@
     received = across(send, 8)
     stay, _ = lax.optimization_barrier((stay, send))
     stay = [stay[0]] + [across(stay[r], 2 * r) for r in (1, 2, 3)]
-    here, stay[1], stay[2], stay[3] = lax.optimization_barrier((here, stay[1], stay[2], stay[3]))
+    here, stay[1], stay[3] = lax.optimization_barrier((here, stay[1], stay[3]))
     cross = swapped(here)
     basis = out_basis
     matrices = (*stay, here, cross)

time: 46.4 us -> 46.4 us (level)
  starting transfers between devices: 21.1 us -> 22.6 us
  waiting for transfers between devices: 14.8 us -> 13.4 us
    ppermute x13, starting transfers between devices: 17.9 us -> 19.4 us  [across(): return lax.ppermute(value, AXES, [(s, s ^ mask) for s in range(16)])]
    ppermute x2, waiting for transfers between devices: 2.34 us -> 0.86 us  [swapped(): return lax.ppermute(value, 'groups', [(0, 1), (1, 0)])]
  transfers between devices with their start and end apart: 15 -> 15, of which waited for: 12 -> 10; matrix products, arithmetic and copies ran while one was open for 0% -> 0% of each run, Pallas kernels for 16% -> 16%
where the time goes in v9:
time: 46.4 us; the launch traced here: 46.3 us
  starting transfers between devices  22.6 us (49%)
  waiting for transfers between devices  13.4 us (29%)
  Pallas kernels  10.2 us (22%)
    ppermute x13, starting transfers between devices, across(): return lax.ppermute(value, AXES, [(s, s ^ mask) for s in range(16)])  19.4 us
    ppermute x13, waiting for transfers between devices, across(): return lax.ppermute(value, AXES, [(s, s ^ mask) for s in range(16)])  12.5 us
    pallas_call x9, Pallas kernels, placed(): run(*(pltpu.with_memory_space_constraint(operand, space) if space == pltp...  10.2 us
    ppermute x2, starting transfers between devices, swapped(): return lax.ppermute(value, 'groups', [(0, 1), (1, 0)])  3.2 us
  transfers between devices with their start and end apart: 15, of which 10 were waited for; matrix products, arithmetic and copies ran while one was open for 0% of the time, Pallas kernels for 16%

profile of v9, /device:TPU:0, one launch (start us, length us, event | category | flops | bytes accessed | tf_op | source)
XLA Modules:
  0.0 46.3 jit_solution(15025958248260303252)
XLA Ops:
  0.0 1.1 %shard_map.55 = (bf16[656,128]{1,0:T(8,128)(2,1)S(1)}, bf16[656,128]{1,0:T(8,128)(2,1)S(1)}, bf16[656,128]{1,0:T(8,128)(2,1)S(1)}) custom-call(s32[32]{0:T(128)} %refs_4_.1, bf16[2,2,2,2,2,576,128]{6,5,4,3,2,1,0:T(8,128)(2,1)} %bitcast.3), custom_call_target="tpu_custom_call" | custom-call | bytes 1048576 | tf_op jit(solution)/shard_map/pallas_call | solution.py:370
  1.1 3.0 %collective-permute-start = (bf16[656,128]{1,0:T(8,128)(2,1)S(1)}, bf16[656,128]{1,0:T(8,128)(2,1)S(1)}, u32[]{:S(2)}, u32[]{:S(2)}) collective-permute-start(bf16[656,128]{1,0:T(8,128)(2,1)S(1)} %get-tuple-element.43), channel_id=1, source_target_pairs={{0,2},{1,3},{2,0},{3,1},{4,6},{5,7},{6,4},{7,5},{8,10},{9,11},{10,... | collective-permute-start | bytes 503816 | tf_op jit(solution)/shard_map/ppermute | solution.py:396
  4.1 1.6 %collective-permute-start.1 = (bf16[656,128]{1,0:T(8,128)(2,1)S(1)}, bf16[656,128]{1,0:T(8,128)(2,1)S(1)}, u32[]{:S(2)}, u32[]{:S(2)}) collective-permute-start(bf16[656,128]{1,0:T(8,128)(2,1)S(1)} %get-tuple-element.44), channel_id=1, source_target_pairs={{0,4},{1,5},{2,6},{3,7},{4,0},{5,1},{6,2},{7,3},{8,12},{9,13},{10,... | collective-permute-start | bytes 503816 | tf_op jit(solution)/shard_map/ppermute | solution.py:396
  5.7 0.0 collective-permute-start.2
  5.7 5.0 %shard_map.56 = (bf16[32,64,128]{2,1,0:T(8,128)(2,1)S(1)}, bf16[32,64,128]{2,1,0:T(8,128)(2,1)S(1)}, bf16[2,2,2,128,128]{4,3,2,1,0:T(8,128)(2,1)S(1)}, bf16[272,...) custom-call(bf16[32,256,128]{2,1,0:T(8,128)(2,1)} %bitcast.5, ...), custom_call_target="tpu_custom_call" | custom-call | flops 469762048 | bytes 6291456 | tf_op jit(solution)/shard_map/pallas_call | solution.py:370
  10.7 0.6 %collective-permute-done.1.refs_1_.refs_6_.refs_2_ = bf16[656,128]{1,0:T(8,128)(2,1)S(1)} collective-permute-done((bf16[656,128]{1,0:T(8,128)(2,1)S(1)}, bf16[656,128]{1,0:T(8,128)(2,1)S(1)}, u32[]{:S(2)}, u32[]{:S(2)}) %collective-permute-start.1) | collective-permute-done | bytes 167968 | tf_op jit(solution)/shard_map/ppermute | solution.py:396
  11.3 1.9 %collective-permute-done.2.refs_2_.refs_7_.refs_3_ = bf16[656,128]{1,0:T(8,128)(2,1)S(1)} collective-permute-done((bf16[656,128]{1,0:T(8,128)(2,1)S(1)}, bf16[656,128]{1,0:T(8,128)(2,1)S(1)}, u32[]{:S(2)}, u32[]{:S(2)}) %collective-permute-start.2) | collective-permute-done | bytes 167968 | tf_op jit(solution)/shard_map/ppermute | solution.py:396
  13.3 1.7 %collective-permute-start.7 = (bf16[3,512,128]{2,1,0:T(8,128)(2,1)S(1)}, bf16[3,512,128]{2,1,0:T(8,128)(2,1)S(1)}, u32[]{:S(2)}, u32[]{:S(2)}) collective-permute-start(bf16[3,512,128]{2,1,0:T(8,128)(2,1)S(1)} %shard_map.58), channel_id=1, source_target_pairs={{0,16},{16,0},{1,17},{17,1},{2,18},{18,2},{3,19},{19,3},{4,20},{20... | collective-permute-start | bytes 1179656 | tf_op jit(solution)/shard_map/ppermute | solution.py:399
  15.0 0.2 collective-permute-done.3.other_ref
  15.2 0.4 shard_map.57
  15.6 0.0 copy-start
  15.6 1.7 %collective-permute-start.4 = (bf16[4,2,64,128]{3,2,1,0:T(8,128)(2,1)S(1)}, bf16[4,2,64,128]{3,2,1,0:T(8,128)(2,1)S(1)}, u32[]{:S(2)}, u32[]{:S(2)}) collective-permute-start(bf16[4,2,64,128]{3,2,1,0:T(8,128)(2,1)S(1)} %get-tuple-element.49), channel_id=1, source_target_pairs={{0,2},{1,3},{2,0},{3,1},{4,6},{5,7},{6,4},{7,5},{8,10},{9,11},{10,... | collective-permute-start | bytes 393224 | tf_op jit(solution)/shard_map/ppermute | solution.py:396
  17.3 1.6 %collective-permute-start.5 = (bf16[4,2,64,128]{3,2,1,0:T(8,128)(2,1)S(1)}, bf16[4,2,64,128]{3,2,1,0:T(8,128)(2,1)S(1)}, u32[]{:S(2)}, u32[]{:S(2)}) collective-permute-start(bf16[4,2,64,128]{3,2,1,0:T(8,128)(2,1)S(1)} %get-tuple-element.50), channel_id=1, source_target_pairs={{0,4},{1,5},{2,6},{3,7},{4,0},{5,1},{6,2},{7,3},{8,12},{9,13},{10,... | collective-permute-start | bytes 393224 | tf_op jit(solution)/shard_map/ppermute | solution.py:396
  18.9 0.2 collective-permute-start.6
  19.2 2.0 %collective-permute-done.4.refs_1_ = bf16[4,2,64,128]{3,2,1,0:T(8,128)(2,1)S(1)} collective-permute-done((bf16[4,2,64,128]{3,2,1,0:T(8,128)(2,1)S(1)}, bf16[4,2,64,128]{3,2,1,0:T(8,128)(2,1)S(1)}, u32[]{:S(2)}, u32[]{:S(2)}) %collective-permute-start.4) | collective-permute-done | bytes 131104 | tf_op jit(solution)/shard_map/ppermute | solution.py:396
  21.2 2.8 %collective-permute-start.9 = (bf16[528,128]{1,0:T(8,128)(2,1)S(1)}, bf16[528,128]{1,0:T(8,128)(2,1)S(1)}, u32[]{:S(2)}, u32[]{:S(2)}) collective-permute-start(bf16[528,128]{1,0:T(8,128)(2,1)S(1)} %shard_map.60), channel_id=1, source_target_pairs={{0,8},{1,9},{2,10},{3,11},{4,12},{5,13},{6,14},{7,15},{8,0},{9,1},... | collective-permute-start | bytes 405512 | tf_op jit(solution)/shard_map/ppermute | solution.py:396
  24.0 0.9 %collective-permute-done.7.refs_8_ = bf16[3,512,128]{2,1,0:T(8,128)(2,1)S(1)} collective-permute-done((bf16[3,512,128]{2,1,0:T(8,128)(2,1)S(1)}, bf16[3,512,128]{2,1,0:T(8,128)(2,1)S(1)}, u32[]{:S(2)}, u32[]{:S(2)}) %collective-permute-start.7) | collective-permute-done | bytes 393248 | tf_op jit(solution)/shard_map/ppermute | solution.py:399
  24.9 0.6 %collective-permute-done.6.refs_3_ = bf16[4,2,64,128]{3,2,1,0:T(8,128)(2,1)S(1)} collective-permute-done((bf16[4,2,64,128]{3,2,1,0:T(8,128)(2,1)S(1)}, bf16[4,2,64,128]{3,2,1,0:T(8,128)(2,1)S(1)}, u32[]{:S(2)}, u32[]{:S(2)}) %collective-permute-start.6) | collective-permute-done | bytes 131104 | tf_op jit(solution)/shard_map/ppermute | solution.py:396
  25.5 0.7 %shard_map.59 = (bf16[4,4,64,128]{3,2,1,0:T(8,128)(2,1)S(1)}, bf16[4,4,64,128]{3,2,1,0:T(8,128)(2,1)S(1)}) custom-call(bf16[4,2,64,128]{3,2,1,0:T(8,128)(2,1)S(1)} %get-tuple-element.48.refs_0_, bf16[4,2,64,128]{3,2,1,0:T(8,128)(2,1)S(1)} %collective-permute-done.4.refs_1_, bf16[4,2,64,128]{3,2,1,0:T(8,128)(2,1)S(1)} %collective-permute-done.5.refs_2_, ...), custom_call_target="tpu_custom_call" | custom-call | flops 268435456 | bytes 2097152 | tf_op jit(solution)/shard_map/pallas_call | solution.py:370
  26.1 3.4 %collective-permute-start.8 = (bf16[4,4,64,128]{3,2,1,0:T(8,128)(2,1)S(1)}, bf16[4,4,64,128]{3,2,1,0:T(8,128)(2,1)S(1)}, u32[]{:S(2)}, u32[]{:S(2)}) collective-permute-start(bf16[4,4,64,128]{3,2,1,0:T(8,128)(2,1)S(1)} %get-tuple-element.57), channel_id=1, source_target_pairs={{0,8},{1,9},{2,10},{3,11},{4,12},{5,13},{6,14},{7,15},{8,0},{9,1},... | collective-permute-start | bytes 786440 | tf_op jit(solution)/shard_map/ppermute | solution.py:396
  29.6 1.7 %collective-permute-start.10 = (bf16[272,128]{1,0:T(8,128)(2,1)S(1)}, bf16[272,128]{1,0:T(8,128)(2,1)S(1)}, u32[]{:S(2)}, u32[]{:S(2)}) collective-permute-start(bf16[272,128]{1,0:T(8,128)(2,1)S(1)} %get-tuple-element.65), channel_id=1, source_target_pairs={{0,2},{1,3},{2,0},{3,1},{4,6},{5,7},{6,4},{7,5},{8,10},{9,11},{10,... | collective-permute-start | bytes 208904 | tf_op jit(solution)/shard_map/ppermute | solution.py:396
  31.3 1.0 %collective-permute-start.11 = (bf16[272,128]{1,0:T(8,128)(2,1)S(1)}, bf16[272,128]{1,0:T(8,128)(2,1)S(1)}, u32[]{:S(2)}, u32[]{:S(2)}) collective-permute-start(bf16[272,128]{1,0:T(8,128)(2,1)S(1)} %get-tuple-element.66), channel_id=1, source_target_pairs={{0,6},{1,7},{2,4},{3,5},{4,2},{5,3},{6,0},{7,1},{8,14},{9,15},{10,... | collective-permute-start | bytes 208904 | tf_op jit(solution)/shard_map/ppermute | solution.py:396
  32.3 1.8 %collective-permute-done.10.refs_3_ = bf16[272,128]{1,0:T(8,128)(2,1)S(1)} collective-permute-done((bf16[272,128]{1,0:T(8,128)(2,1)S(1)}, bf16[272,128]{1,0:T(8,128)(2,1)S(1)}, u32[]{:S(2)}, u32[]{:S(2)}) %collective-permute-start.10) | collective-permute-done | bytes 69664 | tf_op jit(solution)/shard_map/ppermute | solution.py:396
  34.0 2.5 %collective-permute-done.11.refs_5_ = bf16[272,128]{1,0:T(8,128)(2,1)S(1)} collective-permute-done((bf16[272,128]{1,0:T(8,128)(2,1)S(1)}, bf16[272,128]{1,0:T(8,128)(2,1)S(1)}, u32[]{:S(2)}, u32[]{:S(2)}) %collective-permute-start.11) | collective-permute-done | bytes 69664 | tf_op jit(solution)/shard_map/ppermute | solution.py:396
  36.5 1.5 %collective-permute-start.13 = (bf16[528,128]{1,0:T(8,128)(2,1)S(1)}, bf16[528,128]{1,0:T(8,128)(2,1)S(1)}, u32[]{:S(2)}, u32[]{:S(2)}) collective-permute-start(bf16[528,128]{1,0:T(8,128)(2,1)S(1)} %collective-permute-done.9.refs_6_), channel_id=1, source_target_pairs={{0,16},{16,0},{1,17},{17,1},{2,18},{18,2},{3,19},{19,3},{4,20},{20... | collective-permute-start | bytes 405512 | tf_op jit(solution)/shard_map/ppermute | solution.py:399
  38.0 2.3 %collective-permute-start.12 = (bf16[272,128]{1,0:T(8,128)(2,1)S(1)}, bf16[272,128]{1,0:T(8,128)(2,1)S(1)}, u32[]{:S(2)}, u32[]{:S(2)}) collective-permute-start(bf16[272,128]{1,0:T(8,128)(2,1)S(1)} %get-tuple-element.68), channel_id=1, source_target_pairs={{0,4},{1,5},{2,6},{3,7},{4,0},{5,1},{6,2},{7,3},{8,12},{9,13},{10,... | collective-permute-start | bytes 208904 | tf_op jit(solution)/shard_map/ppermute | solution.py:396
  40.3 2.8 %collective-permute-done.12.refs_4_ = bf16[272,128]{1,0:T(8,128)(2,1)S(1)} collective-permute-done((bf16[272,128]{1,0:T(8,128)(2,1)S(1)}, bf16[272,128]{1,0:T(8,128)(2,1)S(1)}, u32[]{:S(2)}, u32[]{:S(2)}) %collective-permute-start.12) | collective-permute-done | bytes 69664 | tf_op jit(solution)/shard_map/ppermute | solution.py:396
  43.1 0.3 shard_map.61
  43.3 0.1 collective-permute-start.14
  43.4 1.4 %shard_map.62.refs_2_ = bf16[32,256,128]{2,1,0:T(8,128)(2,1)} custom-call(bf16[4,4,64,128]{3,2,1,0:T(8,128)(2,1)S(1)} %get-tuple-element.56.refs_0_, bf16[4,4,64,128]{3,2,1,0:T(8,128)(2,1)S(1)} %collective-permute-done.8.refs_1_, bf16[272,128]{1,0:T(8,128)(2,1)S(1)} %get-tuple-element.62.refs_2_, bf16[272,128]{1,0:T(8,128)(2,1)S(1)} %collective-permute-done.10.refs_3_, ...), custom_call_target="tpu_custom_call" | custom-call | flops 134217728 | bytes 2097152 | tf_op jit(solution)/shard_map/pallas_call | solution.py:370
  44.8 0.1 collective-permute-done.14.refs_0_
  45.0 1.3 %shard_map.63 = bf16[32,256,128]{2,1,0:T(8,128)(2,1)} custom-call(bf16[1040,128]{1,0:T(8,128)(2,1)S(1)} %collective-permute-done.14.refs_0_, bf16[32,64,256]{2,1,0:T(8,128)(2,1)S(1)} %copy-done, bf16[32,256,128]{2,1,0:T(8,128)(2,1)} %shard_map.62.refs_2_), custom_call_target="tpu_custom_call", output_to_operand_aliasing={{}: (2, {})} | custom-call | flops 134217728 | bytes 2097152 | tf_op jit(solution)/shard_map/pallas_call | solution.py:370
  (9 shorter events, 0.1 us)
Async XLA Ops:
  1.1 9.6 %collective-permute-start = (bf16[656,128]{1,0:T(8,128)(2,1)S(1)}, bf16[656,128]{1,0:T(8,128)(2,1)S(1)}, u32[]{:S(2)}, u32[]{:S(2)}) collective-permute-start(bf16[656,128]{1,0:T(8,128)(2,1)S(1)} %get-tuple-element.43), channel_id=1, source_target_pairs={{0,2},{1,3},{2,0},{3,1},{4,6},{5,7},{6,4},{7,5},{8,10},{9,11},{10,... | collective-permute-start | bytes 503816 | tf_op jit(solution)/shard_map/ppermute | solution.py:396
  4.1 7.2 %collective-permute-start.1 = (bf16[656,128]{1,0:T(8,128)(2,1)S(1)}, bf16[656,128]{1,0:T(8,128)(2,1)S(1)}, u32[]{:S(2)}, u32[]{:S(2)}) collective-permute-start(bf16[656,128]{1,0:T(8,128)(2,1)S(1)} %get-tuple-element.44), channel_id=1, source_target_pairs={{0,4},{1,5},{2,6},{3,7},{4,0},{5,1},{6,2},{7,3},{8,12},{9,13},{10,... | collective-permute-start | bytes 503816 | tf_op jit(solution)/shard_map/ppermute | solution.py:396
  5.7 7.6 %collective-permute-start.2 = (bf16[656,128]{1,0:T(8,128)(2,1)S(1)}, bf16[656,128]{1,0:T(8,128)(2,1)S(1)}, u32[]{:S(2)}, u32[]{:S(2)}) collective-permute-start(bf16[656,128]{1,0:T(8,128)(2,1)S(1)} %get-tuple-element.45), channel_id=1, source_target_pairs={{0,6},{1,7},{2,4},{3,5},{4,2},{5,3},{6,0},{7,1},{8,14},{9,15},{10,... | collective-permute-start | bytes 503816 | tf_op jit(solution)/shard_map/ppermute | solution.py:396
  13.3 1.9 %collective-permute-start.3 = (bf16[32,64,128]{2,1,0:T(8,128)(2,1)S(1)}, bf16[32,64,128]{2,1,0:T(8,128)(2,1)S(1)}, u32[]{:S(2)}, u32[]{:S(2)}) collective-permute-start(bf16[32,64,128]{2,1,0:T(8,128)(2,1)S(1)} %get-tuple-element.46.own_ref), channel_id=1, source_target_pairs={{0,1},{1,0},{2,3},{3,2},{4,5},{5,4},{6,7},{7,6},{8,9},{9,8},{10,11... | collective-permute-start | bytes 1572872 | tf_op jit(solution)/shard_map/ppermute | solution.py:396
  13.3 11.6 %collective-permute-start.7 = (bf16[3,512,128]{2,1,0:T(8,128)(2,1)S(1)}, bf16[3,512,128]{2,1,0:T(8,128)(2,1)S(1)}, u32[]{:S(2)}, u32[]{:S(2)}) collective-permute-start(bf16[3,512,128]{2,1,0:T(8,128)(2,1)S(1)} %shard_map.58), channel_id=1, source_target_pairs={{0,16},{16,0},{1,17},{17,1},{2,18},{18,2},{3,19},{19,3},{4,20},{20... | collective-permute-start | bytes 1179656 | tf_op jit(solution)/shard_map/ppermute | solution.py:399
  15.6 27.8 %copy-start = (bf16[32,64,256]{2,1,0:T(8,128)(2,1)S(1)}, bf16[32,64,256]{2,1,0:T(8,128)(2,1)}, u32[]{:S(2)}) copy-start(bf16[32,64,256]{2,1,0:T(8,128)(2,1)} %refs_1_.3) | copy-start | bytes 3145732
  15.6 5.6 %collective-permute-start.4 = (bf16[4,2,64,128]{3,2,1,0:T(8,128)(2,1)S(1)}, bf16[4,2,64,128]{3,2,1,0:T(8,128)(2,1)S(1)}, u32[]{:S(2)}, u32[]{:S(2)}) collective-permute-start(bf16[4,2,64,128]{3,2,1,0:T(8,128)(2,1)S(1)} %get-tuple-element.49), channel_id=1, source_target_pairs={{0,2},{1,3},{2,0},{3,1},{4,6},{5,7},{6,4},{7,5},{8,10},{9,11},{10,... | collective-permute-start | bytes 393224 | tf_op jit(solution)/shard_map/ppermute | solution.py:396
  17.3 7.6 %collective-permute-start.5 = (bf16[4,2,64,128]{3,2,1,0:T(8,128)(2,1)S(1)}, bf16[4,2,64,128]{3,2,1,0:T(8,128)(2,1)S(1)}, u32[]{:S(2)}, u32[]{:S(2)}) collective-permute-start(bf16[4,2,64,128]{3,2,1,0:T(8,128)(2,1)S(1)} %get-tuple-element.50), channel_id=1, source_target_pairs={{0,4},{1,5},{2,6},{3,7},{4,0},{5,1},{6,2},{7,3},{8,12},{9,13},{10,... | collective-permute-start | bytes 393224 | tf_op jit(solution)/shard_map/ppermute | solution.py:396
  18.9 6.6 %collective-permute-start.6 = (bf16[4,2,64,128]{3,2,1,0:T(8,128)(2,1)S(1)}, bf16[4,2,64,128]{3,2,1,0:T(8,128)(2,1)S(1)}, u32[]{:S(2)}, u32[]{:S(2)}) collective-permute-start(bf16[4,2,64,128]{3,2,1,0:T(8,128)(2,1)S(1)} %get-tuple-element.51), channel_id=1, source_target_pairs={{0,6},{1,7},{2,4},{3,5},{4,2},{5,3},{6,0},{7,1},{8,14},{9,15},{10,... | collective-permute-start | bytes 393224 | tf_op jit(solution)/shard_map/ppermute | solution.py:396
  21.2 15.3 %collective-permute-start.9 = (bf16[528,128]{1,0:T(8,128)(2,1)S(1)}, bf16[528,128]{1,0:T(8,128)(2,1)S(1)}, u32[]{:S(2)}, u32[]{:S(2)}) collective-permute-start(bf16[528,128]{1,0:T(8,128)(2,1)S(1)} %shard_map.60), channel_id=1, source_target_pairs={{0,8},{1,9},{2,10},{3,11},{4,12},{5,13},{6,14},{7,15},{8,0},{9,1},... | collective-permute-start | bytes 405512 | tf_op jit(solution)/shard_map/ppermute | solution.py:396
  26.1 16.9 %collective-permute-start.8 = (bf16[4,4,64,128]{3,2,1,0:T(8,128)(2,1)S(1)}, bf16[4,4,64,128]{3,2,1,0:T(8,128)(2,1)S(1)}, u32[]{:S(2)}, u32[]{:S(2)}) collective-permute-start(bf16[4,4,64,128]{3,2,1,0:T(8,128)(2,1)S(1)} %get-tuple-element.57), channel_id=1, source_target_pairs={{0,8},{1,9},{2,10},{3,11},{4,12},{5,13},{6,14},{7,15},{8,0},{9,1},... | collective-permute-start | bytes 786440 | tf_op jit(solution)/shard_map/ppermute | solution.py:396
  29.6 4.5 %collective-permute-start.10 = (bf16[272,128]{1,0:T(8,128)(2,1)S(1)}, bf16[272,128]{1,0:T(8,128)(2,1)S(1)}, u32[]{:S(2)}, u32[]{:S(2)}) collective-permute-start(bf16[272,128]{1,0:T(8,128)(2,1)S(1)} %get-tuple-element.65), channel_id=1, source_target_pairs={{0,2},{1,3},{2,0},{3,1},{4,6},{5,7},{6,4},{7,5},{8,10},{9,11},{10,... | collective-permute-start | bytes 208904 | tf_op jit(solution)/shard_map/ppermute | solution.py:396
  31.3 5.2 %collective-permute-start.11 = (bf16[272,128]{1,0:T(8,128)(2,1)S(1)}, bf16[272,128]{1,0:T(8,128)(2,1)S(1)}, u32[]{:S(2)}, u32[]{:S(2)}) collective-permute-start(bf16[272,128]{1,0:T(8,128)(2,1)S(1)} %get-tuple-element.66), channel_id=1, source_target_pairs={{0,6},{1,7},{2,4},{3,5},{4,2},{5,3},{6,0},{7,1},{8,14},{9,15},{10,... | collective-permute-start | bytes 208904 | tf_op jit(solution)/shard_map/ppermute | solution.py:396
  36.5 6.5 %collective-permute-start.13 = (bf16[528,128]{1,0:T(8,128)(2,1)S(1)}, bf16[528,128]{1,0:T(8,128)(2,1)S(1)}, u32[]{:S(2)}, u32[]{:S(2)}) collective-permute-start(bf16[528,128]{1,0:T(8,128)(2,1)S(1)} %collective-permute-done.9.refs_6_), channel_id=1, source_target_pairs={{0,16},{16,0},{1,17},{17,1},{2,18},{18,2},{3,19},{19,3},{4,20},{20... | collective-permute-start | bytes 405512 | tf_op jit(solution)/shard_map/ppermute | solution.py:399
  38.0 5.0 %collective-permute-start.12 = (bf16[272,128]{1,0:T(8,128)(2,1)S(1)}, bf16[272,128]{1,0:T(8,128)(2,1)S(1)}, u32[]{:S(2)}, u32[]{:S(2)}) collective-permute-start(bf16[272,128]{1,0:T(8,128)(2,1)S(1)} %get-tuple-element.68), channel_id=1, source_target_pairs={{0,4},{1,5},{2,6},{3,7},{4,0},{5,1},{6,2},{7,3},{8,12},{9,13},{10,... | collective-permute-start | bytes 208904 | tf_op jit(solution)/shard_map/ppermute | solution.py:396
  43.3 1.6 %collective-permute-start.14 = (bf16[1040,128]{1,0:T(8,128)(2,1)S(1)}, bf16[1040,128]{1,0:T(8,128)(2,1)S(1)}, u32[]{:S(2)}, u32[]{:S(2)}) collective-permute-start(bf16[1040,128]{1,0:T(8,128)(2,1)S(1)} %shard_map.61), channel_id=1, source_target_pairs={{0,1},{1,0},{2,3},{3,2},{4,5},{5,4},{6,7},{7,6},{8,9},{9,8},{10,11... | collective-permute-start | bytes 798728 | tf_op jit(solution)/shard_map/ppermute | solution.py:396
